TPU v7x, 512 devices: a whole 4x8x8 slice. The times are simulated.
512 devices in a mesh: replica: 16 (over y_lo, x, core), fsdp: 32 (over z, y_hi).
Axes of the slice: x: 4, y: 8 (y_hi: 4, y_lo: 2; y = y_hi * 2 + y_lo), z: 8, core: 2. Of those that a mesh axis runs over, the one named last changes fastest.
Arguments:
- activations: bfloat16 [16, 4096, 8192], P('replica', 'fsdp'), may hold values from -30 to 30, as said below
- key_cotangent: bfloat16 [16, 4096, 512], P('replica', 'fsdp'), may hold values from -6 to 6
- key_gain: float32 [128], replicated, may hold values from 0.25 to 1.75
- local_weight: float32 [16, 8192, 512], P('replica', 'fsdp'), may hold values from -6 to 6
- global_weight: float32 [8192, 512], P('fsdp', 'replica'), may hold values from -6 to 6
- outer_momentum: float32 [8192, 512], P('fsdp', 'replica'), may hold values from -6 to 6
- late_delta: float32 [8192, 512], P('fsdp', 'replica'), may hold values from -6 to 6
Outputs:
- next_local: float32 [16, 8192, 512], P('replica', 'fsdp')
- next_global: float32 [8192, 512], P('fsdp', 'replica')
- next_momentum: float32 [8192, 512], P('fsdp', 'replica')
- outer_delta: float32 [8192, 512], P('fsdp', 'replica')
Inputs may be any that keep to these rules, and one draw needn't show every extreme that they name: The activations are the key projection's normalized inputs, and the scale of each input feature differs from feature to feature (by up to about twentyfold).
All inputs are finite; a program needn't handle non-finite values.
Results may differ from a plain program's by a relative error of at most 0.00083.
Values may be sent and summed in bfloat16 or wider, within the bound.
No kernel may reach another device: no remote copies, remote signals or barrier semaphores. Data moves between devices by JAX's collectives and lax.ppermute only.
A program may use at most 64 MiB of HBM per device.

v0:
```python
import jax
import jax.numpy as jnp
from jax import lax
from jax.sharding import PartitionSpec as P

HEAD = 128


inner_rate = 0.5
outer_rate = 0.7
keep_rate = 0.9
blend_rate = 0.5
epsilon = 1e-06


def shards(
    activations, key_cotangent, key_gain, local_weight, global_weight, outer_momentum, late_delta
):
    feats = activations[0]
    cotangent = key_cotangent[0]
    own_rows = local_weight[0]
    width = feats.shape[1]
    columns = own_rows.shape[1]
    tokens = feats.shape[0]
    factor = width ** (-0.5)
    weight_copy = own_rows.astype(jnp.bfloat16)
    picked = feats
    hidden = (
        jnp.dot(
            picked,
            lax.all_gather(weight_copy, "fsdp", axis=0, tiled=True),
            preferred_element_type=jnp.float32,
        )
        * factor
    )
    shaped = hidden.reshape(tokens, -1, HEAD)
    spread = jnp.sqrt(jnp.mean(shaped * shaped, axis=-1, keepdims=True) + epsilon)
    unit = shaped / spread
    slope = cotangent.astype(jnp.float32).reshape(tokens, -1, HEAD) * key_gain
    key_slope = (slope - unit * jnp.mean(slope * unit, axis=-1, keepdims=True)) / spread
    key_slope = key_slope.reshape(tokens, columns).astype(jnp.bfloat16)
    owned_features = lax.all_to_all(feats, "fsdp", split_axis=1, concat_axis=0, tiled=True)
    picked = owned_features
    gradient = (
        lax.dot_general(
            picked,
            lax.all_gather(key_slope, "fsdp", axis=0, tiled=True),
            (((0,), (0,)), ((), ())),
            preferred_element_type=jnp.float32,
        )
        * factor
    )
    squares = lax.psum(jnp.sum(gradient * gradient), "fsdp")
    grad_scale = jnp.sqrt(squares / (width * columns) + epsilon)
    after_step = own_rows - inner_rate * gradient / grad_scale
    replicas = lax.axis_size("replica")
    whole_global = lax.all_gather(global_weight, "replica", axis=1, tiled=True)
    outer_delta = (
        lax.psum_scatter(whole_global - after_step, "replica", scatter_dimension=1, tiled=True)
        / replicas
    )
    next_momentum = keep_rate * outer_momentum + late_delta
    next_global = global_weight - outer_rate * (late_delta + keep_rate * next_momentum)
    new_rows = lax.all_gather(next_global, "replica", axis=1, tiled=True)
    next_local = blend_rate * new_rows + (1.0 - blend_rate) * after_step
    return (next_local[None], next_global, next_momentum, outer_delta)


def solution(mesh):
    in_specs = (
        P("replica", "fsdp", None),
        P("replica", "fsdp", None),
        P(),
        P("replica", "fsdp", None),
        P("fsdp", "replica"),
        P("fsdp", "replica"),
        P("fsdp", "replica"),
    )
    out_specs = (
        P("replica", "fsdp", None),
        P("fsdp", "replica"),
        P("fsdp", "replica"),
        P("fsdp", "replica"),
    )
    return jax.shard_map(shards, mesh=mesh, in_specs=in_specs, out_specs=out_specs, check_vma=False)
```

profile of v0, /device:TPU:1, one launch (start us, length us, event | category | flops | bytes accessed | tf_op | source)
XLA Modules:
  0.0 460.0 jit_solution(13017366998081578982)
XLA Ops:
  7.2 1.4 copy.15
  8.6 0.7 bitcast_convert_fusion
  9.5 0.1 reshape.54
  9.6 147.5 %all-gather.3.cloned.1.call-done = bf16[8192,512]{0,1:T(8,128)(2,1)} async-done(((bf16[256,512]{0,1:T(8,128)(2,1)}), bf16[8192,512]{0,1:T(8,128)(2,1)}) %all-gather.3.cloned.1.call-update) | async-done | bytes 8388624 | tf_op jit(solution)/shard_map/all_gather | solution.py:31
  157.0 6.3 %fusion.2 = f32[128,512]{1,0:T(8,128)S(1)} fusion(bf16[8192,512]{0,1:T(8,128)(2,1)} %all-gather.3.cloned.1.call-done, bf16[1,128,8192]{2,1,0:T(8,128)(2,1)S(1)} %copy-done), kind=kOutput, calls=%fused_computation.2 | convolution fusion | flops 1073807360 | bytes 10747904 | tf_op jit(solution)/shard_map/dot_general | solution.py:29
  163.3 0.1 reshape.52
  163.4 0.2 multiply_reduce_fusion.1
  163.7 0.4 fusion.8
  164.1 0.2 mul.95
  164.3 0.2 div.49
  164.5 0.8 fusion.7
  165.3 2.4 copy.16
  167.7 10.9 %all-to-all-start = ((bf16[128,32,256]{0,2,1:T(8,128)(2,1)}), bf16[128,32,256]{0,2,1:T(8,128)(2,1)S(1)}, u32[]{:S(2)}, u32[]{:S(2)}) async-start(bf16[128,32,256]{0,2,1:T(8,128)(2,1)} %bitcast.48), calls=%async_computation | async-start | bytes 4194304 | tf_op jit(solution)/shard_map/all_to_all | solution.py:42
  178.6 0.6 multiply_subtract_fusion
  179.3 66.9 %all_gather.15 = f32[256,512]{0,1:T(8,128)S(1)} all-gather(f32[256,32]{0,1:T(8,128)S(1)} %copy-done.3), channel_id=1, replica_groups=mesh['replica'=16,'fsdp'=32] {'replica'}, dimensions={1}, use_global_device_ids=true | all-gather | bytes 557056 | tf_op jit(solution)/shard_map/all_gather | solution.py:57
  246.2 21.2 %all_gather.12 = f32[256,512]{0,1:T(8,128)} all-gather(f32[256,32]{0,1:T(8,128)S(1)} %get-tuple-element.16), channel_id=1, replica_groups=mesh['replica'=16,'fsdp'=32] {'replica'}, dimensions={1}, use_global_device_ids=true | all-gather | bytes 557056 | tf_op jit(solution)/shard_map/all_gather | solution.py:64
  267.5 2.9 copy.17
  270.3 34.9 %all-gather.5.cloned.1.call-done = bf16[4096,512]{1,0:T(8,128)(2,1)} async-done(((bf16[128,512]{1,0:T(8,128)(2,1)}), bf16[4096,512]{1,0:T(8,128)(2,1)}) %all-gather.5.cloned.1.call-update) | async-done | bytes 4194320 | tf_op jit(solution)/shard_map/all_gather | solution.py:47
  305.2 4.8 %multiply_reduce_fusion = (f32[]{:T(128)}, f32[512,256]{1,0:T(8,128)S(1)}) fusion(bf16[4096,512]{1,0:T(8,128)(2,1)} %all-gather.5.cloned.1.call-done, bf16[4096,256]{1,0:T(8,128)(2,1)} %bitcast.49), kind=kOutput, calls=%fused_computation.6 | convolution fusion | flops 1074135040 | bytes 6815748 | tf_op jit(solution)/shard_map/dot_general | solution.py:45
  310.0 67.6 %psum.7 = f32[]{:T(128)} all-reduce(f32[]{:T(128)} %get-tuple-element.20), channel_id=1, replica_groups=mesh['replica'=16,'fsdp'=32] {'fsdp'}, use_global_device_ids=true, to_apply=%region_3.0 | all-reduce | flops 1 | bytes 8 | tf_op jit(solution)/shard_map/psum | solution.py:53
  378.3 0.9 fusion.9
  379.3 1.0 copy.18
  380.3 71.8 %reduce-scatter.2.cloned.1.call-done = f32[256,32]{0,1:T(8,128)} async-done(((f32[256,512]{0,1:T(8,128)}), f32[256,32]{0,1:T(8,128)}) %reduce-scatter.2.cloned.1.call-update) | async-done | bytes 32784 | tf_op jit(solution)/shard_map/reduce_scatter | solution.py:59
  452.1 1.4 broadcast_multiply_fusion.1
  (26 shorter events, 0.2 us)
Async XLA Ops:
  7.2 2.3 copy-start.2
  7.2 2.4 copy-start.7
  7.2 149.9 %copy-start = (bf16[1,128,8192]{2,1,0:T(8,128)(2,1)S(1)}, bf16[1,128,8192]{2,1,0:T(8,128)(2,1)}, u32[]{:S(2)}) copy-start(bf16[1,128,8192]{2,1,0:T(8,128)(2,1)} %param.7) | copy-start | bytes 6291460
  7.2 149.8 %all-gather.3.cloned.1.call-start = ((), (), s32[]{:S(2)}) async-start(), calls=%async_computation.2 | async-start | bytes 8650752 | tf_op jit(solution)/shard_map/all_gather | solution.py:31
  9.4 295.8 %all-gather.5.cloned.1.call-start = ((), (), s32[]{:S(2)}) async-start(), calls=%async_computation.3 | async-start | bytes 4325376 | tf_op jit(solution)/shard_map/all_gather | solution.py:47
  167.7 10.9 %copy-start.3 = (f32[256,32]{0,1:T(8,128)S(1)}, f32[256,32]{0,1:T(8,128)}, u32[]{:S(2)}) copy-start(f32[256,32]{0,1:T(8,128)} %param.11) | copy-start | bytes 98308
  167.7 10.9 %copy-start.5 = (f32[256,32]{0,1:T(8,128)S(1)}, f32[256,32]{0,1:T(8,128)}, u32[]{:S(2)}) copy-start(f32[256,32]{0,1:T(8,128)} %param.13) | copy-start | bytes 98308
  167.7 10.9 %copy-start.6 = (f32[256,32]{0,1:T(8,128)S(1)}, f32[256,32]{0,1:T(8,128)}, u32[]{:S(2)}) copy-start(f32[256,32]{0,1:T(8,128)} %param.12) | copy-start | bytes 98308
  167.7 99.8 %all-to-all-start = ((bf16[128,32,256]{0,2,1:T(8,128)(2,1)}), bf16[128,32,256]{0,2,1:T(8,128)(2,1)S(1)}, u32[]{:S(2)}, u32[]{:S(2)}) async-start(bf16[128,32,256]{0,2,1:T(8,128)(2,1)} %bitcast.48), calls=%async_computation | async-start | bytes 4194304 | tf_op jit(solution)/shard_map/all_to_all | solution.py:42
  178.6 273.5 %reduce-scatter.2.cloned.1.call-start = ((), (), s32[]{:S(2)}) async-start(), calls=%async_computation.4 | async-start | bytes 557056 | tf_op jit(solution)/shard_map/reduce_scatter | solution.py:59
  179.3 91.1 %copy-start.4 = (f32[256,32]{0,1:T(8,128)}, f32[256,32]{0,1:T(8,128)S(1)}, u32[]{:S(2)}) copy-start(f32[256,32]{0,1:T(8,128)S(1)} %get-tuple-element.16) | copy-start | bytes 98308
  305.2 73.1 %copy-start.1 = (f32[256,512]{0,1:T(8,128)S(1)}, f32[256,512]{0,1:T(8,128)}, u32[]{:S(2)}) copy-start(f32[256,512]{0,1:T(8,128)} %all_gather.12) | copy-start | bytes 1572868
Sparse Core Ops, SparseCore 0:
  11.6 145.3 all-gather.2
  165.4 139.7 all-gather.4
  379.4 72.6 reduce-scatter.1
where the time goes:
time: 462 us; the launch traced here: 460 us
  waiting for transfers between devices  254 us (55%)
  blocking collectives  156 us (34%)
  between operations  14.6 us (3%)
  matrix products  11.1 us (2%)
  starting transfers between devices  11 us (2%)
  local copies, waits for them, and re-layouts  8.31 us (2%)
  other arithmetic  5.02 us (1%)
    all_gather x1, waiting for transfers between devices, shards(): lax.all_gather(weight_copy, 'fsdp', axis=0, tiled=True)  147 us
    reduce_scatter x1, waiting for transfers between devices, shards(): lax.psum_scatter(whole_global - after_step, 'replica', scatter_dimension=...  71.8 us
    psum x1, blocking collectives, shards(): squares = lax.psum(jnp.sum(gradient * gradient), 'fsdp')  67.6 us
    all_gather x1, blocking collectives, shards(): whole_global = lax.all_gather(global_weight, 'replica', axis=1, tiled=True)  66.9 us
    all_gather x1, waiting for transfers between devices, shards(): lax.all_gather(key_slope, 'fsdp', axis=0, tiled=True)  34.9 us
    all_gather x1, blocking collectives, shards(): new_rows = lax.all_gather(next_global, 'replica', axis=1, tiled=True)  21.2 us
    all_to_all x1, starting transfers between devices, shards(): lax.all_to_all(feats, 'fsdp', split_axis=1, concat_axis=0, tiled=True)  10.9 us
  transfers between devices with their start and end apart: 4, of which 3 were waited for; matrix products, arithmetic and copies ran while one was open for 2% of the time, Pallas kernels for 0%

commit v1 on v0

v1 whole, which is shorter than its diff:
```python
import functools

import jax
import jax.numpy as jnp
from jax import lax
from jax.experimental import pallas as pl
from jax.experimental.pallas import tpu as pltpu
from jax.sharding import Mesh
from jax.sharding import PartitionSpec as P

HEAD = 128

inner_rate = 0.5
outer_rate = 0.7
keep_rate = 0.9
blend_rate = 0.5
epsilon = 1e-06

REPLICA = ("y_lo", "x", "core")
FSDP = ("z", "y_hi")


def slope_kernel(factor, parts_ref, cotangent_ref, gain_ref, out_ref):
    pieces = parts_ref.shape[0]
    gain = gain_ref[...]
    for head in range(out_ref.shape[2] // HEAD):
        lanes = slice(head * HEAD, (head + 1) * HEAD)
        hidden = parts_ref[0, :, lanes].astype(jnp.float32)
        for piece in range(1, pieces):
            hidden = hidden + parts_ref[piece, :, lanes].astype(jnp.float32)
        hidden = hidden * factor
        spread = jnp.sqrt(jnp.mean(hidden * hidden, axis=-1, keepdims=True) + epsilon)
        unit = hidden / spread
        slope = cotangent_ref[:, lanes].astype(jnp.float32) * gain
        key_slope = (slope - unit * jnp.mean(slope * unit, axis=-1, keepdims=True)) / spread
        key_slope = key_slope.astype(jnp.bfloat16)
        for piece in range(out_ref.shape[0]):
            out_ref[piece, :, lanes] = key_slope


def key_slopes(parts, cotangent, gain, factor):
    return pl.pallas_call(
        functools.partial(slope_kernel, factor),
        out_shape=jax.ShapeDtypeStruct(parts.shape, jnp.bfloat16),
        compiler_params=pltpu.CompilerParams(vmem_limit_bytes=16 * 1024 * 1024),
        cost_estimate=pl.CostEstimate(flops=2_000_000, bytes_accessed=2_500_000, transcendentals=2000),
    )(parts, cotangent, gain)


def split_kernel(feats_ref, out_ref, sems):
    pieces, _, width = out_ref.shape
    copies = [
        pltpu.make_async_copy(feats_ref.at[:, pl.ds(i * width, width)], out_ref.at[i], sems.at[i])
        for i in range(pieces)
    ]
    for copy in copies:
        copy.start()
    for copy in copies:
        copy.wait()


def split_columns(feats, pieces):
    tokens, width = feats.shape
    return pl.pallas_call(
        split_kernel,
        out_shape=jax.ShapeDtypeStruct((pieces, tokens, width // pieces), feats.dtype),
        in_specs=[pl.BlockSpec(memory_space=pl.ANY)],
        out_specs=pl.BlockSpec(memory_space=pl.ANY),
        scratch_shapes=[pltpu.SemaphoreType.DMA((pieces,))],
        compiler_params=pltpu.CompilerParams(vmem_limit_bytes=16 * 1024 * 1024),
        cost_estimate=pl.CostEstimate(flops=0, bytes_accessed=4 * tokens * width, transcendentals=0),
    )(feats)


def gather_by_permutes(x, axis):
    size = lax.axis_size(axis)
    me = lax.axis_index(axis)
    out = jnp.zeros((size,) + x.shape, x.dtype)
    for step in range(size):
        piece = x
        if step:
            piece = lax.ppermute(x, axis, [(i, (i + step) % size) for i in range(size)])
        out = lax.dynamic_update_index_in_dim(out, piece, lax.rem(me + size - step, size), 0)
    return out


def shards(
    activations, key_cotangent, key_gain, local_weight, global_weight, outer_momentum, late_delta
):
    feats = activations[0]
    own_rows = local_weight[0]
    tokens, width = feats.shape
    rows, columns = own_rows.shape
    factor = width ** (-0.5)
    z_size = lax.axis_size("z")
    y_size = lax.axis_size("y_hi")
    replicas = lax.axis_size(REPLICA)

    owned = lax.all_to_all(split_columns(feats, z_size), "z", 0, 0)
    owned = owned.reshape(z_size * tokens, width // z_size)

    weight = gather_by_permutes(own_rows.astype(jnp.bfloat16), "y_hi").reshape(-1, columns)
    global_t, momentum_t, late_t = global_weight.T, outer_momentum.T, late_delta.T
    next_momentum_t = keep_rate * momentum_t + late_t
    next_global_t = global_t - outer_rate * (late_t + keep_rate * next_momentum_t)
    new_rows_t = gather_by_permutes(next_global_t, "core")
    new_rows_t = gather_by_permutes(new_rows_t, "y_lo")
    new_rows_t = gather_by_permutes(new_rows_t, "x")
    new_rows = new_rows_t.transpose(1, 0, 2, 3, 4).reshape(columns, rows).T

    partial_hidden = jnp.dot(owned, weight, preferred_element_type=jnp.float32).astype(jnp.bfloat16)
    parts = lax.all_to_all(partial_hidden.reshape(z_size, tokens, columns), "z", 0, 0)
    slopes = key_slopes(parts, key_cotangent[0], key_gain.reshape(1, HEAD), factor)
    slopes = lax.all_to_all(slopes, "z", 0, 0).reshape(z_size * tokens, columns)

    bound = 30.0 * slopes.shape[0] * jnp.max(jnp.abs(slopes)).astype(jnp.float32)
    exponent = jnp.ceil(jnp.log2(jnp.maximum(bound, 1e-30))) - 15.0
    scaled = lax.dot_general(
        owned, slopes, (((0,), (0,)), ((), ())), preferred_element_type=jnp.float32
    ) * jnp.exp2(-exponent)
    scaled = scaled.astype(jnp.float16).reshape(y_size, rows, columns)
    marks = jnp.full((y_size, 16, columns), exponent, jnp.float32).astype(jnp.float16)
    pieces = lax.all_to_all(jnp.concatenate([scaled, marks], axis=1), "y_hi", 0, 0)
    unscale = jnp.exp2(pieces[:, rows, 0].astype(jnp.float32)) * factor
    gradient = jnp.sum(pieces[:, :rows].astype(jnp.float32) * unscale[:, None, None], axis=0)

    squares = jnp.sum(gradient * gradient)
    shares = lax.all_to_all(jnp.broadcast_to(squares, (z_size * y_size, 1, 128)), FSDP, 0, 0)
    squares = jnp.sum(shares[:, 0, 0])
    grad_scale = jnp.sqrt(squares / (width * columns) + epsilon)
    after_step = own_rows - inner_rate * gradient / grad_scale

    sent_rows = after_step.T.reshape(replicas, columns // replicas, rows)
    received = lax.all_to_all(sent_rows, REPLICA, 0, 0)
    outer_delta_t = global_t - jnp.sum(received, axis=0) / replicas
    next_local = blend_rate * new_rows + (1.0 - blend_rate) * after_step
    return (next_local[None], next_global_t.T, next_momentum_t.T, outer_delta_t.T)


def solution(mesh):
    split = Mesh(mesh.devices.reshape(2, 4, 2, 8, 4), ("y_lo", "x", "core", "z", "y_hi"))
    whole = P(REPLICA, FSDP, None)
    outer = P(FSDP, REPLICA)
    return jax.shard_map(
        shards,
        mesh=split,
        in_specs=(whole, whole, P(), whole, outer, outer, outer),
        out_specs=(whole, outer, outer, outer),
        check_vma=False,
    )
```

time: 462 us -> 222 us (0.48)
  waiting for transfers between devices: 254 us -> 48.7 us
  blocking collectives: 156 us -> 82.7 us
  starting transfers between devices: 11 us -> 62.5 us
  between operations: 14.6 us -> 2.46 us
  matrix products: 11.1 us -> 5.73 us
    all_gather x2 -> x0, waiting for transfers between devices: 182 us -> none  [the longest x1 147 us: shards(): lax.all_gather(weight_copy, 'fsdp', axis=0, tiled=True)]
    all_gather x2 -> x0, blocking collectives: 88.2 us -> none  [the longest x1 66.9 us: shards(): whole_global = lax.all_gather(global_weight, 'replica', axis=1, tiled=True)]
    all_to_all x0 -> x3, blocking collectives: none -> 82.7 us  [the longest x1 30.5 us: shards(): lax.all_to_all(partial_hidden.reshape(z_size, tokens, columns), 'z', 0, 0)]
    reduce_scatter x1 -> x0, waiting for transfers between devices: 71.8 us -> none  [shards(): lax.psum_scatter(whole_global - after_step, 'replica', scatter_dimension=...]
    psum x1 -> x0, blocking collectives: 67.6 us -> none  [shards(): squares = lax.psum(jnp.sum(gradient * gradient), 'fsdp')]
    ppermute x0 -> x8, starting transfers between devices: none -> 34 us  [gather_by_permutes(): piece = lax.ppermute(x, axis, [(i, (i + step) % size) for i in range(size)])]
    ppermute x0 -> x8, waiting for transfers between devices: none -> 24.5 us  [gather_by_permutes(): piece = lax.ppermute(x, axis, [(i, (i + step) % size) for i in range(size)])]
    all_to_all x1 -> x3, waiting for transfers between devices: 0.01 us -> 24.2 us  [the longest x1 13.5 us: shards(): owned = lax.all_to_all(split_columns(feats, z_size), 'z', 0, 0)]
  transfers between devices with their start and end apart: 4 -> 11, of which waited for: 3 -> 6; matrix products, arithmetic and copies ran while one was open for 2% -> 4% of each run, Pallas kernels for 0% -> 0%
where the time goes in v1:
time: 222 us; the launch traced here: 221 us
  blocking collectives  82.7 us (37%)
  starting transfers between devices  62.5 us (28%)
  waiting for transfers between devices  48.7 us (22%)
  local copies, waits for them, and re-layouts  12.4 us (6%)
  matrix products  5.73 us (3%)
  other arithmetic  5 us (2%)
  between operations  2.46 us (1%)
    ppermute x8, starting transfers between devices, gather_by_permutes(): piece = lax.ppermute(x, axis, [(i, (i + step) % size) for i in range(size)])  34 us
    all_to_all x1, blocking collectives, shards(): lax.all_to_all(partial_hidden.reshape(z_size, tokens, columns), 'z', 0, 0)  30.5 us
    all_to_all x1, blocking collectives, shards(): slopes = lax.all_to_all(slopes, 'z', 0, 0).reshape(z_size * tokens, columns)  28.8 us
    ppermute x8, waiting for transfers between devices, gather_by_permutes(): piece = lax.ppermute(x, axis, [(i, (i + step) % size) for i in range(size)])  24.5 us
    all_to_all x1, blocking collectives, shards(): received = lax.all_to_all(sent_rows, REPLICA, 0, 0)  23.4 us
    all_to_all x1, waiting for transfers between devices, shards(): owned = lax.all_to_all(split_columns(feats, z_size), 'z', 0, 0)  13.5 us
    all_to_all x1, starting transfers between devices, shards(): owned = lax.all_to_all(split_columns(feats, z_size), 'z', 0, 0)  11 us
    all_to_all x1, starting transfers between devices, shards(): lax.all_to_all(jnp.broadcast_to(squares, (z_size * y_size, 1, 128)), FSDP...  10.7 us
  transfers between devices with their start and end apart: 11, of which 6 were waited for; matrix products, arithmetic and copies ran while one was open for 4% of the time, Pallas kernels for 0%

profile of v1, /device:TPU:1, one launch (start us, length us, event | category | flops | bytes accessed | tf_op | source)
XLA Modules:
  0.0 221.3 jit_solution(15701374358883308457)
XLA Ops:
  0.6 1.6 copy-done
  3.7 11.0 %all-to-all-start = ((bf16[8,128,1024]{2,1,0:T(8,128)(2,1)}), bf16[8,128,1024]{2,1,0:T(8,128)(2,1)S(1)}, u32[]{:S(2)}, u32[]{:S(2)}) async-start(bf16[8,128,1024]{2,1,0:T(8,128)(2,1)} %shard_map.102), calls=%async_computation | async-start | bytes 4194304 | tf_op jit(solution)/shard_map/all_to_all | solution.py:99
  14.7 4.2 %collective-permute-start.5 = (bf16[256,512]{1,0:T(8,128)(2,1)S(1)}, bf16[256,512]{1,0:T(8,128)(2,1)}, u32[]{:S(2)}, u32[]{:S(2)}) collective-permute-start(bf16[256,512]{1,0:T(8,128)(2,1)S(1)} %bitcast_convert_fusion), channel_id=1, source_target_pairs={{0,1},{1,2},{2,3},{3,0},{4,5},{5,6},{6,7},{7,4},{8,9},{9,10},{10,1... | collective-permute-start | bytes 786440 | tf_op jit(solution)/shard_map/ppermute | solution.py:82
  18.9 5.7 %collective-permute-start.6 = (bf16[256,512]{1,0:T(8,128)(2,1)S(1)}, bf16[256,512]{1,0:T(8,128)(2,1)S(1)}, u32[]{:S(2)}, u32[]{:S(2)}) collective-permute-start(bf16[256,512]{1,0:T(8,128)(2,1)S(1)} %bitcast_convert_fusion), channel_id=1, source_target_pairs={{0,2},{1,3},{2,0},{3,1},{4,6},{5,7},{6,4},{7,5},{8,10},{9,11},{10,... | collective-permute-start | bytes 786440 | tf_op jit(solution)/shard_map/ppermute | solution.py:82
  24.6 5.0 %collective-permute-start.7 = (bf16[256,512]{1,0:T(8,128)(2,1)S(1)}, bf16[256,512]{1,0:T(8,128)(2,1)S(1)}, u32[]{:S(2)}, u32[]{:S(2)}) collective-permute-start(bf16[256,512]{1,0:T(8,128)(2,1)S(1)} %bitcast_convert_fusion), channel_id=1, source_target_pairs={{0,3},{1,0},{2,1},{3,2},{4,7},{5,4},{6,5},{7,6},{8,11},{9,8},{10,9... | collective-permute-start | bytes 786440 | tf_op jit(solution)/shard_map/ppermute | solution.py:82
  31.4 1.7 bitcast_dynamic-update-slice_fusion.2
  33.1 7.0 %collective-permute-done.6 = bf16[256,512]{1,0:T(8,128)(2,1)S(1)} collective-permute-done((bf16[256,512]{1,0:T(8,128)(2,1)S(1)}, bf16[256,512]{1,0:T(8,128)(2,1)S(1)}, u32[]{:S(2)}, u32[]{:S(2)}) %collective-permute-start.6) | collective-permute-done | bytes 262176 | tf_op jit(solution)/shard_map/ppermute | solution.py:82
  40.9 8.0 %collective-permute-done.7 = bf16[256,512]{1,0:T(8,128)(2,1)S(1)} collective-permute-done((bf16[256,512]{1,0:T(8,128)(2,1)S(1)}, bf16[256,512]{1,0:T(8,128)(2,1)S(1)}, u32[]{:S(2)}, u32[]{:S(2)}) %collective-permute-start.7) | collective-permute-done | bytes 262176 | tf_op jit(solution)/shard_map/ppermute | solution.py:82
  49.6 13.5 %all-to-all-done = bf16[8,128,1024]{2,1,0:T(8,128)(2,1)S(1)} async-done(((bf16[8,128,1024]{2,1,0:T(8,128)(2,1)}), bf16[8,128,1024]{2,1,0:T(8,128)(2,1)S(1)}, u32[]{:S(2)}, u32[]{:S(2)}) %all-to-all-start) | async-done | bytes 2097184 | tf_op jit(solution)/shard_map/all_to_all | solution.py:99
  63.1 3.5 %fusion.1 = bf16[1024,512]{0,1:T(8,128)(2,1)} fusion(bf16[1024,512]{1,0:T(8,128)(2,1)} %bitcast.21, bf16[1024,1024]{1,0:T(8,128)(2,1)S(1)} %bitcast.92), kind=kOutput, calls=%fused_computation.4 | convolution fusion | flops 1074266112 | bytes 4194304 | tf_op jit(solution)/shard_map/dot_general | solution.py:111
  68.1 30.5 %all_to_all.30.parts_ref = bf16[8,128,512]{2,1,0:T(8,128)(2,1)S(1)} all-to-all(bf16[8,128,512]{2,1,0:T(8,128)(2,1)S(1)} %bitcast.94), channel_id=1, replica_groups=mesh['y_lo'=2,'x'=4,'core'=2,'z'=8,'y_hi'=4] {'z'}, dimensions={0} | all-to-all | bytes 2097152 | tf_op jit(solution)/shard_map/all_to_all | solution.py:112
  99.1 28.8 %all_to_all.31 = bf16[8,128,512]{2,1,0:T(8,128)(2,1)S(1)} all-to-all(bf16[8,128,512]{2,1,0:T(8,128)(2,1)S(1)} %shard_map.103), channel_id=1, replica_groups=mesh['y_lo'=2,'x'=4,'core'=2,'z'=8,'y_hi'=4] {'z'}, dimensions={0} | all-to-all | bytes 2097152 | tf_op jit(solution)/shard_map/all_to_all | solution.py:114
  129.4 2.2 %fusion.2 = f16[1024,512]{0,1:T(8,128)(2,1)} fusion(bf16[8,128,512]{2,1,0:T(8,128)(2,1)S(1)} %all_to_all.31, bf16[8,128,1024]{2,1,0:T(8,128)(2,1)S(1)} %all-to-all-done, f32[]{:T(128)S(6)} %exp2.15), kind=kOutput, calls=%fused_computation.5 | convolution fusion | flops 1074790400 | bytes 4194308 | tf_op jit(solution)/shard_map/dot_general | solution.py:118
  131.6 2.0 copy.75
  134.9 6.8 %all-to-all-start.3 = ((f16[4,272,512]{2,1,0:T(8,128)(2,1)}), f16[4,272,512]{2,1,0:T(8,128)(2,1)S(1)}, u32[]{:S(2)}, u32[]{:S(2)}) async-start(f16[4,272,512]{2,1,0:T(8,128)(2,1)} %concatenate.3), calls=%async_computation.3 | async-start | bytes 2228224 | tf_op jit(solution)/shard_map/all_to_all | solution.py:123
  141.8 6.3 %collective-permute-start = (f32[32,256]{1,0:T(8,128)S(1)}, f32[32,256]{1,0:T(8,128)S(1)}, u32[]{:S(2)}, u32[]{:S(2)}) collective-permute-start(f32[32,256]{1,0:T(8,128)S(1)} %get-tuple-element.15), channel_id=1, source_target_pairs={{0,32},{32,0},{1,33},{33,1},{2,34},{34,2},{3,35},{35,3},{4,36},{36... | collective-permute-start | bytes 98312 | tf_op jit(solution)/shard_map/ppermute | solution.py:82
  148.9 2.3 %collective-permute-start.1 = (f32[2,32,256]{2,1,0:T(8,128)S(1)}, f32[2,32,256]{2,1,0:T(8,128)S(1)}, u32[]{:S(2)}, u32[]{:S(2)}) collective-permute-start(f32[2,32,256]{2,1,0:T(8,128)S(1)} %bitcast_dynamic-update-slice_fusion.9), channel_id=1, source_target_pairs={{0,256},{256,0},{1,257},{257,1},{2,258},{258,2},{3,259},{259,3},{4... | collective-permute-start | bytes 196616 | tf_op jit(solution)/shard_map/ppermute | solution.py:82
  151.3 8.6 %collective-permute-done.1 = f32[2,32,256]{2,1,0:T(8,128)S(1)} collective-permute-done((f32[2,32,256]{2,1,0:T(8,128)S(1)}, f32[2,32,256]{2,1,0:T(8,128)S(1)}, u32[]{:S(2)}, u32[]{:S(2)}) %collective-permute-start.1) | collective-permute-done | bytes 65568 | tf_op jit(solution)/shard_map/ppermute | solution.py:82
  159.9 3.1 %collective-permute-start.2 = (f32[2,2,32,256]{3,2,1,0:T(8,128)S(1)}, f32[2,2,32,256]{3,2,1,0:T(8,128)S(1)}, u32[]{:S(2)}, u32[]{:S(2)}) collective-permute-start(f32[2,2,32,256]{3,2,1,0:T(8,128)S(1)} %bitcast_dynamic-update-slice_fusion.7), channel_id=1, source_target_pairs={{0,64},{64,128},{128,192},{192,0},{1,65},{65,129},{129,193},{193,1... | collective-permute-start | bytes 393224 | tf_op jit(solution)/shard_map/ppermute | solution.py:82
  163.0 4.4 %collective-permute-start.3 = (f32[2,2,32,256]{3,2,1,0:T(8,128)S(1)}, f32[2,2,32,256]{3,2,1,0:T(8,128)S(1)}, u32[]{:S(2)}, u32[]{:S(2)}) collective-permute-start(f32[2,2,32,256]{3,2,1,0:T(8,128)S(1)} %bitcast_dynamic-update-slice_fusion.7), channel_id=1, source_target_pairs={{0,128},{64,192},{128,0},{192,64},{1,129},{65,193},{129,1},{193,65... | collective-permute-start | bytes 393224 | tf_op jit(solution)/shard_map/ppermute | solution.py:82
  167.4 3.1 %collective-permute-start.4 = (f32[2,2,32,256]{3,2,1,0:T(8,128)S(1)}, f32[2,2,32,256]{3,2,1,0:T(8,128)S(1)}, u32[]{:S(2)}, u32[]{:S(2)}) collective-permute-start(f32[2,2,32,256]{3,2,1,0:T(8,128)S(1)} %bitcast_dynamic-update-slice_fusion.7), channel_id=1, source_target_pairs={{0,192},{64,0},{128,64},{192,128},{1,193},{65,1},{129,65},{193,129... | collective-permute-start | bytes 393224 | tf_op jit(solution)/shard_map/ppermute | solution.py:82
  173.1 10.7 %all-to-all-start.4 = ((f32[32,1,128]{2,1,0:T(1,128)}), f32[32,1,128]{2,1,0:T(1,128)S(1)}, u32[]{:S(2)}, u32[]{:S(2)}) async-start(f32[32,1,128]{2,1,0:T(1,128)} %broadcast_in_dim.73), calls=%async_computation.4 | async-start | bytes 32768 | tf_op jit(solution)/shard_map/all_to_all | solution.py:128
  184.0 10.7 %all-to-all-done.4 = f32[32,1,128]{2,1,0:T(1,128)S(1)} async-done(((f32[32,1,128]{2,1,0:T(1,128)}), f32[32,1,128]{2,1,0:T(1,128)S(1)}, u32[]{:S(2)}, u32[]{:S(2)}) %all-to-all-start.4) | async-done | bytes 16416 | tf_op jit(solution)/shard_map/all_to_all | solution.py:128
  197.2 23.4 %all_to_all.32 = f32[16,32,256]{2,1,0:T(8,128)S(1)} all-to-all(f32[16,32,256]{2,1,0:T(8,128)S(1)} %bitcast.96), channel_id=1, replica_groups=mesh['y_lo'=2,'x'=4,'core'=2,'z'=8,'y_hi'=4] {'y_lo','x','core'}, dimensions={0} | all-to-all | bytes 1048576 | tf_op jit(solution)/shard_map/all_to_all | solution.py:134
  (52 shorter events, 14.8 us)
Async XLA Ops:
  0.6 1.6 copy-start
  3.6 11.0 %copy-start.3 = (f32[1,256,512]{2,1,0:T(8,128)S(1)}, f32[1,256,512]{2,1,0:T(8,128)}, u32[]{:S(2)}) copy-start(f32[1,256,512]{2,1,0:T(8,128)} %param.10) | copy-start | bytes 1572868
  3.7 59.4 %all-to-all-start = ((bf16[8,128,1024]{2,1,0:T(8,128)(2,1)}), bf16[8,128,1024]{2,1,0:T(8,128)(2,1)S(1)}, u32[]{:S(2)}, u32[]{:S(2)}) async-start(bf16[8,128,1024]{2,1,0:T(8,128)(2,1)} %shard_map.102), calls=%async_computation | async-start | bytes 4194304 | tf_op jit(solution)/shard_map/all_to_all | solution.py:99
  14.7 16.7 %collective-permute-start.5 = (bf16[256,512]{1,0:T(8,128)(2,1)S(1)}, bf16[256,512]{1,0:T(8,128)(2,1)}, u32[]{:S(2)}, u32[]{:S(2)}) collective-permute-start(bf16[256,512]{1,0:T(8,128)(2,1)S(1)} %bitcast_convert_fusion), channel_id=1, source_target_pairs={{0,1},{1,2},{2,3},{3,0},{4,5},{5,6},{6,7},{7,4},{8,9},{9,10},{10,1... | collective-permute-start | bytes 786440 | tf_op jit(solution)/shard_map/ppermute | solution.py:82
  18.9 21.2 %collective-permute-start.6 = (bf16[256,512]{1,0:T(8,128)(2,1)S(1)}, bf16[256,512]{1,0:T(8,128)(2,1)S(1)}, u32[]{:S(2)}, u32[]{:S(2)}) collective-permute-start(bf16[256,512]{1,0:T(8,128)(2,1)S(1)} %bitcast_convert_fusion), channel_id=1, source_target_pairs={{0,2},{1,3},{2,0},{3,1},{4,6},{5,7},{6,4},{7,5},{8,10},{9,11},{10,... | collective-permute-start | bytes 786440 | tf_op jit(solution)/shard_map/ppermute | solution.py:82
  24.6 24.3 %collective-permute-start.7 = (bf16[256,512]{1,0:T(8,128)(2,1)S(1)}, bf16[256,512]{1,0:T(8,128)(2,1)S(1)}, u32[]{:S(2)}, u32[]{:S(2)}) collective-permute-start(bf16[256,512]{1,0:T(8,128)(2,1)S(1)} %bitcast_convert_fusion), channel_id=1, source_target_pairs={{0,3},{1,0},{2,1},{3,2},{4,7},{5,4},{6,5},{7,6},{8,11},{9,8},{10,9... | collective-permute-start | bytes 786440 | tf_op jit(solution)/shard_map/ppermute | solution.py:82
  66.6 32.1 %copy-start.1 = (bf16[1,128,512]{2,1,0:T(8,128)(2,1)S(1)}, bf16[1,128,512]{2,1,0:T(8,128)(2,1)}, u32[]{:S(2)}) copy-start(bf16[1,128,512]{2,1,0:T(8,128)(2,1)} %param.8) | copy-start | bytes 393220
  66.6 32.1 %copy-start.2 = (f32[128]{0:T(128)S(1)}, f32[128]{0:T(128)}, u32[]{:S(2)}) copy-start(f32[128]{0:T(128)} %param.9) | copy-start | bytes 1540
  133.6 8.1 %copy-start.5 = (f32[256,32]{0,1:T(8,128)S(1)}, f32[256,32]{0,1:T(8,128)}, u32[]{:S(2)}) copy-start(f32[256,32]{0,1:T(8,128)} %param.12) | copy-start | bytes 98308
  133.7 8.1 %copy-start.6 = (f32[256,32]{0,1:T(8,128)S(1)}, f32[256,32]{0,1:T(8,128)}, u32[]{:S(2)}) copy-start(f32[256,32]{0,1:T(8,128)} %param.13) | copy-start | bytes 98308
  133.7 8.1 %copy-start.7 = (f32[256,32]{0,1:T(8,128)S(1)}, f32[256,32]{0,1:T(8,128)}, u32[]{:S(2)}) copy-start(f32[256,32]{0,1:T(8,128)} %param.11) | copy-start | bytes 98308
  134.9 35.7 %all-to-all-start.3 = ((f16[4,272,512]{2,1,0:T(8,128)(2,1)}), f16[4,272,512]{2,1,0:T(8,128)(2,1)S(1)}, u32[]{:S(2)}, u32[]{:S(2)}) async-start(f16[4,272,512]{2,1,0:T(8,128)(2,1)} %concatenate.3), calls=%async_computation.3 | async-start | bytes 2228224 | tf_op jit(solution)/shard_map/all_to_all | solution.py:123
  141.8 7.2 %collective-permute-start = (f32[32,256]{1,0:T(8,128)S(1)}, f32[32,256]{1,0:T(8,128)S(1)}, u32[]{:S(2)}, u32[]{:S(2)}) collective-permute-start(f32[32,256]{1,0:T(8,128)S(1)} %get-tuple-element.15), channel_id=1, source_target_pairs={{0,32},{32,0},{1,33},{33,1},{2,34},{34,2},{3,35},{35,3},{4,36},{36... | collective-permute-start | bytes 98312 | tf_op jit(solution)/shard_map/ppermute | solution.py:82
  148.9 10.9 %collective-permute-start.1 = (f32[2,32,256]{2,1,0:T(8,128)S(1)}, f32[2,32,256]{2,1,0:T(8,128)S(1)}, u32[]{:S(2)}, u32[]{:S(2)}) collective-permute-start(f32[2,32,256]{2,1,0:T(8,128)S(1)} %bitcast_dynamic-update-slice_fusion.9), channel_id=1, source_target_pairs={{0,256},{256,0},{1,257},{257,1},{2,258},{258,2},{3,259},{259,3},{4... | collective-permute-start | bytes 196616 | tf_op jit(solution)/shard_map/ppermute | solution.py:82
  159.9 10.6 %collective-permute-start.2 = (f32[2,2,32,256]{3,2,1,0:T(8,128)S(1)}, f32[2,2,32,256]{3,2,1,0:T(8,128)S(1)}, u32[]{:S(2)}, u32[]{:S(2)}) collective-permute-start(f32[2,2,32,256]{3,2,1,0:T(8,128)S(1)} %bitcast_dynamic-update-slice_fusion.7), channel_id=1, source_target_pairs={{0,64},{64,128},{128,192},{192,0},{1,65},{65,129},{129,193},{193,1... | collective-permute-start | bytes 393224 | tf_op jit(solution)/shard_map/ppermute | solution.py:82
  163.0 7.6 %collective-permute-start.3 = (f32[2,2,32,256]{3,2,1,0:T(8,128)S(1)}, f32[2,2,32,256]{3,2,1,0:T(8,128)S(1)}, u32[]{:S(2)}, u32[]{:S(2)}) collective-permute-start(f32[2,2,32,256]{3,2,1,0:T(8,128)S(1)} %bitcast_dynamic-update-slice_fusion.7), channel_id=1, source_target_pairs={{0,128},{64,192},{128,0},{192,64},{1,129},{65,193},{129,1},{193,65... | collective-permute-start | bytes 393224 | tf_op jit(solution)/shard_map/ppermute | solution.py:82
  167.4 16.4 %collective-permute-start.4 = (f32[2,2,32,256]{3,2,1,0:T(8,128)S(1)}, f32[2,2,32,256]{3,2,1,0:T(8,128)S(1)}, u32[]{:S(2)}, u32[]{:S(2)}) collective-permute-start(f32[2,2,32,256]{3,2,1,0:T(8,128)S(1)} %bitcast_dynamic-update-slice_fusion.7), channel_id=1, source_target_pairs={{0,192},{64,0},{128,64},{192,128},{1,193},{65,1},{129,65},{193,129... | collective-permute-start | bytes 393224 | tf_op jit(solution)/shard_map/ppermute | solution.py:82
  170.5 25.5 %copy-start.4 = (f32[1,256,512]{2,1,0:T(8,128)S(1)}, f32[1,256,512]{2,1,0:T(8,128)}, u32[]{:S(2)}) copy-start(f32[1,256,512]{2,1,0:T(8,128)} %param.10) | copy-start | bytes 1572868
  173.1 21.6 %all-to-all-start.4 = ((f32[32,1,128]{2,1,0:T(1,128)}), f32[32,1,128]{2,1,0:T(1,128)S(1)}, u32[]{:S(2)}, u32[]{:S(2)}) async-start(f32[32,1,128]{2,1,0:T(1,128)} %broadcast_in_dim.73), calls=%async_computation.4 | async-start | bytes 32768 | tf_op jit(solution)/shard_map/all_to_all | solution.py:128

commit v2 on v1

--- a/solution.py
+++ b/solution.py
@@ -84,6 +84,76 @@
     return out
 
 
+def project_kernel(owned_ref, weight_ref, out_ref):
+    out_ref[...] = jnp.dot(
+        owned_ref[...], weight_ref[...], preferred_element_type=jnp.float32
+    ).astype(out_ref.dtype)
+
+
+def project(owned, weight):
+    rows, depth = owned.shape
+    columns = weight.shape[1]
+    block = rows // 4
+    return pl.pallas_call(
+        project_kernel,
+        grid=(rows // block,),
+        out_shape=jax.ShapeDtypeStruct((rows, columns), jnp.bfloat16),
+        in_specs=[
+            pl.BlockSpec((block, depth), lambda i: (i, 0)),
+            pl.BlockSpec((depth, columns), lambda i: (0, 0)),
+        ],
+        out_specs=pl.BlockSpec((block, columns), lambda i: (i, 0)),
+        compiler_params=pltpu.CompilerParams(vmem_limit_bytes=24 * 1024 * 1024),
+        cost_estimate=pl.CostEstimate(
+            flops=2 * rows * depth * columns,
+            bytes_accessed=2 * (rows * depth + depth * columns + rows * columns),
+            transcendentals=0,
+        ),
+    )(owned, weight)
+
+
+MARKS = 16
+
+
+def gradient_kernel(owned_ref, slopes_ref, out_ref, exponent_ref):
+    @pl.when(pl.program_id(0) == 0)
+    def _():
+        largest = jnp.max(jnp.abs(slopes_ref[...]).astype(jnp.float32), axis=0, keepdims=True)
+        bound = 30.0 * slopes_ref.shape[0] * jnp.max(largest, axis=1, keepdims=True)
+        exponent = jnp.ceil(jnp.log2(jnp.maximum(bound, 1e-30))) - 15.0
+        exponent_ref[...] = jnp.broadcast_to(exponent, exponent_ref.shape)
+
+    rows = out_ref.shape[1] - MARKS
+    sums = lax.dot_general(
+        owned_ref[...], slopes_ref[...], (((0,), (0,)), ((), ())), preferred_element_type=jnp.float32
+    )
+    out_ref[0, :rows] = sums * jnp.exp2(-exponent_ref[0:1, 0:1])
+    out_ref[0, rows:] = jnp.broadcast_to(exponent_ref[0:1, 0:1], (MARKS, out_ref.shape[2]))
+
+
+def gradient_parts(owned, slopes, pieces):
+    tokens, width = owned.shape
+    columns = slopes.shape[1]
+    rows = width // pieces
+    return pl.pallas_call(
+        gradient_kernel,
+        grid=(pieces,),
+        out_shape=jax.ShapeDtypeStruct((pieces, rows + MARKS, columns), jnp.float32),
+        in_specs=[
+            pl.BlockSpec((tokens, rows), lambda i: (0, i)),
+            pl.BlockSpec((tokens, columns), lambda i: (0, 0)),
+        ],
+        out_specs=pl.BlockSpec((1, rows + MARKS, columns), lambda i: (i, 0, 0)),
+        scratch_shapes=[pltpu.VMEM((8, 128), jnp.float32)],
+        compiler_params=pltpu.CompilerParams(vmem_limit_bytes=24 * 1024 * 1024),
+        cost_estimate=pl.CostEstimate(
+            flops=2 * tokens * width * columns,
+            bytes_accessed=2 * (tokens * width + tokens * columns) + 4 * width * columns,
+            transcendentals=0,
+        ),
+    )(owned, slopes)
+
+
 def shards(
     activations, key_cotangent, key_gain, local_weight, global_weight, outer_momentum, late_delta
 ):
@@ -108,19 +178,14 @@
     new_rows_t = gather_by_permutes(new_rows_t, "x")
     new_rows = new_rows_t.transpose(1, 0, 2, 3, 4).reshape(columns, rows).T
 
-    partial_hidden = jnp.dot(owned, weight, preferred_element_type=jnp.float32).astype(jnp.bfloat16)
-    parts = lax.all_to_all(partial_hidden.reshape(z_size, tokens, columns), "z", 0, 0)
+    owned, weight, new_rows = lax.optimization_barrier((owned, weight, new_rows))
+    parts = project(owned, weight).reshape(z_size, tokens, columns)
+    parts = lax.all_to_all(parts, "z", 0, 0)
     slopes = key_slopes(parts, key_cotangent[0], key_gain.reshape(1, HEAD), factor)
     slopes = lax.all_to_all(slopes, "z", 0, 0).reshape(z_size * tokens, columns)
 
-    bound = 30.0 * slopes.shape[0] * jnp.max(jnp.abs(slopes)).astype(jnp.float32)
-    exponent = jnp.ceil(jnp.log2(jnp.maximum(bound, 1e-30))) - 15.0
-    scaled = lax.dot_general(
-        owned, slopes, (((0,), (0,)), ((), ())), preferred_element_type=jnp.float32
-    ) * jnp.exp2(-exponent)
-    scaled = scaled.astype(jnp.float16).reshape(y_size, rows, columns)
-    marks = jnp.full((y_size, 16, columns), exponent, jnp.float32).astype(jnp.float16)
-    pieces = lax.all_to_all(jnp.concatenate([scaled, marks], axis=1), "y_hi", 0, 0)
+    scaled = gradient_parts(owned, slopes, y_size).astype(jnp.float16)
+    pieces = lax.all_to_all(scaled, "y_hi", 0, 0)
     unscale = jnp.exp2(pieces[:, rows, 0].astype(jnp.float32)) * factor
     gradient = jnp.sum(pieces[:, :rows].astype(jnp.float32) * unscale[:, None, None], axis=0)
 
@@ -130,8 +195,8 @@
     grad_scale = jnp.sqrt(squares / (width * columns) + epsilon)
     after_step = own_rows - inner_rate * gradient / grad_scale
 
-    sent_rows = after_step.T.reshape(replicas, columns // replicas, rows)
-    received = lax.all_to_all(sent_rows, REPLICA, 0, 0)
+    sent_rows = after_step.T.reshape(replicas, columns // replicas, rows).astype(jnp.float16)
+    received = lax.all_to_all(sent_rows, REPLICA, 0, 0).astype(jnp.float32)
     outer_delta_t = global_t - jnp.sum(received, axis=0) / replicas
     next_local = blend_rate * new_rows + (1.0 - blend_rate) * after_step
     return (next_local[None], next_global_t.T, next_momentum_t.T, outer_delta_t.T)

time: 222 us -> 204 us (0.919)
  blocking collectives: 82.7 us -> 119 us
  waiting for transfers between devices: 48.7 us -> 19.8 us
  starting transfers between devices: 62.5 us -> 38.8 us
  matrix products: 5.73 us -> 0 us
  Pallas kernels: 1.87 us -> 5.02 us
    all_to_all x2 -> x4, blocking collectives: 53.9 us -> 91.2 us  [the longest x1 31.3 us: shards(): parts = lax.all_to_all(parts, 'z', 0, 0)]
    all_to_all x2 -> x0, starting transfers between devices: 17.5 us -> none  [the longest x1 10.7 us: shards(): lax.all_to_all(jnp.broadcast_to(squares, (z_size * y_size, 1, 128)), FSDP...]
    all_to_all x1, waiting for transfers between devices: 13.5 us -> 0.01 us  [shards(): owned = lax.all_to_all(split_columns(feats, z_size), 'z', 0, 0)]
    all_to_all x2 -> x0, waiting for transfers between devices: 10.7 us -> none  [the longest x1 10.7 us: shards(): lax.all_to_all(jnp.broadcast_to(squares, (z_size * y_size, 1, 128)), FSDP...]
    ppermute x8, starting transfers between devices: 34 us -> 27.8 us  [gather_by_permutes(): piece = lax.ppermute(x, axis, [(i, (i + step) % size) for i in range(size)])]
    dot_general x2 -> x0, matrix products: 5.73 us -> none  [the longest x1 3.49 us: shards(): jnp.dot(owned, weight, preferred_element_type=jnp.float32)]
    ppermute x8, waiting for transfers between devices: 24.5 us -> 19.8 us  [gather_by_permutes(): piece = lax.ppermute(x, axis, [(i, (i + step) % size) for i in range(size)])]
    pallas_call x0 -> x2, Pallas kernels: none -> 4.33 us  [the longest x1 2.56 us: gradient_parts(): pl.pallas_call(gradient_kernel, grid=(pieces,), out_shape=jax.ShapeDtypeS...]
  transfers between devices with their start and end apart: 11 -> 9, of which waited for: 6 -> 3; matrix products, arithmetic and copies ran while one was open for 4% -> 5% of each run, Pallas kernels for 0% -> 0%
where the time goes in v2:
time: 204 us; the launch traced here: 203 us
  blocking collectives  119 us (58%)
  starting transfers between devices  38.8 us (19%)
  waiting for transfers between devices  19.8 us (10%)
  local copies, waits for them, and re-layouts  13.2 us (6%)
  other arithmetic  5.5 us (3%)
  Pallas kernels  5.02 us (2%)
    all_to_all x1, blocking collectives, shards(): parts = lax.all_to_all(parts, 'z', 0, 0)  31.3 us
    all_to_all x1, blocking collectives, shards(): slopes = lax.all_to_all(slopes, 'z', 0, 0).reshape(z_size * tokens, columns)  28 us
    ppermute x8, starting transfers between devices, gather_by_permutes(): piece = lax.ppermute(x, axis, [(i, (i + step) % size) for i in range(size)])  27.8 us
    all_to_all x1, blocking collectives, shards(): pieces = lax.all_to_all(scaled, 'y_hi', 0, 0)  20.5 us
    all_to_all x1, blocking collectives, shards(): lax.all_to_all(jnp.broadcast_to(squares, (z_size * y_size, 1, 128)), FSDP...  19.8 us
    ppermute x8, waiting for transfers between devices, gather_by_permutes(): piece = lax.ppermute(x, axis, [(i, (i + step) % size) for i in range(size)])  19.8 us
    all_to_all x1, blocking collectives, shards(): received = lax.all_to_all(sent_rows, REPLICA, 0, 0).astype(jnp.float32)  19.5 us
    all_to_all x1, starting transfers between devices, shards(): owned = lax.all_to_all(split_columns(feats, z_size), 'z', 0, 0)  11 us
  transfers between devices with their start and end apart: 9, of which 3 were waited for; matrix products, arithmetic and copies ran while one was open for 5% of the time, Pallas kernels for 0%

profile of v2, /device:TPU:1, one launch (start us, length us, event | category | flops | bytes accessed | tf_op | source)
XLA Modules:
  0.0 203.4 jit_solution(6266163250058941342)
XLA Ops:
  0.6 1.6 copy-done.1
  2.5 1.3 copy-done
  3.8 11.0 %all-to-all-start = ((bf16[8,128,1024]{2,1,0:T(8,128)(2,1)}), bf16[8,128,1024]{2,1,0:T(8,128)(2,1)S(1)}, u32[]{:S(2)}, u32[]{:S(2)}) async-start(bf16[8,128,1024]{2,1,0:T(8,128)(2,1)} %copy-done), calls=%async_computation | async-start | bytes 4194304 | tf_op jit(solution)/shard_map/all_to_all | solution.py:169
  14.9 5.9 %collective-permute-start.2 = (bf16[256,512]{1,0:T(8,128)(2,1)S(1)}, bf16[256,512]{1,0:T(8,128)(2,1)}, u32[]{:S(2)}, u32[]{:S(2)}) collective-permute-start(bf16[256,512]{1,0:T(8,128)(2,1)S(1)} %bitcast_convert_fusion), channel_id=1, source_target_pairs={{0,3},{1,0},{2,1},{3,2},{4,7},{5,4},{6,5},{7,6},{8,11},{9,8},{10,9... | collective-permute-start | bytes 786440 | tf_op jit(solution)/shard_map/ppermute | solution.py:82
  20.8 3.5 %collective-permute-start.1 = (bf16[256,512]{1,0:T(8,128)(2,1)S(1)}, bf16[256,512]{1,0:T(8,128)(2,1)}, u32[]{:S(2)}, u32[]{:S(2)}) collective-permute-start(bf16[256,512]{1,0:T(8,128)(2,1)S(1)} %bitcast_convert_fusion), channel_id=1, source_target_pairs={{0,2},{1,3},{2,0},{3,1},{4,6},{5,7},{6,4},{7,5},{8,10},{9,11},{10,... | collective-permute-start | bytes 786440 | tf_op jit(solution)/shard_map/ppermute | solution.py:82
  24.3 4.2 %collective-permute-start = (bf16[256,512]{1,0:T(8,128)(2,1)S(1)}, bf16[256,512]{1,0:T(8,128)(2,1)}, u32[]{:S(2)}, u32[]{:S(2)}) collective-permute-start(bf16[256,512]{1,0:T(8,128)(2,1)S(1)} %bitcast_convert_fusion), channel_id=1, source_target_pairs={{0,1},{1,2},{2,3},{3,0},{4,5},{5,6},{6,7},{7,4},{8,9},{9,10},{10,1... | collective-permute-start | bytes 786440 | tf_op jit(solution)/shard_map/ppermute | solution.py:82
  29.2 3.7 %collective-permute-start.3 = (f32[32,256]{1,0:T(8,128)}, f32[32,256]{1,0:T(8,128)}, u32[]{:S(2)}, u32[]{:S(2)}) collective-permute-start(f32[32,256]{1,0:T(8,128)} %get-tuple-element.17), channel_id=1, source_target_pairs={{0,32},{32,0},{1,33},{33,1},{2,34},{34,2},{3,35},{35,3},{4,36},{36... | collective-permute-start | bytes 98312 | tf_op jit(solution)/shard_map/ppermute | solution.py:82
  33.0 1.1 convert_dynamic-update-slice_fusion
  34.9 2.3 %collective-permute-start.4 = (f32[2,32,256]{2,1,0:T(8,128)S(1)}, f32[2,32,256]{2,1,0:T(8,128)S(1)}, u32[]{:S(2)}, u32[]{:S(2)}) collective-permute-start(f32[2,32,256]{2,1,0:T(8,128)S(1)} %bitcast_dynamic-update-slice_fusion.9), channel_id=1, source_target_pairs={{0,256},{256,0},{1,257},{257,1},{2,258},{258,2},{3,259},{259,3},{4... | collective-permute-start | bytes 196616 | tf_op jit(solution)/shard_map/ppermute | solution.py:82
  37.3 11.3 %collective-permute-done.4 = f32[2,32,256]{2,1,0:T(8,128)S(1)} collective-permute-done((f32[2,32,256]{2,1,0:T(8,128)S(1)}, f32[2,32,256]{2,1,0:T(8,128)S(1)}, u32[]{:S(2)}, u32[]{:S(2)}) %collective-permute-start.4) | collective-permute-done | bytes 65568 | tf_op jit(solution)/shard_map/ppermute | solution.py:82
  48.6 4.4 %collective-permute-start.7 = (f32[2,2,32,256]{3,2,1,0:T(8,128)S(1)}, f32[2,2,32,256]{3,2,1,0:T(8,128)S(1)}, u32[]{:S(2)}, u32[]{:S(2)}) collective-permute-start(f32[2,2,32,256]{3,2,1,0:T(8,128)S(1)} %bitcast_dynamic-update-slice_fusion.7), channel_id=1, source_target_pairs={{0,192},{64,0},{128,64},{192,128},{1,193},{65,1},{129,65},{193,129... | collective-permute-start | bytes 393224 | tf_op jit(solution)/shard_map/ppermute | solution.py:82
  53.0 1.9 collective-permute-start.5
  56.4 3.9 %collective-permute-done.5 = f32[2,2,32,256]{3,2,1,0:T(8,128)S(1)} collective-permute-done((f32[2,2,32,256]{3,2,1,0:T(8,128)S(1)}, f32[2,2,32,256]{3,2,1,0:T(8,128)S(1)}, u32[]{:S(2)}, u32[]{:S(2)}) %collective-permute-start.5) | collective-permute-done | bytes 131104 | tf_op jit(solution)/shard_map/ppermute | solution.py:82
  60.3 1.9 collective-permute-start.6
  62.9 4.6 %collective-permute-done.6 = f32[2,2,32,256]{3,2,1,0:T(8,128)S(1)} collective-permute-done((f32[2,2,32,256]{3,2,1,0:T(8,128)S(1)}, f32[2,2,32,256]{3,2,1,0:T(8,128)S(1)}, u32[]{:S(2)}, u32[]{:S(2)}) %collective-permute-start.6) | collective-permute-done | bytes 131104 | tf_op jit(solution)/shard_map/ppermute | solution.py:82
  68.9 2.0 %copy.35 = f32[512,256]{0,1:T(8,128)} copy(f32[512,256]{1,0:T(8,128)} %bitcast.22) | data formatting | bytes 1048576 | tf_op jit(solution)/shard_map/reshape | solution.py:179
  73.9 1.8 shard_map.103
  75.7 31.3 %all_to_all.30.parts_ref = bf16[8,128,512]{2,1,0:T(8,128)(2,1)S(1)} all-to-all(bf16[8,128,512]{2,1,0:T(8,128)(2,1)S(1)} %bitcast.74), channel_id=1, replica_groups=mesh['y_lo'=2,'x'=4,'core'=2,'z'=8,'y_hi'=4] {'z'}, dimensions={0} | all-to-all | bytes 2097152 | tf_op jit(solution)/shard_map/all_to_all | solution.py:183
  107.5 28.0 %all_to_all.31 = bf16[8,128,512]{2,1,0:T(8,128)(2,1)S(1)} all-to-all(bf16[8,128,512]{2,1,0:T(8,128)(2,1)S(1)} %shard_map.104), channel_id=1, replica_groups=mesh['y_lo'=2,'x'=4,'core'=2,'z'=8,'y_hi'=4] {'z'}, dimensions={0} | all-to-all | bytes 2097152 | tf_op jit(solution)/shard_map/all_to_all | solution.py:185
  135.5 2.6 %shard_map.105 = f32[4,272,512]{2,1,0:T(8,128)S(1)} custom-call(bf16[1024,1024]{1,0:T(8,128)(2,1)S(1)} %bitcast.71, bf16[1024,512]{1,0:T(8,128)(2,1)S(1)} %bitcast.73), custom_call_target="tpu_custom_call" | custom-call | flops 1073741824 | bytes 5242880 | tf_op jit(solution)/shard_map/pallas_call | solution.py:138
  138.3 20.5 %all_to_all.32 = f16[4,272,512]{2,1,0:T(8,128)(2,1)S(1)} all-to-all(f16[4,272,512]{2,1,0:T(8,128)(2,1)S(1)} %convert_element_type.30), channel_id=1, replica_groups=mesh['y_lo'=2,'x'=4,'core'=2,'z'=8,'y_hi'=4] {'y_hi'}, dimensions={0} | all-to-all | bytes 2228224 | tf_op jit(solution)/shard_map/all_to_all | solution.py:188
  160.8 19.8 %all_to_all.33 = f32[32,1,128]{2,1,0:T(1,128)S(1)} all-to-all(f32[32,1,128]{2,1,0:T(1,128)S(1)} %broadcast_in_dim.72), channel_id=1, replica_groups=mesh['y_lo'=2,'x'=4,'core'=2,'z'=8,'y_hi'=4] {'z','y_hi'}, dimensions={0} | all-to-all | bytes 32768 | tf_op jit(solution)/shard_map/all_to_all | solution.py:193
  181.9 1.0 convert_bitcast_fusion
  183.2 19.5 %all_to_all.34 = f16[16,32,256]{2,1,0:T(8,128)(2,1)S(1)} all-to-all(f16[16,32,256]{2,1,0:T(8,128)(2,1)S(1)} %bitcast.79), channel_id=1, replica_groups=mesh['y_lo'=2,'x'=4,'core'=2,'z'=8,'y_hi'=4] {'y_lo','x','core'}, dimensions={0} | all-to-all | bytes 524288 | tf_op jit(solution)/shard_map/all_to_all | solution.py:199
  (53 shorter events, 12.4 us)
Async XLA Ops:
  0.6 1.6 copy-start.1
  2.5 1.3 copy-start
  3.8 11.0 %copy-start.4 = (f32[1,256,512]{2,1,0:T(8,128)S(1)}, f32[1,256,512]{2,1,0:T(8,128)}, u32[]{:S(2)}) copy-start(f32[1,256,512]{2,1,0:T(8,128)} %param.10) | copy-start | bytes 1572868
  3.8 24.8 %copy-start.7 = (f32[256,32]{0,1:T(8,128)S(1)}, f32[256,32]{0,1:T(8,128)}, u32[]{:S(2)}) copy-start(f32[256,32]{0,1:T(8,128)} %param.12) | copy-start | bytes 98308
  3.8 24.8 %copy-start.8 = (f32[256,32]{0,1:T(8,128)S(1)}, f32[256,32]{0,1:T(8,128)}, u32[]{:S(2)}) copy-start(f32[256,32]{0,1:T(8,128)} %param.13) | copy-start | bytes 98308
  3.8 24.8 %copy-start.9 = (f32[256,32]{0,1:T(8,128)S(1)}, f32[256,32]{0,1:T(8,128)}, u32[]{:S(2)}) copy-start(f32[256,32]{0,1:T(8,128)} %param.11) | copy-start | bytes 98308
  3.8 70.1 %all-to-all-start = ((bf16[8,128,1024]{2,1,0:T(8,128)(2,1)}), bf16[8,128,1024]{2,1,0:T(8,128)(2,1)S(1)}, u32[]{:S(2)}, u32[]{:S(2)}) async-start(bf16[8,128,1024]{2,1,0:T(8,128)(2,1)} %copy-done), calls=%async_computation | async-start | bytes 4194304 | tf_op jit(solution)/shard_map/all_to_all | solution.py:169
  14.9 58.0 %collective-permute-start.2 = (bf16[256,512]{1,0:T(8,128)(2,1)S(1)}, bf16[256,512]{1,0:T(8,128)(2,1)}, u32[]{:S(2)}, u32[]{:S(2)}) collective-permute-start(bf16[256,512]{1,0:T(8,128)(2,1)S(1)} %bitcast_convert_fusion), channel_id=1, source_target_pairs={{0,3},{1,0},{2,1},{3,2},{4,7},{5,4},{6,5},{7,6},{8,11},{9,8},{10,9... | collective-permute-start | bytes 786440 | tf_op jit(solution)/shard_map/ppermute | solution.py:82
  20.8 51.1 %collective-permute-start.1 = (bf16[256,512]{1,0:T(8,128)(2,1)S(1)}, bf16[256,512]{1,0:T(8,128)(2,1)}, u32[]{:S(2)}, u32[]{:S(2)}) collective-permute-start(bf16[256,512]{1,0:T(8,128)(2,1)S(1)} %bitcast_convert_fusion), channel_id=1, source_target_pairs={{0,2},{1,3},{2,0},{3,1},{4,6},{5,7},{6,4},{7,5},{8,10},{9,11},{10,... | collective-permute-start | bytes 786440 | tf_op jit(solution)/shard_map/ppermute | solution.py:82
  24.3 46.6 %collective-permute-start = (bf16[256,512]{1,0:T(8,128)(2,1)S(1)}, bf16[256,512]{1,0:T(8,128)(2,1)}, u32[]{:S(2)}, u32[]{:S(2)}) collective-permute-start(bf16[256,512]{1,0:T(8,128)(2,1)S(1)} %bitcast_convert_fusion), channel_id=1, source_target_pairs={{0,1},{1,2},{2,3},{3,0},{4,5},{5,6},{6,7},{7,4},{8,9},{9,10},{10,1... | collective-permute-start | bytes 786440 | tf_op jit(solution)/shard_map/ppermute | solution.py:82
  29.2 5.0 %collective-permute-start.3 = (f32[32,256]{1,0:T(8,128)}, f32[32,256]{1,0:T(8,128)}, u32[]{:S(2)}, u32[]{:S(2)}) collective-permute-start(f32[32,256]{1,0:T(8,128)} %get-tuple-element.17), channel_id=1, source_target_pairs={{0,32},{32,0},{1,33},{33,1},{2,34},{34,2},{3,35},{35,3},{4,36},{36... | collective-permute-start | bytes 98312 | tf_op jit(solution)/shard_map/ppermute | solution.py:82
  34.9 13.6 %collective-permute-start.4 = (f32[2,32,256]{2,1,0:T(8,128)S(1)}, f32[2,32,256]{2,1,0:T(8,128)S(1)}, u32[]{:S(2)}, u32[]{:S(2)}) collective-permute-start(f32[2,32,256]{2,1,0:T(8,128)S(1)} %bitcast_dynamic-update-slice_fusion.9), channel_id=1, source_target_pairs={{0,256},{256,0},{1,257},{257,1},{2,258},{258,2},{3,259},{259,3},{4... | collective-permute-start | bytes 196616 | tf_op jit(solution)/shard_map/ppermute | solution.py:82
  48.6 19.6 %collective-permute-start.7 = (f32[2,2,32,256]{3,2,1,0:T(8,128)S(1)}, f32[2,2,32,256]{3,2,1,0:T(8,128)S(1)}, u32[]{:S(2)}, u32[]{:S(2)}) collective-permute-start(f32[2,2,32,256]{3,2,1,0:T(8,128)S(1)} %bitcast_dynamic-update-slice_fusion.7), channel_id=1, source_target_pairs={{0,192},{64,0},{128,64},{192,128},{1,193},{65,1},{129,65},{193,129... | collective-permute-start | bytes 393224 | tf_op jit(solution)/shard_map/ppermute | solution.py:82
  53.0 7.4 %collective-permute-start.5 = (f32[2,2,32,256]{3,2,1,0:T(8,128)S(1)}, f32[2,2,32,256]{3,2,1,0:T(8,128)S(1)}, u32[]{:S(2)}, u32[]{:S(2)}) collective-permute-start(f32[2,2,32,256]{3,2,1,0:T(8,128)S(1)} %bitcast_dynamic-update-slice_fusion.7), channel_id=1, source_target_pairs={{0,64},{64,128},{128,192},{192,0},{1,65},{65,129},{129,193},{193,1... | collective-permute-start | bytes 393224 | tf_op jit(solution)/shard_map/ppermute | solution.py:82
  60.3 7.2 %collective-permute-start.6 = (f32[2,2,32,256]{3,2,1,0:T(8,128)S(1)}, f32[2,2,32,256]{3,2,1,0:T(8,128)S(1)}, u32[]{:S(2)}, u32[]{:S(2)}) collective-permute-start(f32[2,2,32,256]{3,2,1,0:T(8,128)S(1)} %bitcast_dynamic-update-slice_fusion.7), channel_id=1, source_target_pairs={{0,128},{64,192},{128,0},{192,64},{1,129},{65,193},{129,1},{193,65... | collective-permute-start | bytes 393224 | tf_op jit(solution)/shard_map/ppermute | solution.py:82
  75.7 31.4 %copy-start.2 = (bf16[1,128,512]{2,1,0:T(8,128)(2,1)S(1)}, bf16[1,128,512]{2,1,0:T(8,128)(2,1)}, u32[]{:S(2)}) copy-start(bf16[1,128,512]{2,1,0:T(8,128)(2,1)} %param.8) | copy-start | bytes 393220
  75.7 31.4 %copy-start.3 = (f32[128]{0:T(128)S(1)}, f32[128]{0:T(128)}, u32[]{:S(2)}) copy-start(f32[128]{0:T(128)} %param.9) | copy-start | bytes 1540
  138.3 43.6 %copy-start.5 = (f32[1,256,512]{2,1,0:T(8,128)S(1)}, f32[1,256,512]{2,1,0:T(8,128)}, u32[]{:S(2)}) copy-start(f32[1,256,512]{2,1,0:T(8,128)} %param.10) | copy-start | bytes 1572868
  158.9 23.1 %copy-start.6 = (f32[512,256]{0,1:T(8,128)S(1)}, f32[512,256]{0,1:T(8,128)}, u32[]{:S(2)}) copy-start(f32[512,256]{0,1:T(8,128)} %copy.35) | copy-start | bytes 1572868
  159.3 43.4 %copy-start.10 = (f32[256,32]{0,1:T(8,128)S(1)}, f32[256,32]{0,1:T(8,128)}, u32[]{:S(2)}) copy-start(f32[256,32]{0,1:T(8,128)} %param.11) | copy-start | bytes 98308

commit v3 on v2

--- a/solution.py
+++ b/solution.py
@@ -18,6 +18,23 @@
 
 REPLICA = ("y_lo", "x", "core")
 FSDP = ("z", "y_hi")
+ALL = REPLICA + FSDP
+
+EIGHT, FOUR = 8, 4
+
+
+def place(core, p, q):
+    return (p, q) if core == 0 else (2 * q + p // 4, p % 4)
+
+
+def device(y_lo, x, core, p, q):
+    z, y_hi = place(core, p, q)
+    return (((y_lo * 4 + x) * 2 + core) * 8 + z) * 4 + y_hi
+
+
+TEAMS = [(y_lo, x, core) for y_lo in range(2) for x in range(4) for core in range(2)]
+RINGS_OF_8 = [[device(*team, p, q) for p in range(EIGHT)] for team in TEAMS for q in range(FOUR)]
+RINGS_OF_4 = [[device(*team, p, q) for q in range(FOUR)] for team in TEAMS for p in range(EIGHT)]
 
 
 def slope_kernel(factor, parts_ref, cotangent_ref, gain_ref, out_ref):
@@ -47,29 +64,52 @@
     )(parts, cotangent, gain)
 
 
-def split_kernel(feats_ref, out_ref, sems):
-    pieces, _, width = out_ref.shape
-    copies = [
-        pltpu.make_async_copy(feats_ref.at[:, pl.ds(i * width, width)], out_ref.at[i], sems.at[i])
-        for i in range(pieces)
-    ]
+def split_kernel(core_ref, feats_ref, out_ref, sems):
+    core = core_ref[0]
+    width = feats_ref.shape[1] // (EIGHT * FOUR)
+    copies = []
+    for p in range(EIGHT):
+        for q in range(FOUR):
+            block = jnp.where(core == 0, FOUR * p + q, EIGHT * q + p)
+            copies.append(
+                pltpu.make_async_copy(
+                    feats_ref.at[:, pl.ds(pl.multiple_of(block * width, width), width)],
+                    out_ref.at[p, :, pl.ds(q * width, width)],
+                    sems.at[p, q],
+                )
+            )
     for copy in copies:
         copy.start()
     for copy in copies:
         copy.wait()
 
 
-def split_columns(feats, pieces):
+def split_columns(core, feats):
     tokens, width = feats.shape
     return pl.pallas_call(
         split_kernel,
-        out_shape=jax.ShapeDtypeStruct((pieces, tokens, width // pieces), feats.dtype),
-        in_specs=[pl.BlockSpec(memory_space=pl.ANY)],
-        out_specs=pl.BlockSpec(memory_space=pl.ANY),
-        scratch_shapes=[pltpu.SemaphoreType.DMA((pieces,))],
-        compiler_params=pltpu.CompilerParams(vmem_limit_bytes=16 * 1024 * 1024),
+        out_shape=jax.ShapeDtypeStruct((EIGHT, tokens, width // EIGHT), feats.dtype),
+        in_specs=[pl.BlockSpec(memory_space=pltpu.SMEM), pl.BlockSpec(memory_space=pltpu.HBM)],
+        out_specs=pl.BlockSpec(memory_space=pltpu.HBM),
+        scratch_shapes=[pltpu.SemaphoreType.DMA((EIGHT, FOUR))],
+        compiler_params=pltpu.CompilerParams(vmem_limit_bytes=60 * 1024 * 1024),
         cost_estimate=pl.CostEstimate(flops=0, bytes_accessed=4 * tokens * width, transcendentals=0),
-    )(feats)
+    )(core, feats)
+
+
+def gather_rows(x, q):
+    out = jnp.zeros((FOUR,) + x.shape, x.dtype)
+    for step in range(FOUR):
+        piece = x
+        if step:
+            pairs = [(ring[i], ring[(i + step) % FOUR]) for ring in RINGS_OF_4 for i in range(FOUR)]
+            piece = lax.ppermute(x, ALL, pairs)
+        out = lax.dynamic_update_index_in_dim(out, piece, lax.rem(q + FOUR - step, FOUR), 0)
+    return out
+
+
+def exchange(x, rings):
+    return lax.all_to_all(x, ALL, 0, 0, axis_index_groups=rings)
 
 
 def gather_by_permutes(x, axis):
@@ -162,35 +202,38 @@
     tokens, width = feats.shape
     rows, columns = own_rows.shape
     factor = width ** (-0.5)
-    z_size = lax.axis_size("z")
-    y_size = lax.axis_size("y_hi")
     replicas = lax.axis_size(REPLICA)
 
-    owned = lax.all_to_all(split_columns(feats, z_size), "z", 0, 0)
-    owned = owned.reshape(z_size * tokens, width // z_size)
-
-    weight = gather_by_permutes(own_rows.astype(jnp.bfloat16), "y_hi").reshape(-1, columns)
+    core = lax.axis_index("core")
+    q = jnp.where(core == 0, lax.axis_index("y_hi"), lax.axis_index("z") // 2)
+
+    owned = exchange(split_columns(core.reshape(1), feats), RINGS_OF_8)
+    owned = owned.reshape(EIGHT * tokens, width // EIGHT)
+    weight = gather_rows(own_rows.astype(jnp.bfloat16), q).reshape(-1, columns)
+    owned, weight = lax.optimization_barrier((owned, weight))
+    parts = project(owned, weight).reshape(EIGHT, tokens, columns)
+
     global_t, momentum_t, late_t = global_weight.T, outer_momentum.T, late_delta.T
     next_momentum_t = keep_rate * momentum_t + late_t
     next_global_t = global_t - outer_rate * (late_t + keep_rate * next_momentum_t)
-    new_rows_t = gather_by_permutes(next_global_t, "core")
-    new_rows_t = gather_by_permutes(new_rows_t, "y_lo")
+    parts, new_rows_t = lax.optimization_barrier((parts, next_global_t))
+    new_rows_t = gather_by_permutes(gather_by_permutes(new_rows_t, "core"), "y_lo")
+    parts = exchange(parts, RINGS_OF_8)
+    parts, new_rows_t = lax.optimization_barrier((parts, new_rows_t))
+    slopes = key_slopes(parts, key_cotangent[0], key_gain.reshape(1, HEAD), factor)
+    slopes, new_rows_t = lax.optimization_barrier((slopes, new_rows_t))
     new_rows_t = gather_by_permutes(new_rows_t, "x")
     new_rows = new_rows_t.transpose(1, 0, 2, 3, 4).reshape(columns, rows).T
-
-    owned, weight, new_rows = lax.optimization_barrier((owned, weight, new_rows))
-    parts = project(owned, weight).reshape(z_size, tokens, columns)
-    parts = lax.all_to_all(parts, "z", 0, 0)
-    slopes = key_slopes(parts, key_cotangent[0], key_gain.reshape(1, HEAD), factor)
-    slopes = lax.all_to_all(slopes, "z", 0, 0).reshape(z_size * tokens, columns)
-
-    scaled = gradient_parts(owned, slopes, y_size).astype(jnp.float16)
-    pieces = lax.all_to_all(scaled, "y_hi", 0, 0)
+    slopes = exchange(slopes, RINGS_OF_8).reshape(EIGHT * tokens, columns)
+    slopes, new_rows = lax.optimization_barrier((slopes, new_rows))
+
+    scaled = gradient_parts(owned, slopes, FOUR).astype(jnp.float16)
+    pieces = exchange(scaled, RINGS_OF_4)
     unscale = jnp.exp2(pieces[:, rows, 0].astype(jnp.float32)) * factor
     gradient = jnp.sum(pieces[:, :rows].astype(jnp.float32) * unscale[:, None, None], axis=0)
 
     squares = jnp.sum(gradient * gradient)
-    shares = lax.all_to_all(jnp.broadcast_to(squares, (z_size * y_size, 1, 128)), FSDP, 0, 0)
+    shares = lax.all_to_all(jnp.broadcast_to(squares, (EIGHT * FOUR, 1, 128)), FSDP, 0, 0)
     squares = jnp.sum(shares[:, 0, 0])
     grad_scale = jnp.sqrt(squares / (width * columns) + epsilon)
     after_step = own_rows - inner_rate * gradient / grad_scale

time: 204 us -> 247 us (1.21)
  Pallas kernels: 5.02 us -> 70.7 us
  blocking collectives: 119 us -> 65.1 us
  starting transfers between devices: 38.8 us -> 56.9 us
  waiting for transfers between devices: 19.8 us -> 36 us
  local copies, waits for them, and re-layouts: 13.2 us -> 10.6 us
    pallas_call x1, Pallas kernels: 0.23 us -> 64.9 us  [split_columns(): pl.pallas_call(split_kernel, out_shape=jax.ShapeDtypeStruct((EIGHT, token...]
    all_to_all x4 -> x2, blocking collectives: 99.7 us -> 44.8 us  [the longest x1 27.1 us: exchange(): return lax.all_to_all(x, ALL, 0, 0, axis_index_groups=rings)]
    ppermute x0 -> x3, waiting for transfers between devices: none -> 28.1 us  [gather_rows(): piece = lax.ppermute(x, ALL, pairs)]
    ppermute x0 -> x3, starting transfers between devices: none -> 17.1 us  [gather_rows(): piece = lax.ppermute(x, ALL, pairs)]
    ppermute x8 -> x5, waiting for transfers between devices: 19.8 us -> 7.87 us  [gather_by_permutes(): piece = lax.ppermute(x, axis, [(i, (i + step) % size) for i in range(size)])]
    all_to_all x1 -> x3, starting transfers between devices: 11 us -> 21.7 us  [exchange(): return lax.all_to_all(x, ALL, 0, 0, axis_index_groups=rings)]
    ppermute x8 -> x5, starting transfers between devices: 27.8 us -> 18 us  [gather_by_permutes(): piece = lax.ppermute(x, axis, [(i, (i + step) % size) for i in range(size)])]
    dynamic_update_slice x10 -> x8, local copies, waits for them, and re-layouts: 6.37 us -> 2.69 us  [gather_by_permutes(): lax.dynamic_update_index_in_dim(out, piece, lax.rem(me + size - step, siz...]
  transfers between devices with their start and end apart: 9 -> 11, of which waited for: 3 -> 5; matrix products, arithmetic and copies ran while one was open for 5% -> 4% of each run, Pallas kernels for 0% -> 0%
where the time goes in v3:
time: 247 us; the launch traced here: 246 us
  Pallas kernels  70.7 us (29%)
  blocking collectives  65.1 us (26%)
  starting transfers between devices  56.9 us (23%)
  waiting for transfers between devices  36 us (15%)
  local copies, waits for them, and re-layouts  10.6 us (4%)
  other arithmetic  4.88 us (2%)
    pallas_call x1, Pallas kernels, split_columns(): pl.pallas_call(split_kernel, out_shape=jax.ShapeDtypeStruct((EIGHT, token...  64.9 us
    ppermute x3, waiting for transfers between devices, gather_rows(): piece = lax.ppermute(x, ALL, pairs)  28.1 us
    all_to_all x1, blocking collectives, exchange(): return lax.all_to_all(x, ALL, 0, 0, axis_index_groups=rings)  27.1 us
    all_to_all x3, starting transfers between devices, exchange(): return lax.all_to_all(x, ALL, 0, 0, axis_index_groups=rings)  21.7 us
    all_to_all x1, blocking collectives, shards(): received = lax.all_to_all(sent_rows, REPLICA, 0, 0).astype(jnp.float32)  20.3 us
    ppermute x5, starting transfers between devices, gather_by_permutes(): piece = lax.ppermute(x, axis, [(i, (i + step) % size) for i in range(size)])  18 us
    all_to_all x1, blocking collectives, shards(): lax.all_to_all(jnp.broadcast_to(squares, (EIGHT * FOUR, 1, 128)), FSDP, 0...  17.8 us
    ppermute x3, starting transfers between devices, gather_rows(): piece = lax.ppermute(x, ALL, pairs)  17.1 us
  transfers between devices with their start and end apart: 11, of which 5 were waited for; matrix products, arithmetic and copies ran while one was open for 4% of the time, Pallas kernels for 0%

profile of v3, /device:TPU:1, one launch (start us, length us, event | category | flops | bytes accessed | tf_op | source)
XLA Modules:
  0.0 245.8 jit_solution(9784576206124395441)
XLA Ops:
  0.6 64.9 %shard_map.102 = bf16[8,128,1024]{2,1,0:T(8,128)(2,1)} custom-call(s32[1]{0:T(128)} %bitcast.core_ref, bf16[128,8192]{1,0:T(8,128)(2,1)} %bitcast.76), custom_call_target="tpu_custom_call" | custom-call | bytes 4194304 | tf_op jit(solution)/shard_map/pallas_call | solution.py:89
  65.6 9.6 %all-to-all-start = ((bf16[8,128,1024]{2,1,0:T(8,128)(2,1)}), bf16[8,128,1024]{2,1,0:T(8,128)(2,1)S(1)}, u32[]{:S(2)}, u32[]{:S(2)}) async-start(bf16[8,128,1024]{2,1,0:T(8,128)(2,1)} %shard_map.102), calls=%async_computation | async-start | bytes 4194304 | tf_op jit(solution)/shard_map/all_to_all | solution.py:112
  75.3 5.8 %collective-permute-start = (bf16[256,512]{1,0:T(8,128)(2,1)S(1)}, bf16[256,512]{1,0:T(8,128)(2,1)}, u32[]{:S(2)}, u32[]{:S(2)}) collective-permute-start(bf16[256,512]{1,0:T(8,128)(2,1)S(1)} %bitcast_convert_fusion), channel_id=1, source_target_pairs={{0,1},{1,2},{2,3},{3,0},{4,5},{5,6},{6,7},{7,4},{8,9},{9,10},{10,1... | collective-permute-start | bytes 786440 | tf_op jit(solution)/shard_map/ppermute | solution.py:106
  81.1 7.9 %collective-permute-start.1 = (bf16[256,512]{1,0:T(8,128)(2,1)S(1)}, bf16[256,512]{1,0:T(8,128)(2,1)}, u32[]{:S(2)}, u32[]{:S(2)}) collective-permute-start(bf16[256,512]{1,0:T(8,128)(2,1)S(1)} %bitcast_convert_fusion), channel_id=1, source_target_pairs={{0,2},{1,3},{2,0},{3,1},{4,6},{5,7},{6,4},{7,5},{8,10},{9,11},{10,... | collective-permute-start | bytes 786440 | tf_op jit(solution)/shard_map/ppermute | solution.py:106
  89.0 3.4 %collective-permute-start.2 = (bf16[256,512]{1,0:T(8,128)(2,1)S(1)}, bf16[256,512]{1,0:T(8,128)(2,1)}, u32[]{:S(2)}, u32[]{:S(2)}) collective-permute-start(bf16[256,512]{1,0:T(8,128)(2,1)S(1)} %bitcast_convert_fusion), channel_id=1, source_target_pairs={{0,3},{1,0},{2,1},{3,2},{4,7},{5,4},{6,5},{7,6},{8,11},{9,8},{10,9... | collective-permute-start | bytes 786440 | tf_op jit(solution)/shard_map/ppermute | solution.py:106
  92.5 1.1 convert_dynamic-update-slice_fusion
  93.7 18.2 %collective-permute-done = bf16[256,512]{1,0:T(8,128)(2,1)} collective-permute-done((bf16[256,512]{1,0:T(8,128)(2,1)S(1)}, bf16[256,512]{1,0:T(8,128)(2,1)}, u32[]{:S(2)}, u32[]{:S(2)}) %collective-permute-start) | collective-permute-done | bytes 262176 | tf_op jit(solution)/shard_map/ppermute | solution.py:106
  112.9 9.9 %collective-permute-done.1 = bf16[256,512]{1,0:T(8,128)(2,1)} collective-permute-done((bf16[256,512]{1,0:T(8,128)(2,1)S(1)}, bf16[256,512]{1,0:T(8,128)(2,1)}, u32[]{:S(2)}, u32[]{:S(2)}) %collective-permute-start.1) | collective-permute-done | bytes 262176 | tf_op jit(solution)/shard_map/ppermute | solution.py:106
  124.7 1.8 shard_map.103
  127.5 5.5 %all-to-all-start.1 = ((bf16[8,128,512]{2,1,0:T(8,128)(2,1)}), bf16[8,128,512]{2,1,0:T(8,128)(2,1)S(1)}, u32[]{:S(2)}, u32[]{:S(2)}) async-start(bf16[8,128,512]{2,1,0:T(8,128)(2,1)} %bitcast.71), calls=%async_computation.1 | async-start | bytes 2097152 | tf_op jit(solution)/shard_map/all_to_all | solution.py:112
  133.0 5.1 %collective-permute-start.3 = (f32[32,256]{1,0:T(8,128)S(1)}, f32[32,256]{1,0:T(8,128)S(1)}, u32[]{:S(2)}, u32[]{:S(2)}) collective-permute-start(f32[32,256]{1,0:T(8,128)S(1)} %fusion.3), channel_id=1, source_target_pairs={{0,32},{32,0},{1,33},{33,1},{2,34},{34,2},{3,35},{35,3},{4,36},{36... | collective-permute-start | bytes 98312 | tf_op jit(solution)/shard_map/ppermute | solution.py:122
  139.0 2.3 collective-permute-start.4
  141.4 7.0 %collective-permute-done.4 = f32[2,32,256]{2,1,0:T(8,128)S(1)} collective-permute-done((f32[2,32,256]{2,1,0:T(8,128)S(1)}, f32[2,32,256]{2,1,0:T(8,128)S(1)}, u32[]{:S(2)}, u32[]{:S(2)}) %collective-permute-start.4) | collective-permute-done | bytes 65568 | tf_op jit(solution)/shard_map/ppermute | solution.py:122
  148.4 1.4 shard_map.104
  149.9 6.6 %all-to-all-start.2 = ((bf16[8,128,512]{2,1,0:T(8,128)(2,1)}), bf16[8,128,512]{2,1,0:T(8,128)(2,1)S(1)}, u32[]{:S(2)}, u32[]{:S(2)}) async-start(bf16[8,128,512]{2,1,0:T(8,128)(2,1)} %shard_map.104), calls=%async_computation.2 | async-start | bytes 2097152 | tf_op jit(solution)/shard_map/all_to_all | solution.py:112
  156.4 3.1 %collective-permute-start.5 = (f32[2,2,32,256]{3,2,1,0:T(8,128)S(1)}, f32[2,2,32,256]{3,2,1,0:T(8,128)S(1)}, u32[]{:S(2)}, u32[]{:S(2)}) collective-permute-start(f32[2,2,32,256]{3,2,1,0:T(8,128)S(1)} %bitcast_dynamic-update-slice_fusion.7), channel_id=1, source_target_pairs={{0,64},{64,128},{128,192},{192,0},{1,65},{65,129},{129,193},{193,1... | collective-permute-start | bytes 393224 | tf_op jit(solution)/shard_map/ppermute | solution.py:122
  159.5 4.4 %collective-permute-start.6 = (f32[2,2,32,256]{3,2,1,0:T(8,128)S(1)}, f32[2,2,32,256]{3,2,1,0:T(8,128)S(1)}, u32[]{:S(2)}, u32[]{:S(2)}) collective-permute-start(f32[2,2,32,256]{3,2,1,0:T(8,128)S(1)} %bitcast_dynamic-update-slice_fusion.7), channel_id=1, source_target_pairs={{0,128},{64,192},{128,0},{192,64},{1,129},{65,193},{129,1},{193,65... | collective-permute-start | bytes 393224 | tf_op jit(solution)/shard_map/ppermute | solution.py:122
  163.9 3.1 %collective-permute-start.7 = (f32[2,2,32,256]{3,2,1,0:T(8,128)S(1)}, f32[2,2,32,256]{3,2,1,0:T(8,128)S(1)}, u32[]{:S(2)}, u32[]{:S(2)}) collective-permute-start(f32[2,2,32,256]{3,2,1,0:T(8,128)S(1)} %bitcast_dynamic-update-slice_fusion.7), channel_id=1, source_target_pairs={{0,192},{64,0},{128,64},{192,128},{1,193},{65,1},{129,65},{193,129... | collective-permute-start | bytes 393224 | tf_op jit(solution)/shard_map/ppermute | solution.py:122
  170.6 2.1 copy.35
  172.7 2.6 %shard_map.105 = f32[4,272,512]{2,1,0:T(8,128)S(1)} custom-call(bf16[1024,1024]{1,0:T(8,128)(2,1)S(1)} %bitcast.69, bf16[1024,512]{1,0:T(8,128)(2,1)S(1)} %bitcast.70), custom_call_target="tpu_custom_call" | custom-call | flops 1073741824 | bytes 5242880 | tf_op jit(solution)/shard_map/pallas_call | solution.py:178
  175.5 27.1 %all_to_all.30 = f16[4,272,512]{2,1,0:T(8,128)(2,1)S(1)} all-to-all(f16[4,272,512]{2,1,0:T(8,128)(2,1)S(1)} %convert_element_type.30), channel_id=1, replica_groups={{0,1,2,3},{4,5,6,7},{8,9,10,11},{12,13,14,15},{16,17,18,19},{20,21,22,2..., dimensions={0} | all-to-all | bytes 2228224 | tf_op jit(solution)/shard_map/all_to_all | solution.py:112
  204.5 17.8 %all_to_all.31 = f32[32,1,128]{2,1,0:T(1,128)S(1)} all-to-all(f32[32,1,128]{2,1,0:T(1,128)S(1)} %broadcast_in_dim.72), channel_id=1, replica_groups=mesh['y_lo'=2,'x'=4,'core'=2,'z'=8,'y_hi'=4] {'z','y_hi'}, dimensions={0} | all-to-all | bytes 32768 | tf_op jit(solution)/shard_map/all_to_all | solution.py:236
  223.6 1.0 convert_bitcast_fusion
  224.8 20.3 %all_to_all.32 = f16[16,32,256]{2,1,0:T(8,128)(2,1)S(1)} all-to-all(f16[16,32,256]{2,1,0:T(8,128)(2,1)S(1)} %bitcast.77), channel_id=1, replica_groups=mesh['y_lo'=2,'x'=4,'core'=2,'z'=8,'y_hi'=4] {'y_lo','x','core'}, dimensions={0} | all-to-all | bytes 524288 | tf_op jit(solution)/shard_map/all_to_all | solution.py:242
  (52 shorter events, 12.2 us)
Async XLA Ops:
  65.6 9.6 %copy-start.3 = (f32[1,256,512]{2,1,0:T(8,128)S(1)}, f32[1,256,512]{2,1,0:T(8,128)}, u32[]{:S(2)}) copy-start(f32[1,256,512]{2,1,0:T(8,128)} %param.10) | copy-start | bytes 1572868
  65.6 59.1 %all-to-all-start = ((bf16[8,128,1024]{2,1,0:T(8,128)(2,1)}), bf16[8,128,1024]{2,1,0:T(8,128)(2,1)S(1)}, u32[]{:S(2)}, u32[]{:S(2)}) async-start(bf16[8,128,1024]{2,1,0:T(8,128)(2,1)} %shard_map.102), calls=%async_computation | async-start | bytes 4194304 | tf_op jit(solution)/shard_map/all_to_all | solution.py:112
  75.2 18.4 %copy-start.6 = (f32[256,32]{0,1:T(8,128)S(1)}, f32[256,32]{0,1:T(8,128)}, u32[]{:S(2)}) copy-start(f32[256,32]{0,1:T(8,128)} %param.13) | copy-start | bytes 98308
  75.2 18.4 %copy-start.7 = (f32[256,32]{0,1:T(8,128)S(1)}, f32[256,32]{0,1:T(8,128)}, u32[]{:S(2)}) copy-start(f32[256,32]{0,1:T(8,128)} %param.11) | copy-start | bytes 98308
  75.2 18.4 %copy-start.8 = (f32[256,32]{0,1:T(8,128)S(1)}, f32[256,32]{0,1:T(8,128)}, u32[]{:S(2)}) copy-start(f32[256,32]{0,1:T(8,128)} %param.12) | copy-start | bytes 98308
  75.3 36.7 %collective-permute-start = (bf16[256,512]{1,0:T(8,128)(2,1)S(1)}, bf16[256,512]{1,0:T(8,128)(2,1)}, u32[]{:S(2)}, u32[]{:S(2)}) collective-permute-start(bf16[256,512]{1,0:T(8,128)(2,1)S(1)} %bitcast_convert_fusion), channel_id=1, source_target_pairs={{0,1},{1,2},{2,3},{3,0},{4,5},{5,6},{6,7},{7,4},{8,9},{9,10},{10,1... | collective-permute-start | bytes 786440 | tf_op jit(solution)/shard_map/ppermute | solution.py:106
  81.1 41.7 %collective-permute-start.1 = (bf16[256,512]{1,0:T(8,128)(2,1)S(1)}, bf16[256,512]{1,0:T(8,128)(2,1)}, u32[]{:S(2)}, u32[]{:S(2)}) collective-permute-start(bf16[256,512]{1,0:T(8,128)(2,1)S(1)} %bitcast_convert_fusion), channel_id=1, source_target_pairs={{0,2},{1,3},{2,0},{3,1},{4,6},{5,7},{6,4},{7,5},{8,10},{9,11},{10,... | collective-permute-start | bytes 786440 | tf_op jit(solution)/shard_map/ppermute | solution.py:106
  89.0 34.7 %collective-permute-start.2 = (bf16[256,512]{1,0:T(8,128)(2,1)S(1)}, bf16[256,512]{1,0:T(8,128)(2,1)}, u32[]{:S(2)}, u32[]{:S(2)}) collective-permute-start(bf16[256,512]{1,0:T(8,128)(2,1)S(1)} %bitcast_convert_fusion), channel_id=1, source_target_pairs={{0,3},{1,0},{2,1},{3,2},{4,7},{5,4},{6,5},{7,6},{8,11},{9,8},{10,9... | collective-permute-start | bytes 786440 | tf_op jit(solution)/shard_map/ppermute | solution.py:106
  126.5 1.0 copy-start
  127.5 20.9 %copy-start.1 = (bf16[1,128,512]{2,1,0:T(8,128)(2,1)S(1)}, bf16[1,128,512]{2,1,0:T(8,128)(2,1)}, u32[]{:S(2)}) copy-start(bf16[1,128,512]{2,1,0:T(8,128)(2,1)} %param.8) | copy-start | bytes 393220
  127.5 20.9 %copy-start.2 = (f32[128]{0:T(128)S(1)}, f32[128]{0:T(128)}, u32[]{:S(2)}) copy-start(f32[128]{0:T(128)} %param.9) | copy-start | bytes 1540
  127.5 20.9 %all-to-all-start.1 = ((bf16[8,128,512]{2,1,0:T(8,128)(2,1)}), bf16[8,128,512]{2,1,0:T(8,128)(2,1)S(1)}, u32[]{:S(2)}, u32[]{:S(2)}) async-start(bf16[8,128,512]{2,1,0:T(8,128)(2,1)} %bitcast.71), calls=%async_computation.1 | async-start | bytes 2097152 | tf_op jit(solution)/shard_map/all_to_all | solution.py:112
  133.0 6.0 %collective-permute-start.3 = (f32[32,256]{1,0:T(8,128)S(1)}, f32[32,256]{1,0:T(8,128)S(1)}, u32[]{:S(2)}, u32[]{:S(2)}) collective-permute-start(f32[32,256]{1,0:T(8,128)S(1)} %fusion.3), channel_id=1, source_target_pairs={{0,32},{32,0},{1,33},{33,1},{2,34},{34,2},{3,35},{35,3},{4,36},{36... | collective-permute-start | bytes 98312 | tf_op jit(solution)/shard_map/ppermute | solution.py:122
  139.0 9.4 %collective-permute-start.4 = (f32[2,32,256]{2,1,0:T(8,128)S(1)}, f32[2,32,256]{2,1,0:T(8,128)S(1)}, u32[]{:S(2)}, u32[]{:S(2)}) collective-permute-start(f32[2,32,256]{2,1,0:T(8,128)S(1)} %bitcast_dynamic-update-slice_fusion.9), channel_id=1, source_target_pairs={{0,256},{256,0},{1,257},{257,1},{2,258},{258,2},{3,259},{259,3},{4... | collective-permute-start | bytes 196616 | tf_op jit(solution)/shard_map/ppermute | solution.py:122
  149.9 22.8 %all-to-all-start.2 = ((bf16[8,128,512]{2,1,0:T(8,128)(2,1)}), bf16[8,128,512]{2,1,0:T(8,128)(2,1)S(1)}, u32[]{:S(2)}, u32[]{:S(2)}) async-start(bf16[8,128,512]{2,1,0:T(8,128)(2,1)} %shard_map.104), calls=%async_computation.2 | async-start | bytes 2097152 | tf_op jit(solution)/shard_map/all_to_all | solution.py:112
  156.4 12.1 %collective-permute-start.5 = (f32[2,2,32,256]{3,2,1,0:T(8,128)S(1)}, f32[2,2,32,256]{3,2,1,0:T(8,128)S(1)}, u32[]{:S(2)}, u32[]{:S(2)}) collective-permute-start(f32[2,2,32,256]{3,2,1,0:T(8,128)S(1)} %bitcast_dynamic-update-slice_fusion.7), channel_id=1, source_target_pairs={{0,64},{64,128},{128,192},{192,0},{1,65},{65,129},{129,193},{193,1... | collective-permute-start | bytes 393224 | tf_op jit(solution)/shard_map/ppermute | solution.py:122
  159.5 9.6 %collective-permute-start.6 = (f32[2,2,32,256]{3,2,1,0:T(8,128)S(1)}, f32[2,2,32,256]{3,2,1,0:T(8,128)S(1)}, u32[]{:S(2)}, u32[]{:S(2)}) collective-permute-start(f32[2,2,32,256]{3,2,1,0:T(8,128)S(1)} %bitcast_dynamic-update-slice_fusion.7), channel_id=1, source_target_pairs={{0,128},{64,192},{128,0},{192,64},{1,129},{65,193},{129,1},{193,65... | collective-permute-start | bytes 393224 | tf_op jit(solution)/shard_map/ppermute | solution.py:122
  163.9 6.0 %collective-permute-start.7 = (f32[2,2,32,256]{3,2,1,0:T(8,128)S(1)}, f32[2,2,32,256]{3,2,1,0:T(8,128)S(1)}, u32[]{:S(2)}, u32[]{:S(2)}) collective-permute-start(f32[2,2,32,256]{3,2,1,0:T(8,128)S(1)} %bitcast_dynamic-update-slice_fusion.7), channel_id=1, source_target_pairs={{0,192},{64,0},{128,64},{192,128},{1,193},{65,1},{129,65},{193,129... | collective-permute-start | bytes 393224 | tf_op jit(solution)/shard_map/ppermute | solution.py:122
  175.5 48.1 %copy-start.4 = (f32[1,256,512]{2,1,0:T(8,128)S(1)}, f32[1,256,512]{2,1,0:T(8,128)}, u32[]{:S(2)}) copy-start(f32[1,256,512]{2,1,0:T(8,128)} %param.10) | copy-start | bytes 1572868
  175.5 48.1 %copy-start.5 = (f32[512,256]{0,1:T(8,128)S(1)}, f32[512,256]{0,1:T(8,128)}, u32[]{:S(2)}) copy-start(f32[512,256]{0,1:T(8,128)} %copy.35) | copy-start | bytes 1572868

commit v4 on v3

--- a/solution.py
+++ b/solution.py
@@ -64,34 +64,44 @@
     )(parts, cotangent, gain)
 
 
-def split_kernel(core_ref, feats_ref, out_ref, sems):
+def split_kernel(core_ref, feats_ref, out_ref, held, sems, out_sems):
     core = core_ref[0]
     width = feats_ref.shape[1] // (EIGHT * FOUR)
-    copies = []
+    loads, stores = [], []
     for p in range(EIGHT):
         for q in range(FOUR):
             block = jnp.where(core == 0, FOUR * p + q, EIGHT * q + p)
-            copies.append(
+            loads.append(
                 pltpu.make_async_copy(
                     feats_ref.at[:, pl.ds(pl.multiple_of(block * width, width), width)],
-                    out_ref.at[p, :, pl.ds(q * width, width)],
+                    held.at[p, :, pl.ds(q * width, width)],
                     sems.at[p, q],
                 )
             )
-    for copy in copies:
-        copy.start()
-    for copy in copies:
-        copy.wait()
+        stores.append(pltpu.make_async_copy(held.at[p], out_ref.at[p], out_sems.at[p]))
+    for load in loads:
+        load.start()
+    for p in range(EIGHT):
+        for load in loads[FOUR * p : FOUR * (p + 1)]:
+            load.wait()
+        stores[p].start()
+    for store in stores:
+        store.wait()
 
 
 def split_columns(core, feats):
     tokens, width = feats.shape
+    shape = (EIGHT, tokens, width // EIGHT)
     return pl.pallas_call(
         split_kernel,
-        out_shape=jax.ShapeDtypeStruct((EIGHT, tokens, width // EIGHT), feats.dtype),
+        out_shape=jax.ShapeDtypeStruct(shape, feats.dtype),
         in_specs=[pl.BlockSpec(memory_space=pltpu.SMEM), pl.BlockSpec(memory_space=pltpu.HBM)],
         out_specs=pl.BlockSpec(memory_space=pltpu.HBM),
-        scratch_shapes=[pltpu.SemaphoreType.DMA((EIGHT, FOUR))],
+        scratch_shapes=[
+            pltpu.VMEM(shape, feats.dtype),
+            pltpu.SemaphoreType.DMA((EIGHT, FOUR)),
+            pltpu.SemaphoreType.DMA((EIGHT,)),
+        ],
         compiler_params=pltpu.CompilerParams(vmem_limit_bytes=60 * 1024 * 1024),
         cost_estimate=pl.CostEstimate(flops=0, bytes_accessed=4 * tokens * width, transcendentals=0),
     )(core, feats)
@@ -143,7 +153,7 @@
             pl.BlockSpec((depth, columns), lambda i: (0, 0)),
         ],
         out_specs=pl.BlockSpec((block, columns), lambda i: (i, 0)),
-        compiler_params=pltpu.CompilerParams(vmem_limit_bytes=24 * 1024 * 1024),
+        compiler_params=pltpu.CompilerParams(vmem_limit_bytes=60 * 1024 * 1024),
         cost_estimate=pl.CostEstimate(
             flops=2 * rows * depth * columns,
             bytes_accessed=2 * (rows * depth + depth * columns + rows * columns),

time: 247 us -> 188 us (0.76)
  Pallas kernels: 70.7 us -> 11.4 us
    pallas_call x1, Pallas kernels: 64.9 us -> 2.7 us  [split_columns(): pl.pallas_call(split_kernel, out_shape=jax.ShapeDtypeStruct(shape, feats....]
    pallas_call x1, Pallas kernels: 1.77 us -> 4.74 us  [project(): pl.pallas_call(project_kernel, grid=(rows // block,), out_shape=jax.Shape...]
  transfers between devices with their start and end apart: 11 -> 11, of which waited for: 5 -> 5; matrix products, arithmetic and copies ran while one was open for 4% -> 5% of each run, Pallas kernels for 0% -> 0%
where the time goes in v4:
time: 188 us; the launch traced here: 187 us
  blocking collectives  65.6 us (35%)
  starting transfers between devices  57.6 us (31%)
  waiting for transfers between devices  34.6 us (18%)
  local copies, waits for them, and re-layouts  12.1 us (6%)
  Pallas kernels  11.4 us (6%)
  other arithmetic  3.84 us (2%)
    ppermute x3, waiting for transfers between devices, gather_rows(): piece = lax.ppermute(x, ALL, pairs)  27.3 us
    all_to_all x1, blocking collectives, exchange(): return lax.all_to_all(x, ALL, 0, 0, axis_index_groups=rings)  27.1 us
    all_to_all x3, starting transfers between devices, exchange(): return lax.all_to_all(x, ALL, 0, 0, axis_index_groups=rings)  21.8 us
    all_to_all x1, blocking collectives, shards(): received = lax.all_to_all(sent_rows, REPLICA, 0, 0).astype(jnp.float32)  20.5 us
    ppermute x5, starting transfers between devices, gather_by_permutes(): piece = lax.ppermute(x, axis, [(i, (i + step) % size) for i in range(size)])  18.7 us
    all_to_all x1, blocking collectives, shards(): lax.all_to_all(jnp.broadcast_to(squares, (EIGHT * FOUR, 1, 128)), FSDP, 0...  18 us
    ppermute x3, starting transfers between devices, gather_rows(): piece = lax.ppermute(x, ALL, pairs)  17.1 us
    ppermute x5, waiting for transfers between devices, gather_by_permutes(): piece = lax.ppermute(x, axis, [(i, (i + step) % size) for i in range(size)])  7.23 us
  transfers between devices with their start and end apart: 11, of which 5 were waited for; matrix products, arithmetic and copies ran while one was open for 5% of the time, Pallas kernels for 0%

profile of v4, /device:TPU:1, one launch (start us, length us, event | category | flops | bytes accessed | tf_op | source)
XLA Modules:
  0.0 186.9 jit_solution(3768592929873147199)
XLA Ops:
  0.6 2.7 %shard_map.102 = bf16[8,128,1024]{2,1,0:T(8,128)(2,1)} custom-call(s32[1]{0:T(128)} %bitcast.core_ref, bf16[128,8192]{1,0:T(8,128)(2,1)} %bitcast.76), custom_call_target="tpu_custom_call" | custom-call | bytes 4194304 | tf_op jit(solution)/shard_map/pallas_call | solution.py:95
  3.4 9.6 %all-to-all-start = ((bf16[8,128,1024]{2,1,0:T(8,128)(2,1)}), bf16[8,128,1024]{2,1,0:T(8,128)(2,1)S(1)}, u32[]{:S(2)}, u32[]{:S(2)}) async-start(bf16[8,128,1024]{2,1,0:T(8,128)(2,1)} %shard_map.102), calls=%async_computation | async-start | bytes 4194304 | tf_op jit(solution)/shard_map/all_to_all | solution.py:122
  13.0 5.8 %collective-permute-start = (bf16[256,512]{1,0:T(8,128)(2,1)S(1)}, bf16[256,512]{1,0:T(8,128)(2,1)}, u32[]{:S(2)}, u32[]{:S(2)}) collective-permute-start(bf16[256,512]{1,0:T(8,128)(2,1)S(1)} %bitcast_convert_fusion), channel_id=1, source_target_pairs={{0,1},{1,2},{2,3},{3,0},{4,5},{5,6},{6,7},{7,4},{8,9},{9,10},{10,1... | collective-permute-start | bytes 786440 | tf_op jit(solution)/shard_map/ppermute | solution.py:116
  18.9 7.9 %collective-permute-start.1 = (bf16[256,512]{1,0:T(8,128)(2,1)S(1)}, bf16[256,512]{1,0:T(8,128)(2,1)S(1)}, u32[]{:S(2)}, u32[]{:S(2)}) collective-permute-start(bf16[256,512]{1,0:T(8,128)(2,1)S(1)} %bitcast_convert_fusion), channel_id=1, source_target_pairs={{0,2},{1,3},{2,0},{3,1},{4,6},{5,7},{6,4},{7,5},{8,10},{9,11},{10,... | collective-permute-start | bytes 786440 | tf_op jit(solution)/shard_map/ppermute | solution.py:116
  26.8 3.4 %collective-permute-start.2 = (bf16[256,512]{1,0:T(8,128)(2,1)S(1)}, bf16[256,512]{1,0:T(8,128)(2,1)S(1)}, u32[]{:S(2)}, u32[]{:S(2)}) collective-permute-start(bf16[256,512]{1,0:T(8,128)(2,1)S(1)} %bitcast_convert_fusion), channel_id=1, source_target_pairs={{0,3},{1,0},{2,1},{3,2},{4,7},{5,4},{6,5},{7,6},{8,11},{9,8},{10,9... | collective-permute-start | bytes 786440 | tf_op jit(solution)/shard_map/ppermute | solution.py:116
  31.4 18.2 %collective-permute-done = bf16[256,512]{1,0:T(8,128)(2,1)} collective-permute-done((bf16[256,512]{1,0:T(8,128)(2,1)S(1)}, bf16[256,512]{1,0:T(8,128)(2,1)}, u32[]{:S(2)}, u32[]{:S(2)}) %collective-permute-start) | collective-permute-done | bytes 262176 | tf_op jit(solution)/shard_map/ppermute | solution.py:116
  49.6 1.7 bitcast_dynamic-update-slice_fusion.2
  51.3 9.1 %collective-permute-done.1 = bf16[256,512]{1,0:T(8,128)(2,1)S(1)} collective-permute-done((bf16[256,512]{1,0:T(8,128)(2,1)S(1)}, bf16[256,512]{1,0:T(8,128)(2,1)S(1)}, u32[]{:S(2)}, u32[]{:S(2)}) %collective-permute-start.1) | collective-permute-done | bytes 262176 | tf_op jit(solution)/shard_map/ppermute | solution.py:116
  61.9 1.3 copy-done
  63.2 4.7 %shard_map.103 = bf16[1024,512]{1,0:T(8,128)(2,1)} custom-call(bf16[1024,1024]{1,0:T(8,128)(2,1)} %bitcast.68, bf16[1024,512]{1,0:T(8,128)(2,1)} %bitcast.74), custom_call_target="tpu_custom_call" | custom-call | flops 1073741824 | bytes 4194304 | tf_op jit(solution)/shard_map/pallas_call | solution.py:147
  68.0 5.5 %all-to-all-start.1 = ((bf16[8,128,512]{2,1,0:T(8,128)(2,1)}), bf16[8,128,512]{2,1,0:T(8,128)(2,1)S(1)}, u32[]{:S(2)}, u32[]{:S(2)}) async-start(bf16[8,128,512]{2,1,0:T(8,128)(2,1)} %bitcast.73), calls=%async_computation.1 | async-start | bytes 2097152 | tf_op jit(solution)/shard_map/all_to_all | solution.py:122
  73.5 5.8 %collective-permute-start.3 = (f32[32,256]{1,0:T(8,128)S(1)}, f32[32,256]{1,0:T(8,128)S(1)}, u32[]{:S(2)}, u32[]{:S(2)}) collective-permute-start(f32[32,256]{1,0:T(8,128)S(1)} %fusion.3), channel_id=1, source_target_pairs={{0,32},{32,0},{1,33},{33,1},{2,34},{34,2},{3,35},{35,3},{4,36},{36... | collective-permute-start | bytes 98312 | tf_op jit(solution)/shard_map/ppermute | solution.py:132
  80.1 2.3 %collective-permute-start.4 = (f32[2,32,256]{2,1,0:T(8,128)S(1)}, f32[2,32,256]{2,1,0:T(8,128)S(1)}, u32[]{:S(2)}, u32[]{:S(2)}) collective-permute-start(f32[2,32,256]{2,1,0:T(8,128)S(1)} %bitcast_dynamic-update-slice_fusion.9), channel_id=1, source_target_pairs={{0,256},{256,0},{1,257},{257,1},{2,258},{258,2},{3,259},{259,3},{4... | collective-permute-start | bytes 196616 | tf_op jit(solution)/shard_map/ppermute | solution.py:132
  82.5 6.3 %collective-permute-done.4 = f32[2,32,256]{2,1,0:T(8,128)S(1)} collective-permute-done((f32[2,32,256]{2,1,0:T(8,128)S(1)}, f32[2,32,256]{2,1,0:T(8,128)S(1)}, u32[]{:S(2)}, u32[]{:S(2)}) %collective-permute-start.4) | collective-permute-done | bytes 65568 | tf_op jit(solution)/shard_map/ppermute | solution.py:132
  88.9 1.4 shard_map.104
  90.3 6.7 %all-to-all-start.2 = ((bf16[8,128,512]{2,1,0:T(8,128)(2,1)}), bf16[8,128,512]{2,1,0:T(8,128)(2,1)S(1)}, u32[]{:S(2)}, u32[]{:S(2)}) async-start(bf16[8,128,512]{2,1,0:T(8,128)(2,1)} %shard_map.104), calls=%async_computation.2 | async-start | bytes 2097152 | tf_op jit(solution)/shard_map/all_to_all | solution.py:122
  97.0 3.1 %collective-permute-start.5 = (f32[2,2,32,256]{3,2,1,0:T(8,128)S(1)}, f32[2,2,32,256]{3,2,1,0:T(8,128)S(1)}, u32[]{:S(2)}, u32[]{:S(2)}) collective-permute-start(f32[2,2,32,256]{3,2,1,0:T(8,128)S(1)} %bitcast_dynamic-update-slice_fusion.7), channel_id=1, source_target_pairs={{0,64},{64,128},{128,192},{192,0},{1,65},{65,129},{129,193},{193,1... | collective-permute-start | bytes 393224 | tf_op jit(solution)/shard_map/ppermute | solution.py:132
  100.2 4.4 %collective-permute-start.6 = (f32[2,2,32,256]{3,2,1,0:T(8,128)S(1)}, f32[2,2,32,256]{3,2,1,0:T(8,128)S(1)}, u32[]{:S(2)}, u32[]{:S(2)}) collective-permute-start(f32[2,2,32,256]{3,2,1,0:T(8,128)S(1)} %bitcast_dynamic-update-slice_fusion.7), channel_id=1, source_target_pairs={{0,128},{64,192},{128,0},{192,64},{1,129},{65,193},{129,1},{193,65... | collective-permute-start | bytes 393224 | tf_op jit(solution)/shard_map/ppermute | solution.py:132
  104.5 3.1 %collective-permute-start.7 = (f32[2,2,32,256]{3,2,1,0:T(8,128)S(1)}, f32[2,2,32,256]{3,2,1,0:T(8,128)S(1)}, u32[]{:S(2)}, u32[]{:S(2)}) collective-permute-start(f32[2,2,32,256]{3,2,1,0:T(8,128)S(1)} %bitcast_dynamic-update-slice_fusion.7), channel_id=1, source_target_pairs={{0,192},{64,0},{128,64},{192,128},{1,193},{65,1},{129,65},{193,129... | collective-permute-start | bytes 393224 | tf_op jit(solution)/shard_map/ppermute | solution.py:132
  111.2 2.1 %copy.35 = f32[512,256]{0,1:T(8,128)} copy(f32[512,256]{1,0:T(8,128)} %bitcast.27) | data formatting | bytes 1048576 | tf_op jit(solution)/shard_map/reshape | solution.py:236
  113.3 2.6 %shard_map.105 = f32[4,272,512]{2,1,0:T(8,128)S(1)} custom-call(bf16[1024,1024]{1,0:T(8,128)(2,1)S(1)} %bitcast.69, bf16[1024,512]{1,0:T(8,128)(2,1)S(1)} %bitcast.70), custom_call_target="tpu_custom_call" | custom-call | flops 1073741824 | bytes 5242880 | tf_op jit(solution)/shard_map/pallas_call | solution.py:188
  116.1 27.1 %all_to_all.30 = f16[4,272,512]{2,1,0:T(8,128)(2,1)S(1)} all-to-all(f16[4,272,512]{2,1,0:T(8,128)(2,1)S(1)} %convert_element_type.30), channel_id=1, replica_groups={{0,1,2,3},{4,5,6,7},{8,9,10,11},{12,13,14,15},{16,17,18,19},{20,21,22,2..., dimensions={0} | all-to-all | bytes 2228224 | tf_op jit(solution)/shard_map/all_to_all | solution.py:122
  145.1 18.0 %all_to_all.31 = f32[32,1,128]{2,1,0:T(1,128)S(1)} all-to-all(f32[32,1,128]{2,1,0:T(1,128)S(1)} %broadcast_in_dim.72), channel_id=1, replica_groups=mesh['y_lo'=2,'x'=4,'core'=2,'z'=8,'y_hi'=4] {'z','y_hi'}, dimensions={0} | all-to-all | bytes 32768 | tf_op jit(solution)/shard_map/all_to_all | solution.py:246
  165.7 20.5 %all_to_all.32 = f16[16,32,256]{2,1,0:T(8,128)(2,1)S(1)} all-to-all(f16[16,32,256]{2,1,0:T(8,128)(2,1)S(1)} %bitcast.77), channel_id=1, replica_groups=mesh['y_lo'=2,'x'=4,'core'=2,'z'=8,'y_hi'=4] {'y_lo','x','core'}, dimensions={0} | all-to-all | bytes 524288 | tf_op jit(solution)/shard_map/all_to_all | solution.py:252
  (56 shorter events, 11.8 us)
Async XLA Ops:
  3.3 9.6 %copy-start.4 = (f32[1,256,512]{2,1,0:T(8,128)S(1)}, f32[1,256,512]{2,1,0:T(8,128)}, u32[]{:S(2)}) copy-start(f32[1,256,512]{2,1,0:T(8,128)} %param.10) | copy-start | bytes 1572868
  3.4 58.5 %all-to-all-start = ((bf16[8,128,1024]{2,1,0:T(8,128)(2,1)}), bf16[8,128,1024]{2,1,0:T(8,128)(2,1)S(1)}, u32[]{:S(2)}, u32[]{:S(2)}) async-start(bf16[8,128,1024]{2,1,0:T(8,128)(2,1)} %shard_map.102), calls=%async_computation | async-start | bytes 4194304 | tf_op jit(solution)/shard_map/all_to_all | solution.py:122
  13.0 18.4 %copy-start.8 = (f32[256,32]{0,1:T(8,128)S(1)}, f32[256,32]{0,1:T(8,128)}, u32[]{:S(2)}) copy-start(f32[256,32]{0,1:T(8,128)} %param.13) | copy-start | bytes 98308
  13.0 18.4 %copy-start.9 = (f32[256,32]{0,1:T(8,128)S(1)}, f32[256,32]{0,1:T(8,128)}, u32[]{:S(2)}) copy-start(f32[256,32]{0,1:T(8,128)} %param.11) | copy-start | bytes 98308
  13.0 18.4 %copy-start.10 = (f32[256,32]{0,1:T(8,128)S(1)}, f32[256,32]{0,1:T(8,128)}, u32[]{:S(2)}) copy-start(f32[256,32]{0,1:T(8,128)} %param.12) | copy-start | bytes 98308
  13.0 36.6 %collective-permute-start = (bf16[256,512]{1,0:T(8,128)(2,1)S(1)}, bf16[256,512]{1,0:T(8,128)(2,1)}, u32[]{:S(2)}, u32[]{:S(2)}) collective-permute-start(bf16[256,512]{1,0:T(8,128)(2,1)S(1)} %bitcast_convert_fusion), channel_id=1, source_target_pairs={{0,1},{1,2},{2,3},{3,0},{4,5},{5,6},{6,7},{7,4},{8,9},{9,10},{10,1... | collective-permute-start | bytes 786440 | tf_op jit(solution)/shard_map/ppermute | solution.py:116
  18.9 41.6 %collective-permute-start.1 = (bf16[256,512]{1,0:T(8,128)(2,1)S(1)}, bf16[256,512]{1,0:T(8,128)(2,1)S(1)}, u32[]{:S(2)}, u32[]{:S(2)}) collective-permute-start(bf16[256,512]{1,0:T(8,128)(2,1)S(1)} %bitcast_convert_fusion), channel_id=1, source_target_pairs={{0,2},{1,3},{2,0},{3,1},{4,6},{5,7},{6,4},{7,5},{8,10},{9,11},{10,... | collective-permute-start | bytes 786440 | tf_op jit(solution)/shard_map/ppermute | solution.py:116
  26.8 34.4 %collective-permute-start.2 = (bf16[256,512]{1,0:T(8,128)(2,1)S(1)}, bf16[256,512]{1,0:T(8,128)(2,1)S(1)}, u32[]{:S(2)}, u32[]{:S(2)}) collective-permute-start(bf16[256,512]{1,0:T(8,128)(2,1)S(1)} %bitcast_convert_fusion), channel_id=1, source_target_pairs={{0,3},{1,0},{2,1},{3,2},{4,7},{5,4},{6,5},{7,6},{8,11},{9,8},{10,9... | collective-permute-start | bytes 786440 | tf_op jit(solution)/shard_map/ppermute | solution.py:116
  30.4 1.0 copy-start.6
  61.9 1.3 copy-start
  68.0 20.9 %copy-start.2 = (bf16[1,128,512]{2,1,0:T(8,128)(2,1)S(1)}, bf16[1,128,512]{2,1,0:T(8,128)(2,1)}, u32[]{:S(2)}) copy-start(bf16[1,128,512]{2,1,0:T(8,128)(2,1)} %param.8) | copy-start | bytes 393220
  68.0 20.9 %copy-start.3 = (f32[128]{0:T(128)S(1)}, f32[128]{0:T(128)}, u32[]{:S(2)}) copy-start(f32[128]{0:T(128)} %param.9) | copy-start | bytes 1540
  68.0 20.9 %all-to-all-start.1 = ((bf16[8,128,512]{2,1,0:T(8,128)(2,1)}), bf16[8,128,512]{2,1,0:T(8,128)(2,1)S(1)}, u32[]{:S(2)}, u32[]{:S(2)}) async-start(bf16[8,128,512]{2,1,0:T(8,128)(2,1)} %bitcast.73), calls=%async_computation.1 | async-start | bytes 2097152 | tf_op jit(solution)/shard_map/all_to_all | solution.py:122
  73.5 6.6 %collective-permute-start.3 = (f32[32,256]{1,0:T(8,128)S(1)}, f32[32,256]{1,0:T(8,128)S(1)}, u32[]{:S(2)}, u32[]{:S(2)}) collective-permute-start(f32[32,256]{1,0:T(8,128)S(1)} %fusion.3), channel_id=1, source_target_pairs={{0,32},{32,0},{1,33},{33,1},{2,34},{34,2},{3,35},{35,3},{4,36},{36... | collective-permute-start | bytes 98312 | tf_op jit(solution)/shard_map/ppermute | solution.py:132
  80.1 8.7 %collective-permute-start.4 = (f32[2,32,256]{2,1,0:T(8,128)S(1)}, f32[2,32,256]{2,1,0:T(8,128)S(1)}, u32[]{:S(2)}, u32[]{:S(2)}) collective-permute-start(f32[2,32,256]{2,1,0:T(8,128)S(1)} %bitcast_dynamic-update-slice_fusion.9), channel_id=1, source_target_pairs={{0,256},{256,0},{1,257},{257,1},{2,258},{258,2},{3,259},{259,3},{4... | collective-permute-start | bytes 196616 | tf_op jit(solution)/shard_map/ppermute | solution.py:132
  90.3 22.9 %copy-start.1 = (bf16[8,128,1024]{2,1,0:T(8,128)(2,1)S(1)}, bf16[8,128,1024]{2,1,0:T(8,128)(2,1)}, u32[]{:S(2)}) copy-start(bf16[8,128,1024]{2,1,0:T(8,128)(2,1)} %copy-done) | copy-start | bytes 6291460
  90.3 22.9 %all-to-all-start.2 = ((bf16[8,128,512]{2,1,0:T(8,128)(2,1)}), bf16[8,128,512]{2,1,0:T(8,128)(2,1)S(1)}, u32[]{:S(2)}, u32[]{:S(2)}) async-start(bf16[8,128,512]{2,1,0:T(8,128)(2,1)} %shard_map.104), calls=%async_computation.2 | async-start | bytes 2097152 | tf_op jit(solution)/shard_map/all_to_all | solution.py:122
  97.0 12.1 %collective-permute-start.5 = (f32[2,2,32,256]{3,2,1,0:T(8,128)S(1)}, f32[2,2,32,256]{3,2,1,0:T(8,128)S(1)}, u32[]{:S(2)}, u32[]{:S(2)}) collective-permute-start(f32[2,2,32,256]{3,2,1,0:T(8,128)S(1)} %bitcast_dynamic-update-slice_fusion.7), channel_id=1, source_target_pairs={{0,64},{64,128},{128,192},{192,0},{1,65},{65,129},{129,193},{193,1... | collective-permute-start | bytes 393224 | tf_op jit(solution)/shard_map/ppermute | solution.py:132
  100.2 9.6 %collective-permute-start.6 = (f32[2,2,32,256]{3,2,1,0:T(8,128)S(1)}, f32[2,2,32,256]{3,2,1,0:T(8,128)S(1)}, u32[]{:S(2)}, u32[]{:S(2)}) collective-permute-start(f32[2,2,32,256]{3,2,1,0:T(8,128)S(1)} %bitcast_dynamic-update-slice_fusion.7), channel_id=1, source_target_pairs={{0,128},{64,192},{128,0},{192,64},{1,129},{65,193},{129,1},{193,65... | collective-permute-start | bytes 393224 | tf_op jit(solution)/shard_map/ppermute | solution.py:132
  104.5 6.0 %collective-permute-start.7 = (f32[2,2,32,256]{3,2,1,0:T(8,128)S(1)}, f32[2,2,32,256]{3,2,1,0:T(8,128)S(1)}, u32[]{:S(2)}, u32[]{:S(2)}) collective-permute-start(f32[2,2,32,256]{3,2,1,0:T(8,128)S(1)} %bitcast_dynamic-update-slice_fusion.7), channel_id=1, source_target_pairs={{0,192},{64,0},{128,64},{192,128},{1,193},{65,1},{129,65},{193,129... | collective-permute-start | bytes 393224 | tf_op jit(solution)/shard_map/ppermute | solution.py:132
  116.1 48.3 %copy-start.5 = (f32[1,256,512]{2,1,0:T(8,128)S(1)}, f32[1,256,512]{2,1,0:T(8,128)}, u32[]{:S(2)}) copy-start(f32[1,256,512]{2,1,0:T(8,128)} %param.10) | copy-start | bytes 1572868
  116.1 48.3 %copy-start.7 = (f32[512,256]{0,1:T(8,128)S(1)}, f32[512,256]{0,1:T(8,128)}, u32[]{:S(2)}) copy-start(f32[512,256]{0,1:T(8,128)} %copy.35) | copy-start | bytes 1572868

commit v5 on v4

v5 whole, which is shorter than its diff:
```python
import functools

import jax
import jax.numpy as jnp
from jax import lax
from jax.experimental import pallas as pl
from jax.experimental.pallas import tpu as pltpu
from jax.sharding import Mesh
from jax.sharding import PartitionSpec as P

HEAD = 128

inner_rate = 0.5
outer_rate = 0.7
keep_rate = 0.9
blend_rate = 0.5
epsilon = 1e-06

REPLICA = ("y_lo", "x", "core")
FSDP = ("z", "y_hi")
ALL = REPLICA + FSDP

EIGHT, FOUR = 8, 4


def place(core, p, q):
    return (p, q) if core == 0 else (2 * q + p // 4, p % 4)


def device(y_lo, x, core, p, q):
    z, y_hi = place(core, p, q)
    return (((y_lo * 4 + x) * 2 + core) * 8 + z) * 4 + y_hi


TEAMS = [(y_lo, x, core) for y_lo in range(2) for x in range(4) for core in range(2)]
RINGS_OF_8 = [[device(*team, p, q) for p in range(EIGHT)] for team in TEAMS for q in range(FOUR)]
RINGS_OF_4 = [[device(*team, p, q) for q in range(FOUR)] for team in TEAMS for p in range(EIGHT)]


def slope_kernel(factor, parts_ref, cotangent_ref, gain_ref, out_ref):
    pieces = parts_ref.shape[0]
    gain = gain_ref[...]
    for head in range(out_ref.shape[1] // HEAD):
        lanes = slice(head * HEAD, (head + 1) * HEAD)
        hidden = parts_ref[0, :, lanes].astype(jnp.float32)
        for piece in range(1, pieces):
            hidden = hidden + parts_ref[piece, :, lanes].astype(jnp.float32)
        hidden = hidden * factor
        spread = jnp.sqrt(jnp.mean(hidden * hidden, axis=-1, keepdims=True) + epsilon)
        unit = hidden / spread
        slope = cotangent_ref[:, lanes].astype(jnp.float32) * gain
        key_slope = (slope - unit * jnp.mean(slope * unit, axis=-1, keepdims=True)) / spread
        key_slope = key_slope.T.astype(jnp.bfloat16)
        for piece in range(out_ref.shape[0]):
            out_ref[piece, lanes, :] = key_slope


def key_slopes(parts, cotangent, gain, factor):
    return pl.pallas_call(
        functools.partial(slope_kernel, factor),
        out_shape=jax.ShapeDtypeStruct((parts.shape[0],) + parts.shape[:0:-1], jnp.bfloat16),
        compiler_params=pltpu.CompilerParams(vmem_limit_bytes=8 * 1024 * 1024),
        cost_estimate=pl.CostEstimate(flops=2_000_000, bytes_accessed=2_500_000, transcendentals=2000),
    )(parts, cotangent, gain)


def split_kernel(core_ref, feats_ref, out_ref, held, sems, out_sems):
    core = core_ref[0]
    width = feats_ref.shape[1] // (EIGHT * FOUR)
    loads, stores = [], []
    for p in range(EIGHT):
        for q in range(FOUR):
            block = jnp.where(core == 0, FOUR * p + q, EIGHT * q + p)
            loads.append(
                pltpu.make_async_copy(
                    feats_ref.at[:, pl.ds(pl.multiple_of(block * width, width), width)],
                    held.at[p, :, pl.ds(q * width, width)],
                    sems.at[p, q],
                )
            )
        stores.append(pltpu.make_async_copy(held.at[p], out_ref.at[p], out_sems.at[p]))
    for load in loads:
        load.start()
    for p in range(EIGHT):
        for load in loads[FOUR * p : FOUR * (p + 1)]:
            load.wait()
        stores[p].start()
    for store in stores:
        store.wait()


def split_columns(core, feats):
    tokens, width = feats.shape
    shape = (EIGHT, tokens, width // EIGHT)
    return pl.pallas_call(
        split_kernel,
        out_shape=jax.ShapeDtypeStruct(shape, feats.dtype),
        in_specs=[pl.BlockSpec(memory_space=pltpu.SMEM), pl.BlockSpec(memory_space=pltpu.HBM)],
        out_specs=pl.BlockSpec(memory_space=pltpu.HBM),
        scratch_shapes=[
            pltpu.VMEM(shape, feats.dtype),
            pltpu.SemaphoreType.DMA((EIGHT, FOUR)),
            pltpu.SemaphoreType.DMA((EIGHT,)),
        ],
        compiler_params=pltpu.CompilerParams(vmem_limit_bytes=60 * 1024 * 1024),
        cost_estimate=pl.CostEstimate(flops=0, bytes_accessed=4 * tokens * width, transcendentals=0),
    )(core, feats)


def gather_rows(x):
    out = [x]
    for step in range(1, FOUR):
        pairs = [(ring[i], ring[(i + step) % FOUR]) for ring in RINGS_OF_4 for i in range(FOUR)]
        out.append(lax.ppermute(x, ALL, pairs))
    return out


def exchange(x, rings):
    return lax.all_to_all(x, ALL, 0, 0, axis_index_groups=rings)


def gather_by_permutes(x, axis):
    size = lax.axis_size(axis)
    me = lax.axis_index(axis)
    out = jnp.zeros((size,) + x.shape, x.dtype)
    for step in range(size):
        piece = x
        if step:
            piece = lax.ppermute(x, axis, [(i, (i + step) % size) for i in range(size)])
        out = lax.dynamic_update_index_in_dim(out, piece, lax.rem(me + size - step, size), 0)
    return out


def project_kernel(q_ref, owned_ref, *refs):
    pieces, out_ref, weight_ref = refs[:-2], refs[-2], refs[-1]
    width = pieces[0].shape[0]
    for step, piece in enumerate(pieces):
        first = lax.rem(q_ref[0] + len(pieces) - step, len(pieces)) * width
        weight_ref[pl.ds(pl.multiple_of(first, width), width), :] = piece[...]
    block = owned_ref.shape[0] // 4
    for i in range(4):
        rows = slice(i * block, (i + 1) * block)
        out_ref[rows, :] = jnp.dot(
            owned_ref[rows, :], weight_ref[...], preferred_element_type=jnp.float32
        ).astype(out_ref.dtype)


def project(q, owned, pieces):
    rows, depth = owned.shape
    columns = pieces[0].shape[1]
    return pl.pallas_call(
        project_kernel,
        out_shape=jax.ShapeDtypeStruct((rows, columns), jnp.bfloat16),
        in_specs=[pl.BlockSpec(memory_space=pltpu.SMEM)]
        + [pl.BlockSpec(memory_space=pltpu.VMEM)] * (1 + len(pieces)),
        out_specs=pl.BlockSpec(memory_space=pltpu.VMEM),
        scratch_shapes=[pltpu.VMEM((depth, columns), jnp.bfloat16)],
        compiler_params=pltpu.CompilerParams(vmem_limit_bytes=12 * 1024 * 1024),
        cost_estimate=pl.CostEstimate(
            flops=2 * rows * depth * columns,
            bytes_accessed=2 * (rows * depth + depth * columns + rows * columns),
            transcendentals=0,
        ),
    )(q, owned, *pieces)


MARKS = 16


def gradient_kernel(owned_ref, slopes_ref, out_ref, all_slopes_ref):
    pieces, columns, tokens = slopes_ref.shape
    largest = jnp.abs(slopes_ref[0])
    for piece in range(pieces):
        all_slopes_ref[:, piece * tokens : (piece + 1) * tokens] = slopes_ref[piece]
        if piece:
            largest = jnp.maximum(largest, jnp.abs(slopes_ref[piece]))
    largest = jnp.max(largest.astype(jnp.float32), axis=0, keepdims=True)
    bound = 30.0 * owned_ref.shape[0] * jnp.max(largest, axis=1, keepdims=True)
    exponent = jnp.ceil(jnp.log2(jnp.maximum(bound, 1e-30))) - 15.0
    receivers, _, rows = out_ref.shape
    for i in range(receivers):
        sums = jnp.dot(
            all_slopes_ref[...],
            owned_ref[:, i * rows : (i + 1) * rows],
            preferred_element_type=jnp.float32,
        )
        out_ref[i, :columns] = sums * jnp.exp2(-exponent)
        out_ref[i, columns:] = jnp.broadcast_to(exponent, (MARKS, rows))


def gradient_parts(owned, slopes, receivers):
    tokens, width = owned.shape
    columns = slopes.shape[1]
    rows = width // receivers
    return pl.pallas_call(
        gradient_kernel,
        out_shape=jax.ShapeDtypeStruct((receivers, columns + MARKS, rows), jnp.float32),
        in_specs=[pl.BlockSpec(memory_space=pltpu.VMEM)] * 2,
        out_specs=pl.BlockSpec(memory_space=pltpu.VMEM),
        scratch_shapes=[pltpu.VMEM((columns, tokens), jnp.bfloat16)],
        compiler_params=pltpu.CompilerParams(vmem_limit_bytes=12 * 1024 * 1024),
        cost_estimate=pl.CostEstimate(
            flops=2 * tokens * width * columns,
            bytes_accessed=2 * (tokens * width + tokens * columns) + 4 * width * columns,
            transcendentals=0,
        ),
    )(owned, slopes)


def squares_kernel(gradient_ref, out_ref):
    gradient = gradient_ref[...]
    columns = jnp.sum(gradient * gradient, axis=0, keepdims=True)
    out_ref[...] = jnp.broadcast_to(jnp.sum(columns, axis=1, keepdims=True), out_ref.shape)


def squares_for_all(gradient, receivers):
    return pl.pallas_call(
        squares_kernel,
        out_shape=jax.ShapeDtypeStruct((receivers, 8, 128), jnp.float32),
        compiler_params=pltpu.CompilerParams(vmem_limit_bytes=8 * 1024 * 1024),
        cost_estimate=pl.CostEstimate(flops=2 * gradient.size, bytes_accessed=4 * gradient.size, transcendentals=0),
    )(gradient)


def step_kernel(size, shares_ref, own_ref, gradient_ref, after_ref):
    rate = inner_rate / jnp.sqrt(jnp.sum(shares_ref[...], axis=0) / size + epsilon)
    after_ref[...] = own_ref[...].T - rate[0:1, 0:1] * gradient_ref[...]


def step(shares, own_rows, gradient_t):
    size = shares.shape[0] * own_rows.size
    return pl.pallas_call(
        functools.partial(step_kernel, size),
        out_shape=jax.ShapeDtypeStruct(gradient_t.shape, jnp.float32),
        compiler_params=pltpu.CompilerParams(vmem_limit_bytes=8 * 1024 * 1024),
        cost_estimate=pl.CostEstimate(flops=2 * own_rows.size, bytes_accessed=12 * own_rows.size, transcendentals=0),
    )(shares, own_rows, gradient_t)


def blend_kernel(after_ref, new_ref, out_ref):
    xs, y_los, cores, width, rows = new_ref.shape
    for y_lo in range(y_los):
        for x in range(xs):
            first = (y_lo * xs + x) * cores * width
            part = slice(first, first + cores * width)
            new = new_ref[x, y_lo].reshape(cores * width, rows)
            out_ref[:, part] = (blend_rate * new + (1.0 - blend_rate) * after_ref[part, :]).T


def blend(after_step_t, new_rows_t):
    return pl.pallas_call(
        blend_kernel,
        out_shape=jax.ShapeDtypeStruct(after_step_t.shape[::-1], jnp.float32),
        compiler_params=pltpu.CompilerParams(vmem_limit_bytes=8 * 1024 * 1024),
        cost_estimate=pl.CostEstimate(
            flops=3 * after_step_t.size, bytes_accessed=12 * after_step_t.size, transcendentals=0
        ),
    )(after_step_t, new_rows_t)


def shards(
    activations, key_cotangent, key_gain, local_weight, global_weight, outer_momentum, late_delta
):
    feats = activations[0]
    own_rows = local_weight[0]
    tokens, width = feats.shape
    rows, columns = own_rows.shape
    factor = width ** (-0.5)
    replicas = lax.axis_size(REPLICA)

    core = lax.axis_index("core")
    q = jnp.where(core == 0, lax.axis_index("y_hi"), lax.axis_index("z") // 2)

    owned = exchange(split_columns(core.reshape(1), feats), RINGS_OF_8)
    owned = owned.reshape(EIGHT * tokens, width // EIGHT)
    weight = gather_rows(own_rows.astype(jnp.bfloat16))

    global_t, momentum_t, late_t = global_weight.T, outer_momentum.T, late_delta.T
    next_momentum_t = keep_rate * momentum_t + late_t
    next_global_t = global_t - outer_rate * (late_t + keep_rate * next_momentum_t)
    new_rows_t = gather_by_permutes(gather_by_permutes(next_global_t, "core"), "y_lo")
    owned, weight, new_rows_t = lax.optimization_barrier((owned, weight, new_rows_t))
    parts = project(q.reshape(1), owned, weight).reshape(EIGHT, tokens, columns)
    parts = exchange(parts, RINGS_OF_8)
    slopes = key_slopes(parts, key_cotangent[0], key_gain.reshape(1, HEAD), factor)
    slopes = exchange(slopes, RINGS_OF_8)

    scaled = gradient_parts(owned, slopes, FOUR).astype(jnp.float16)
    scaled, new_rows_t = lax.optimization_barrier((scaled, new_rows_t))
    new_rows_t = gather_by_permutes(new_rows_t, "x")
    pieces = exchange(scaled, RINGS_OF_4)
    pieces, new_rows_t = lax.optimization_barrier((pieces, new_rows_t))
    unscale = jnp.exp2(pieces[:, columns, 0].astype(jnp.float32)) * factor
    gradient_t = jnp.sum(pieces[:, :columns].astype(jnp.float32) * unscale[:, None, None], axis=0)
    shares = lax.all_to_all(squares_for_all(gradient_t, EIGHT * FOUR), FSDP, 0, 0)
    after_step_t = step(shares, own_rows, gradient_t)

    sent_rows = after_step_t.reshape(replicas, columns // replicas, rows)
    received = lax.all_to_all(sent_rows.astype(jnp.float16), REPLICA, 0, 0).astype(jnp.float32)
    outer_delta_t = global_t - jnp.sum(received, axis=0) / replicas
    next_local = blend(after_step_t, new_rows_t)
    return (next_local[None], next_global_t.T, next_momentum_t.T, outer_delta_t.T)


def solution(mesh):
    split = Mesh(mesh.devices.reshape(2, 4, 2, 8, 4), ("y_lo", "x", "core", "z", "y_hi"))
    whole = P(REPLICA, FSDP, None)
    outer = P(FSDP, REPLICA)
    return jax.shard_map(
        shards,
        mesh=split,
        in_specs=(whole, whole, P(), whole, outer, outer, outer),
        out_specs=(whole, outer, outer, outer),
        check_vma=False,
    )
```

time: 188 us -> 178 us (0.947)
  starting transfers between devices: 57.6 us -> 70.8 us
  local copies, waits for them, and re-layouts: 12.1 us -> 2.3 us
  blocking collectives: 65.6 us -> 55.8 us
  Pallas kernels: 11.4 us -> 8.6 us
    all_to_all x2 -> x1, blocking collectives: 38.5 us -> 16.2 us  [shards(): lax.all_to_all(squares_for_all(gradient_t, EIGHT * FOUR), FSDP, 0, 0)]
    ppermute x3, waiting for transfers between devices: 27.3 us -> 10.2 us  [gather_rows(): out.append(lax.ppermute(x, ALL, pairs))]
    all_to_all x0 -> x1, starting transfers between devices: none -> 15.7 us  [shards(): lax.all_to_all(sent_rows.astype(jnp.float16), REPLICA, 0, 0)]
    all_to_all x1 -> x2, blocking collectives: 27.1 us -> 39.6 us  [exchange(): return lax.all_to_all(x, ALL, 0, 0, axis_index_groups=rings)]
    ppermute x5, waiting for transfers between devices: 7.23 us -> 14.5 us  [gather_by_permutes(): piece = lax.ppermute(x, axis, [(i, (i + step) % size) for i in range(size)])]
    all_to_all x0 -> x1, waiting for transfers between devices: none -> 5.89 us  [shards(): lax.all_to_all(sent_rows.astype(jnp.float16), REPLICA, 0, 0)]
    all_to_all x3 -> x2, waiting for transfers between devices: 0.01 us -> 4.18 us  [exchange(): return lax.all_to_all(x, ALL, 0, 0, axis_index_groups=rings)]
    dynamic_update_slice x3 -> x0, local copies, waits for them, and re-layouts: 3.15 us -> none  [gather_rows(): lax.dynamic_update_index_in_dim(out, piece, lax.rem(q + FOUR - step, FOUR...]
  transfers between devices with their start and end apart: 11 -> 11, of which waited for: 5 -> 5; matrix products, arithmetic and copies ran while one was open for 5% -> 2% of each run, Pallas kernels for 0% -> 1%
where the time goes in v5:
time: 178 us; the launch traced here: 177 us
  starting transfers between devices  70.8 us (40%)
  blocking collectives  55.8 us (31%)
  waiting for transfers between devices  34.8 us (20%)
  Pallas kernels  8.6 us (5%)
  other arithmetic  3.74 us (2%)
  local copies, waits for them, and re-layouts  2.3 us (1%)
    all_to_all x2, blocking collectives, exchange(): return lax.all_to_all(x, ALL, 0, 0, axis_index_groups=rings)  39.6 us
    all_to_all x2, starting transfers between devices, exchange(): return lax.all_to_all(x, ALL, 0, 0, axis_index_groups=rings)  22.1 us
    ppermute x5, starting transfers between devices, gather_by_permutes(): piece = lax.ppermute(x, axis, [(i, (i + step) % size) for i in range(size)])  18 us
    all_to_all x1, blocking collectives, shards(): lax.all_to_all(squares_for_all(gradient_t, EIGHT * FOUR), FSDP, 0, 0)  16.2 us
    all_to_all x1, starting transfers between devices, shards(): lax.all_to_all(sent_rows.astype(jnp.float16), REPLICA, 0, 0)  15.7 us
    ppermute x3, starting transfers between devices, gather_rows(): out.append(lax.ppermute(x, ALL, pairs))  15 us
    ppermute x5, waiting for transfers between devices, gather_by_permutes(): piece = lax.ppermute(x, axis, [(i, (i + step) % size) for i in range(size)])  14.5 us
    ppermute x3, waiting for transfers between devices, gather_rows(): out.append(lax.ppermute(x, ALL, pairs))  10.2 us
  transfers between devices with their start and end apart: 11, of which 5 were waited for; matrix products, arithmetic and copies ran while one was open for 2% of the time, Pallas kernels for 1%

profile of v5, /device:TPU:1, one launch (start us, length us, event | category | flops | bytes accessed | tf_op | source)
XLA Modules:
  0.0 177.0 jit_solution(2061701321431693516)
XLA Ops:
  0.6 2.7 %shard_map.102 = bf16[8,128,1024]{2,1,0:T(8,128)(2,1)} custom-call(s32[1]{0:T(128)} %bitcast.core_ref, bf16[128,8192]{1,0:T(8,128)(2,1)} %bitcast.52), custom_call_target="tpu_custom_call" | custom-call | bytes 4194304 | tf_op jit(solution)/shard_map/pallas_call | solution.py:95
  3.4 9.6 %all-to-all-start = ((bf16[8,128,1024]{2,1,0:T(8,128)(2,1)}), bf16[8,128,1024]{2,1,0:T(8,128)(2,1)S(1)}, u32[]{:S(2)}, u32[]{:S(2)}) async-start(bf16[8,128,1024]{2,1,0:T(8,128)(2,1)} %shard_map.102), calls=%async_computation | async-start | bytes 4194304 | tf_op jit(solution)/shard_map/all_to_all | solution.py:119
  14.3 4.3 %collective-permute-start.3 = (f32[32,256]{1,0:T(8,128)S(1)}, f32[32,256]{1,0:T(8,128)S(1)}, u32[]{:S(2)}, u32[]{:S(2)}) collective-permute-start(f32[32,256]{1,0:T(8,128)S(1)} %get-tuple-element.27), channel_id=1, source_target_pairs={{0,32},{32,0},{1,33},{33,1},{2,34},{34,2},{3,35},{35,3},{4,36},{36... | collective-permute-start | bytes 98312 | tf_op jit(solution)/shard_map/ppermute | solution.py:129
  18.6 4.5 %collective-permute-start = (bf16[256,512]{1,0:T(8,128)(2,1)S(1)}, bf16[256,512]{1,0:T(8,128)(2,1)S(1)}, u32[]{:S(2)}, u32[]{:S(2)}) collective-permute-start(bf16[256,512]{1,0:T(8,128)(2,1)S(1)} %bitcast_convert_fusion.refs_0_), channel_id=1, source_target_pairs={{0,1},{1,2},{2,3},{3,0},{4,5},{5,6},{6,7},{7,4},{8,9},{9,10},{10,1... | collective-permute-start | bytes 786440 | tf_op jit(solution)/shard_map/ppermute | solution.py:114
  23.1 6.8 %collective-permute-start.1 = (bf16[256,512]{1,0:T(8,128)(2,1)S(1)}, bf16[256,512]{1,0:T(8,128)(2,1)S(1)}, u32[]{:S(2)}, u32[]{:S(2)}) collective-permute-start(bf16[256,512]{1,0:T(8,128)(2,1)S(1)} %bitcast_convert_fusion.refs_0_), channel_id=1, source_target_pairs={{0,2},{1,3},{2,0},{3,1},{4,6},{5,7},{6,4},{7,5},{8,10},{9,11},{10,... | collective-permute-start | bytes 786440 | tf_op jit(solution)/shard_map/ppermute | solution.py:114
  30.0 3.6 %collective-permute-start.2 = (bf16[256,512]{1,0:T(8,128)(2,1)S(1)}, bf16[256,512]{1,0:T(8,128)(2,1)}, u32[]{:S(2)}, u32[]{:S(2)}) collective-permute-start(bf16[256,512]{1,0:T(8,128)(2,1)S(1)} %bitcast_convert_fusion.refs_0_), channel_id=1, source_target_pairs={{0,3},{1,0},{2,1},{3,2},{4,7},{5,4},{6,5},{7,6},{8,11},{9,8},{10,9... | collective-permute-start | bytes 786440 | tf_op jit(solution)/shard_map/ppermute | solution.py:114
  34.2 3.2 %collective-permute-start.4 = (f32[2,32,256]{2,1,0:T(8,128)}, f32[2,32,256]{2,1,0:T(8,128)S(1)}, u32[]{:S(2)}, u32[]{:S(2)}) collective-permute-start(f32[2,32,256]{2,1,0:T(8,128)} %bitcast_dynamic-update-slice_fusion.6), channel_id=1, source_target_pairs={{0,256},{256,0},{1,257},{257,1},{2,258},{258,2},{3,259},{259,3},{4... | collective-permute-start | bytes 196616 | tf_op jit(solution)/shard_map/ppermute | solution.py:129
  38.3 12.0 %collective-permute-done.4 = f32[2,32,256]{2,1,0:T(8,128)S(1)} collective-permute-done((f32[2,32,256]{2,1,0:T(8,128)}, f32[2,32,256]{2,1,0:T(8,128)S(1)}, u32[]{:S(2)}, u32[]{:S(2)}) %collective-permute-start.4) | collective-permute-done | bytes 65568 | tf_op jit(solution)/shard_map/ppermute | solution.py:129
  50.3 10.2 %collective-permute-done.1.refs_2_ = bf16[256,512]{1,0:T(8,128)(2,1)S(1)} collective-permute-done((bf16[256,512]{1,0:T(8,128)(2,1)S(1)}, bf16[256,512]{1,0:T(8,128)(2,1)S(1)}, u32[]{:S(2)}, u32[]{:S(2)}) %collective-permute-start.1) | collective-permute-done | bytes 262176 | tf_op jit(solution)/shard_map/ppermute | solution.py:114
  60.5 2.3 %shard_map.103 = bf16[1024,512]{1,0:T(8,128)(2,1)S(1)} custom-call(s32[1]{0:T(128)} %bitcast.11.q_ref, bf16[1024,1024]{1,0:T(8,128)(2,1)S(1)} %bitcast.46, bf16[256,512]{1,0:T(8,128)(2,1)S(1)} %bitcast_convert_fusion.refs_0_, bf16[256,512]{1,0:T(8,128)(2,1)S(1)} %collective-permute-done.refs_1_, bf16[256,512]{1,0:T(8,128)(2,1)S(1)} %collective-permute-done.1.refs_2_, ...), custom_call_target="tpu_custom_call" | custom-call | flops 1073741824 | bytes 4194304 | tf_op jit(solution)/shard_map/pallas_call | solution.py:151
  62.8 20.2 %all_to_all.30.parts_ref = bf16[8,128,512]{2,1,0:T(8,128)(2,1)S(1)} all-to-all(bf16[8,128,512]{2,1,0:T(8,128)(2,1)S(1)} %bitcast.48), channel_id=1, replica_groups={{0,4,8,12,16,20,24,28},{1,5,9,13,17,21,25,29},{2,6,10,14,18,22,26,30},{..., dimensions={0} | all-to-all | bytes 2097152 | tf_op jit(solution)/shard_map/all_to_all | solution.py:119
  83.6 19.4 %all_to_all.31.slopes_ref = bf16[8,512,128]{2,1,0:T(8,128)(2,1)S(1)} all-to-all(bf16[8,512,128]{2,1,0:T(8,128)(2,1)S(1)} %shard_map.104), channel_id=1, replica_groups={{0,4,8,12,16,20,24,28},{1,5,9,13,17,21,25,29},{2,6,10,14,18,22,26,30},{..., dimensions={0} | all-to-all | bytes 2097152 | tf_op jit(solution)/shard_map/all_to_all | solution.py:119
  103.0 1.4 shard_map.105
  104.4 1.2 convert_element_type.23
  105.6 12.5 %all-to-all-start.3 = ((f16[4,528,256]{2,1,0:T(8,128)(2,1)}), f16[4,528,256]{2,1,0:T(8,128)(2,1)S(1)}, u32[]{:S(2)}, u32[]{:S(2)}) async-start(f16[4,528,256]{2,1,0:T(8,128)(2,1)} %convert_element_type.23), calls=%async_computation.3 | async-start | bytes 2162688 | tf_op jit(solution)/shard_map/all_to_all | solution.py:119
  118.1 3.1 %collective-permute-start.5 = (f32[2,2,32,256]{3,2,1,0:T(8,128)S(1)}, f32[2,2,32,256]{3,2,1,0:T(8,128)S(1)}, u32[]{:S(2)}, u32[]{:S(2)}) collective-permute-start(f32[2,2,32,256]{3,2,1,0:T(8,128)S(1)} %bitcast_dynamic-update-slice_fusion.4), channel_id=1, source_target_pairs={{0,64},{64,128},{128,192},{192,0},{1,65},{65,129},{129,193},{193,1... | collective-permute-start | bytes 393224 | tf_op jit(solution)/shard_map/ppermute | solution.py:129
  121.3 4.4 %collective-permute-start.6 = (f32[2,2,32,256]{3,2,1,0:T(8,128)S(1)}, f32[2,2,32,256]{3,2,1,0:T(8,128)S(1)}, u32[]{:S(2)}, u32[]{:S(2)}) collective-permute-start(f32[2,2,32,256]{3,2,1,0:T(8,128)S(1)} %bitcast_dynamic-update-slice_fusion.4), channel_id=1, source_target_pairs={{0,128},{64,192},{128,0},{192,64},{1,129},{65,193},{129,1},{193,65... | collective-permute-start | bytes 393224 | tf_op jit(solution)/shard_map/ppermute | solution.py:129
  125.6 3.1 %collective-permute-start.7 = (f32[2,2,32,256]{3,2,1,0:T(8,128)S(1)}, f32[2,2,32,256]{3,2,1,0:T(8,128)S(1)}, u32[]{:S(2)}, u32[]{:S(2)}) collective-permute-start(f32[2,2,32,256]{3,2,1,0:T(8,128)S(1)} %bitcast_dynamic-update-slice_fusion.4), channel_id=1, source_target_pairs={{0,192},{64,0},{128,64},{192,128},{1,193},{65,1},{129,65},{193,129... | collective-permute-start | bytes 393224 | tf_op jit(solution)/shard_map/ppermute | solution.py:129
  128.8 2.5 %collective-permute-done.7 = f32[2,2,32,256]{3,2,1,0:T(8,128)S(1)} collective-permute-done((f32[2,2,32,256]{3,2,1,0:T(8,128)S(1)}, f32[2,2,32,256]{3,2,1,0:T(8,128)S(1)}, u32[]{:S(2)}, u32[]{:S(2)}) %collective-permute-start.7) | collective-permute-done | bytes 131104 | tf_op jit(solution)/shard_map/ppermute | solution.py:129
  131.3 4.2 %all-to-all-done.3 = f16[4,528,256]{2,1,0:T(8,128)(2,1)S(1)} async-done(((f16[4,528,256]{2,1,0:T(8,128)(2,1)}), f16[4,528,256]{2,1,0:T(8,128)(2,1)S(1)}, u32[]{:S(2)}, u32[]{:S(2)}) %all-to-all-start.3) | async-done | bytes 1081376 | tf_op jit(solution)/shard_map/all_to_all | solution.py:119
  136.1 16.2 %all_to_all.32.shares_ref = f32[32,8,128]{2,1,0:T(8,128)S(1)} all-to-all(f32[32,8,128]{2,1,0:T(8,128)S(1)} %shard_map.106), channel_id=1, replica_groups=mesh['y_lo'=2,'x'=4,'core'=2,'z'=8,'y_hi'=4] {'z','y_hi'}, dimensions={0} | all-to-all | bytes 262144 | tf_op jit(solution)/shard_map/all_to_all | solution.py:295
  153.3 15.7 %all-to-all-start.5 = ((f16[16,32,256]{2,1,0:T(8,128)(2,1)}), f16[16,32,256]{2,1,0:T(8,128)(2,1)S(1)}, u32[]{:S(2)}, u32[]{:S(2)}) async-start(f16[16,32,256]{2,1,0:T(8,128)(2,1)} %bitcast.20), calls=%async_computation.5 | async-start | bytes 524288 | tf_op jit(solution)/shard_map/all_to_all | solution.py:299
  169.1 1.3 shard_map.108
  170.4 5.9 %all-to-all-done.5 = f16[16,32,256]{2,1,0:T(8,128)(2,1)S(1)} async-done(((f16[16,32,256]{2,1,0:T(8,128)(2,1)}), f16[16,32,256]{2,1,0:T(8,128)(2,1)S(1)}, u32[]{:S(2)}, u32[]{:S(2)}) %all-to-all-start.5) | async-done | bytes 262176 | tf_op jit(solution)/shard_map/all_to_all | solution.py:299
  (44 shorter events, 5.8 us)
Async XLA Ops:
  3.3 10.3 %copy-start.3 = (f32[256,32]{0,1:T(8,128)S(1)}, f32[256,32]{0,1:T(8,128)}, u32[]{:S(2)}) copy-start(f32[256,32]{0,1:T(8,128)} %param.12) | copy-start | bytes 98308
  3.4 10.3 %copy-start.5 = (f32[256,32]{0,1:T(8,128)S(1)}, f32[256,32]{0,1:T(8,128)}, u32[]{:S(2)}) copy-start(f32[256,32]{0,1:T(8,128)} %param.13) | copy-start | bytes 98308
  3.4 10.3 %copy-start.7 = (f32[256,32]{0,1:T(8,128)S(1)}, f32[256,32]{0,1:T(8,128)}, u32[]{:S(2)}) copy-start(f32[256,32]{0,1:T(8,128)} %param.11) | copy-start | bytes 98308
  3.4 15.2 %copy-start = (f32[1,256,512]{2,1,0:T(8,128)S(1)}, f32[1,256,512]{2,1,0:T(8,128)}, u32[]{:S(2)}) copy-start(f32[1,256,512]{2,1,0:T(8,128)} %param.10) | copy-start | bytes 1572868
  3.4 57.1 %all-to-all-start = ((bf16[8,128,1024]{2,1,0:T(8,128)(2,1)}), bf16[8,128,1024]{2,1,0:T(8,128)(2,1)S(1)}, u32[]{:S(2)}, u32[]{:S(2)}) async-start(bf16[8,128,1024]{2,1,0:T(8,128)(2,1)} %shard_map.102), calls=%async_computation | async-start | bytes 4194304 | tf_op jit(solution)/shard_map/all_to_all | solution.py:119
  14.3 19.3 %collective-permute-start.3 = (f32[32,256]{1,0:T(8,128)S(1)}, f32[32,256]{1,0:T(8,128)S(1)}, u32[]{:S(2)}, u32[]{:S(2)}) collective-permute-start(f32[32,256]{1,0:T(8,128)S(1)} %get-tuple-element.27), channel_id=1, source_target_pairs={{0,32},{32,0},{1,33},{33,1},{2,34},{34,2},{3,35},{35,3},{4,36},{36... | collective-permute-start | bytes 98312 | tf_op jit(solution)/shard_map/ppermute | solution.py:129
  18.6 31.7 %collective-permute-start = (bf16[256,512]{1,0:T(8,128)(2,1)S(1)}, bf16[256,512]{1,0:T(8,128)(2,1)S(1)}, u32[]{:S(2)}, u32[]{:S(2)}) collective-permute-start(bf16[256,512]{1,0:T(8,128)(2,1)S(1)} %bitcast_convert_fusion.refs_0_), channel_id=1, source_target_pairs={{0,1},{1,2},{2,3},{3,0},{4,5},{5,6},{6,7},{7,4},{8,9},{9,10},{10,1... | collective-permute-start | bytes 786440 | tf_op jit(solution)/shard_map/ppermute | solution.py:114
  23.1 37.4 %collective-permute-start.1 = (bf16[256,512]{1,0:T(8,128)(2,1)S(1)}, bf16[256,512]{1,0:T(8,128)(2,1)S(1)}, u32[]{:S(2)}, u32[]{:S(2)}) collective-permute-start(bf16[256,512]{1,0:T(8,128)(2,1)S(1)} %bitcast_convert_fusion.refs_0_), channel_id=1, source_target_pairs={{0,2},{1,3},{2,0},{3,1},{4,6},{5,7},{6,4},{7,5},{8,10},{9,11},{10,... | collective-permute-start | bytes 786440 | tf_op jit(solution)/shard_map/ppermute | solution.py:114
  30.0 30.5 %collective-permute-start.2 = (bf16[256,512]{1,0:T(8,128)(2,1)S(1)}, bf16[256,512]{1,0:T(8,128)(2,1)}, u32[]{:S(2)}, u32[]{:S(2)}) collective-permute-start(bf16[256,512]{1,0:T(8,128)(2,1)S(1)} %bitcast_convert_fusion.refs_0_), channel_id=1, source_target_pairs={{0,3},{1,0},{2,1},{3,2},{4,7},{5,4},{6,5},{7,6},{8,11},{9,8},{10,9... | collective-permute-start | bytes 786440 | tf_op jit(solution)/shard_map/ppermute | solution.py:114
  34.2 16.1 %collective-permute-start.4 = (f32[2,32,256]{2,1,0:T(8,128)}, f32[2,32,256]{2,1,0:T(8,128)S(1)}, u32[]{:S(2)}, u32[]{:S(2)}) collective-permute-start(f32[2,32,256]{2,1,0:T(8,128)} %bitcast_dynamic-update-slice_fusion.6), channel_id=1, source_target_pairs={{0,256},{256,0},{1,257},{257,1},{2,258},{258,2},{3,259},{259,3},{4... | collective-permute-start | bytes 196616 | tf_op jit(solution)/shard_map/ppermute | solution.py:129
  62.8 20.2 %copy-start.1 = (bf16[1,128,512]{2,1,0:T(8,128)(2,1)S(1)}, bf16[1,128,512]{2,1,0:T(8,128)(2,1)}, u32[]{:S(2)}) copy-start(bf16[1,128,512]{2,1,0:T(8,128)(2,1)} %param.8) | copy-start | bytes 393220
  62.8 20.2 %copy-start.2 = (f32[128]{0:T(128)S(1)}, f32[128]{0:T(128)}, u32[]{:S(2)}) copy-start(f32[128]{0:T(128)} %param.9) | copy-start | bytes 1540
  105.6 29.9 %all-to-all-start.3 = ((f16[4,528,256]{2,1,0:T(8,128)(2,1)}), f16[4,528,256]{2,1,0:T(8,128)(2,1)S(1)}, u32[]{:S(2)}, u32[]{:S(2)}) async-start(f16[4,528,256]{2,1,0:T(8,128)(2,1)} %convert_element_type.23), calls=%async_computation.3 | async-start | bytes 2162688 | tf_op jit(solution)/shard_map/all_to_all | solution.py:119
  118.1 10.6 %collective-permute-start.5 = (f32[2,2,32,256]{3,2,1,0:T(8,128)S(1)}, f32[2,2,32,256]{3,2,1,0:T(8,128)S(1)}, u32[]{:S(2)}, u32[]{:S(2)}) collective-permute-start(f32[2,2,32,256]{3,2,1,0:T(8,128)S(1)} %bitcast_dynamic-update-slice_fusion.4), channel_id=1, source_target_pairs={{0,64},{64,128},{128,192},{192,0},{1,65},{65,129},{129,193},{193,1... | collective-permute-start | bytes 393224 | tf_op jit(solution)/shard_map/ppermute | solution.py:129
  121.3 7.5 %collective-permute-start.6 = (f32[2,2,32,256]{3,2,1,0:T(8,128)S(1)}, f32[2,2,32,256]{3,2,1,0:T(8,128)S(1)}, u32[]{:S(2)}, u32[]{:S(2)}) collective-permute-start(f32[2,2,32,256]{3,2,1,0:T(8,128)S(1)} %bitcast_dynamic-update-slice_fusion.4), channel_id=1, source_target_pairs={{0,128},{64,192},{128,0},{192,64},{1,129},{65,193},{129,1},{193,65... | collective-permute-start | bytes 393224 | tf_op jit(solution)/shard_map/ppermute | solution.py:129
  125.6 5.7 %collective-permute-start.7 = (f32[2,2,32,256]{3,2,1,0:T(8,128)S(1)}, f32[2,2,32,256]{3,2,1,0:T(8,128)S(1)}, u32[]{:S(2)}, u32[]{:S(2)}) collective-permute-start(f32[2,2,32,256]{3,2,1,0:T(8,128)S(1)} %bitcast_dynamic-update-slice_fusion.4), channel_id=1, source_target_pairs={{0,192},{64,0},{128,64},{192,128},{1,193},{65,1},{129,65},{193,129... | collective-permute-start | bytes 393224 | tf_op jit(solution)/shard_map/ppermute | solution.py:129
  152.4 23.9 %copy-start.4 = (f32[256,32]{0,1:T(8,128)S(1)}, f32[256,32]{0,1:T(8,128)}, u32[]{:S(2)}) copy-start(f32[256,32]{0,1:T(8,128)} %param.12) | copy-start | bytes 98308
  152.4 23.9 %copy-start.6 = (f32[256,32]{0,1:T(8,128)S(1)}, f32[256,32]{0,1:T(8,128)}, u32[]{:S(2)}) copy-start(f32[256,32]{0,1:T(8,128)} %param.13) | copy-start | bytes 98308
  152.4 23.9 %copy-start.8 = (f32[256,32]{0,1:T(8,128)S(1)}, f32[256,32]{0,1:T(8,128)}, u32[]{:S(2)}) copy-start(f32[256,32]{0,1:T(8,128)} %param.11) | copy-start | bytes 98308
  153.3 22.9 %all-to-all-start.5 = ((f16[16,32,256]{2,1,0:T(8,128)(2,1)}), f16[16,32,256]{2,1,0:T(8,128)(2,1)S(1)}, u32[]{:S(2)}, u32[]{:S(2)}) async-start(f16[16,32,256]{2,1,0:T(8,128)(2,1)} %bitcast.20), calls=%async_computation.5 | async-start | bytes 524288 | tf_op jit(solution)/shard_map/all_to_all | solution.py:299

commit v6 on v5

--- a/solution.py
+++ b/solution.py
@@ -283,13 +283,13 @@
     parts = project(q.reshape(1), owned, weight).reshape(EIGHT, tokens, columns)
     parts = exchange(parts, RINGS_OF_8)
     slopes = key_slopes(parts, key_cotangent[0], key_gain.reshape(1, HEAD), factor)
+    slopes, new_rows_t = lax.optimization_barrier((slopes, new_rows_t))
+    new_rows_t = gather_by_permutes(new_rows_t, "x")
     slopes = exchange(slopes, RINGS_OF_8)
+    slopes, new_rows_t = lax.optimization_barrier((slopes, new_rows_t))
 
     scaled = gradient_parts(owned, slopes, FOUR).astype(jnp.float16)
-    scaled, new_rows_t = lax.optimization_barrier((scaled, new_rows_t))
-    new_rows_t = gather_by_permutes(new_rows_t, "x")
     pieces = exchange(scaled, RINGS_OF_4)
-    pieces, new_rows_t = lax.optimization_barrier((pieces, new_rows_t))
     unscale = jnp.exp2(pieces[:, columns, 0].astype(jnp.float32)) * factor
     gradient_t = jnp.sum(pieces[:, :columns].astype(jnp.float32) * unscale[:, None, None], axis=0)
     shares = lax.all_to_all(squares_for_all(gradient_t, EIGHT * FOUR), FSDP, 0, 0)

time: 178 us -> 176 us (0.989)
  blocking collectives: 55.8 us -> 67.3 us
  starting transfers between devices: 70.8 us -> 61 us
    all_to_all x2, blocking collectives: 39.6 us -> 50.5 us  [exchange(): return lax.all_to_all(x, ALL, 0, 0, axis_index_groups=rings)]
    all_to_all x2, starting transfers between devices: 22.1 us -> 14.4 us  [exchange(): return lax.all_to_all(x, ALL, 0, 0, axis_index_groups=rings)]
    all_to_all x2, waiting for transfers between devices: 4.18 us -> 0.9 us  [exchange(): return lax.all_to_all(x, ALL, 0, 0, axis_index_groups=rings)]
    ppermute x5, waiting for transfers between devices: 14.5 us -> 17 us  [gather_by_permutes(): piece = lax.ppermute(x, axis, [(i, (i + step) % size) for i in range(size)])]
    all_to_all x1, starting transfers between devices: 15.7 us -> 13.6 us  [shards(): lax.all_to_all(sent_rows.astype(jnp.float16), REPLICA, 0, 0)]
  transfers between devices with their start and end apart: 11 -> 11, of which waited for: 5 -> 5; matrix products, arithmetic and copies ran while one was open for 2% -> 0% of each run, Pallas kernels for 1% -> 1%
where the time goes in v6:
time: 176 us; the launch traced here: 175 us
  blocking collectives  67.3 us (38%)
  starting transfers between devices  61 us (35%)
  waiting for transfers between devices  34.2 us (19%)
  Pallas kernels  8.64 us (5%)
  other arithmetic  2.14 us (1%)
    all_to_all x2, blocking collectives, exchange(): return lax.all_to_all(x, ALL, 0, 0, axis_index_groups=rings)  50.5 us
    ppermute x5, starting transfers between devices, gather_by_permutes(): piece = lax.ppermute(x, axis, [(i, (i + step) % size) for i in range(size)])  18 us
    ppermute x5, waiting for transfers between devices, gather_by_permutes(): piece = lax.ppermute(x, axis, [(i, (i + step) % size) for i in range(size)])  17 us
    all_to_all x1, blocking collectives, shards(): lax.all_to_all(squares_for_all(gradient_t, EIGHT * FOUR), FSDP, 0, 0)  16.8 us
    ppermute x3, starting transfers between devices, gather_rows(): out.append(lax.ppermute(x, ALL, pairs))  15 us
    all_to_all x2, starting transfers between devices, exchange(): return lax.all_to_all(x, ALL, 0, 0, axis_index_groups=rings)  14.4 us
    all_to_all x1, starting transfers between devices, shards(): lax.all_to_all(sent_rows.astype(jnp.float16), REPLICA, 0, 0)  13.6 us
    ppermute x3, waiting for transfers between devices, gather_rows(): out.append(lax.ppermute(x, ALL, pairs))  10.4 us
  transfers between devices with their start and end apart: 11, of which 5 were waited for; matrix products, arithmetic and copies ran while one was open for 0% of the time, Pallas kernels for 1%

profile of v6, /device:TPU:1, one launch (start us, length us, event | category | flops | bytes accessed | tf_op | source)
XLA Modules:
  0.0 175.2 jit_solution(1294663751727889708)
XLA Ops:
  0.6 2.7 %shard_map.102 = bf16[8,128,1024]{2,1,0:T(8,128)(2,1)} custom-call(s32[1]{0:T(128)} %bitcast.core_ref, bf16[128,8192]{1,0:T(8,128)(2,1)} %bitcast.52), custom_call_target="tpu_custom_call" | custom-call | bytes 4194304 | tf_op jit(solution)/shard_map/pallas_call | solution.py:95
  3.4 9.6 %all-to-all-start = ((bf16[8,128,1024]{2,1,0:T(8,128)(2,1)}), bf16[8,128,1024]{2,1,0:T(8,128)(2,1)S(1)}, u32[]{:S(2)}, u32[]{:S(2)}) async-start(bf16[8,128,1024]{2,1,0:T(8,128)(2,1)} %shard_map.102), calls=%async_computation | async-start | bytes 4194304 | tf_op jit(solution)/shard_map/all_to_all | solution.py:119
  13.1 4.3 %collective-permute-start.3 = (f32[32,256]{1,0:T(8,128)S(1)}, f32[32,256]{1,0:T(8,128)S(1)}, u32[]{:S(2)}, u32[]{:S(2)}) collective-permute-start(f32[32,256]{1,0:T(8,128)S(1)} %get-tuple-element.27), channel_id=1, source_target_pairs={{0,32},{32,0},{1,33},{33,1},{2,34},{34,2},{3,35},{35,3},{4,36},{36... | collective-permute-start | bytes 98312 | tf_op jit(solution)/shard_map/ppermute | solution.py:129
  17.4 4.5 %collective-permute-start = (bf16[256,512]{1,0:T(8,128)(2,1)S(1)}, bf16[256,512]{1,0:T(8,128)(2,1)S(1)}, u32[]{:S(2)}, u32[]{:S(2)}) collective-permute-start(bf16[256,512]{1,0:T(8,128)(2,1)S(1)} %bitcast_convert_fusion.refs_0_), channel_id=1, source_target_pairs={{0,1},{1,2},{2,3},{3,0},{4,5},{5,6},{6,7},{7,4},{8,9},{9,10},{10,1... | collective-permute-start | bytes 786440 | tf_op jit(solution)/shard_map/ppermute | solution.py:114
  21.9 6.8 %collective-permute-start.1 = (bf16[256,512]{1,0:T(8,128)(2,1)S(1)}, bf16[256,512]{1,0:T(8,128)(2,1)S(1)}, u32[]{:S(2)}, u32[]{:S(2)}) collective-permute-start(bf16[256,512]{1,0:T(8,128)(2,1)S(1)} %bitcast_convert_fusion.refs_0_), channel_id=1, source_target_pairs={{0,2},{1,3},{2,0},{3,1},{4,6},{5,7},{6,4},{7,5},{8,10},{9,11},{10,... | collective-permute-start | bytes 786440 | tf_op jit(solution)/shard_map/ppermute | solution.py:114
  28.8 3.6 %collective-permute-start.2 = (bf16[256,512]{1,0:T(8,128)(2,1)S(1)}, bf16[256,512]{1,0:T(8,128)(2,1)S(1)}, u32[]{:S(2)}, u32[]{:S(2)}) collective-permute-start(bf16[256,512]{1,0:T(8,128)(2,1)S(1)} %bitcast_convert_fusion.refs_0_), channel_id=1, source_target_pairs={{0,3},{1,0},{2,1},{3,2},{4,7},{5,4},{6,5},{7,6},{8,11},{9,8},{10,9... | collective-permute-start | bytes 786440 | tf_op jit(solution)/shard_map/ppermute | solution.py:114
  32.4 3.2 %collective-permute-start.4 = (f32[2,32,256]{2,1,0:T(8,128)S(1)}, f32[2,32,256]{2,1,0:T(8,128)S(1)}, u32[]{:S(2)}, u32[]{:S(2)}) collective-permute-start(f32[2,32,256]{2,1,0:T(8,128)S(1)} %bitcast_dynamic-update-slice_fusion.6), channel_id=1, source_target_pairs={{0,256},{256,0},{1,257},{257,1},{2,258},{258,2},{3,259},{259,3},{4... | collective-permute-start | bytes 196616 | tf_op jit(solution)/shard_map/ppermute | solution.py:129
  35.7 14.5 %collective-permute-done.4 = f32[2,32,256]{2,1,0:T(8,128)S(1)} collective-permute-done((f32[2,32,256]{2,1,0:T(8,128)S(1)}, f32[2,32,256]{2,1,0:T(8,128)S(1)}, u32[]{:S(2)}, u32[]{:S(2)}) %collective-permute-start.4) | collective-permute-done | bytes 65568 | tf_op jit(solution)/shard_map/ppermute | solution.py:129
  50.2 10.4 %collective-permute-done.1.refs_2_ = bf16[256,512]{1,0:T(8,128)(2,1)S(1)} collective-permute-done((bf16[256,512]{1,0:T(8,128)(2,1)S(1)}, bf16[256,512]{1,0:T(8,128)(2,1)S(1)}, u32[]{:S(2)}, u32[]{:S(2)}) %collective-permute-start.1) | collective-permute-done | bytes 262176 | tf_op jit(solution)/shard_map/ppermute | solution.py:114
  60.6 1.3 shard_map.103
  62.0 20.0 %all_to_all.30.parts_ref = bf16[8,128,512]{2,1,0:T(8,128)(2,1)S(1)} all-to-all(bf16[8,128,512]{2,1,0:T(8,128)(2,1)S(1)} %bitcast.48), channel_id=1, replica_groups={{0,4,8,12,16,20,24,28},{1,5,9,13,17,21,25,29},{2,6,10,14,18,22,26,30},{..., dimensions={0} | all-to-all | bytes 2097152 | tf_op jit(solution)/shard_map/all_to_all | solution.py:119
  82.0 1.5 shard_map.104
  83.5 4.8 %all-to-all-start.2 = ((bf16[8,512,128]{2,1,0:T(8,128)(2,1)}), bf16[8,512,128]{2,1,0:T(8,128)(2,1)S(1)}, u32[]{:S(2)}, u32[]{:S(2)}) async-start(bf16[8,512,128]{2,1,0:T(8,128)(2,1)} %shard_map.104), calls=%async_computation.2 | async-start | bytes 2097152 | tf_op jit(solution)/shard_map/all_to_all | solution.py:119
  88.3 3.1 %collective-permute-start.5 = (f32[2,2,32,256]{3,2,1,0:T(8,128)S(1)}, f32[2,2,32,256]{3,2,1,0:T(8,128)S(1)}, u32[]{:S(2)}, u32[]{:S(2)}) collective-permute-start(f32[2,2,32,256]{3,2,1,0:T(8,128)S(1)} %bitcast_dynamic-update-slice_fusion.4), channel_id=1, source_target_pairs={{0,64},{64,128},{128,192},{192,0},{1,65},{65,129},{129,193},{193,1... | collective-permute-start | bytes 393224 | tf_op jit(solution)/shard_map/ppermute | solution.py:129
  91.5 4.4 %collective-permute-start.6 = (f32[2,2,32,256]{3,2,1,0:T(8,128)S(1)}, f32[2,2,32,256]{3,2,1,0:T(8,128)S(1)}, u32[]{:S(2)}, u32[]{:S(2)}) collective-permute-start(f32[2,2,32,256]{3,2,1,0:T(8,128)S(1)} %bitcast_dynamic-update-slice_fusion.4), channel_id=1, source_target_pairs={{0,128},{64,192},{128,0},{192,64},{1,129},{65,193},{129,1},{193,65... | collective-permute-start | bytes 393224 | tf_op jit(solution)/shard_map/ppermute | solution.py:129
  95.8 3.1 %collective-permute-start.7 = (f32[2,2,32,256]{3,2,1,0:T(8,128)S(1)}, f32[2,2,32,256]{3,2,1,0:T(8,128)S(1)}, u32[]{:S(2)}, u32[]{:S(2)}) collective-permute-start(f32[2,2,32,256]{3,2,1,0:T(8,128)S(1)} %bitcast_dynamic-update-slice_fusion.4), channel_id=1, source_target_pairs={{0,192},{64,0},{128,64},{192,128},{1,193},{65,1},{129,65},{193,129... | collective-permute-start | bytes 393224 | tf_op jit(solution)/shard_map/ppermute | solution.py:129
  99.0 2.5 %collective-permute-done.7 = f32[2,2,32,256]{3,2,1,0:T(8,128)S(1)} collective-permute-done((f32[2,2,32,256]{3,2,1,0:T(8,128)S(1)}, f32[2,2,32,256]{3,2,1,0:T(8,128)S(1)}, u32[]{:S(2)}, u32[]{:S(2)}) %collective-permute-start.7) | collective-permute-done | bytes 131104 | tf_op jit(solution)/shard_map/ppermute | solution.py:129
  102.4 0.9 all-to-all-done.2.slopes_ref
  103.2 1.4 shard_map.105
  104.9 30.5 %all_to_all.31 = f16[4,528,256]{2,1,0:T(8,128)(2,1)S(1)} all-to-all(f16[4,528,256]{2,1,0:T(8,128)(2,1)S(1)} %convert_element_type.23), channel_id=1, replica_groups={{0,1,2,3},{4,5,6,7},{8,9,10,11},{12,13,14,15},{16,17,18,19},{20,21,22,2..., dimensions={0} | all-to-all | bytes 2162688 | tf_op jit(solution)/shard_map/all_to_all | solution.py:119
  136.1 16.8 %all_to_all.32.shares_ref = f32[32,8,128]{2,1,0:T(8,128)S(1)} all-to-all(f32[32,8,128]{2,1,0:T(8,128)S(1)} %shard_map.106), channel_id=1, replica_groups=mesh['y_lo'=2,'x'=4,'core'=2,'z'=8,'y_hi'=4] {'z','y_hi'}, dimensions={0} | all-to-all | bytes 262144 | tf_op jit(solution)/shard_map/all_to_all | solution.py:295
  153.8 13.6 %all-to-all-start.5 = ((f16[16,32,256]{2,1,0:T(8,128)(2,1)}), f16[16,32,256]{2,1,0:T(8,128)(2,1)S(1)}, u32[]{:S(2)}, u32[]{:S(2)}) async-start(f16[16,32,256]{2,1,0:T(8,128)(2,1)} %bitcast.20), calls=%async_computation.5 | async-start | bytes 524288 | tf_op jit(solution)/shard_map/all_to_all | solution.py:299
  167.4 1.3 shard_map.108
  168.7 5.9 %all-to-all-done.5 = f16[16,32,256]{2,1,0:T(8,128)(2,1)S(1)} async-done(((f16[16,32,256]{2,1,0:T(8,128)(2,1)}), f16[16,32,256]{2,1,0:T(8,128)(2,1)S(1)}, u32[]{:S(2)}, u32[]{:S(2)}) %all-to-all-start.5) | async-done | bytes 262176 | tf_op jit(solution)/shard_map/all_to_all | solution.py:299
  (44 shorter events, 3.5 us)
Async XLA Ops:
  3.3 9.7 %copy-start.6 = (f32[256,32]{0,1:T(8,128)S(1)}, f32[256,32]{0,1:T(8,128)}, u32[]{:S(2)}) copy-start(f32[256,32]{0,1:T(8,128)} %param.12) | copy-start | bytes 98308
  3.4 9.7 %copy-start.7 = (f32[256,32]{0,1:T(8,128)S(1)}, f32[256,32]{0,1:T(8,128)}, u32[]{:S(2)}) copy-start(f32[256,32]{0,1:T(8,128)} %param.13) | copy-start | bytes 98308
  3.4 9.7 %copy-start.8 = (f32[256,32]{0,1:T(8,128)S(1)}, f32[256,32]{0,1:T(8,128)}, u32[]{:S(2)}) copy-start(f32[256,32]{0,1:T(8,128)} %param.11) | copy-start | bytes 98308
  3.4 14.0 %copy-start.2 = (f32[1,256,512]{2,1,0:T(8,128)S(1)}, f32[1,256,512]{2,1,0:T(8,128)}, u32[]{:S(2)}) copy-start(f32[1,256,512]{2,1,0:T(8,128)} %param.10) | copy-start | bytes 1572868
  3.4 57.2 %all-to-all-start = ((bf16[8,128,1024]{2,1,0:T(8,128)(2,1)}), bf16[8,128,1024]{2,1,0:T(8,128)(2,1)S(1)}, u32[]{:S(2)}, u32[]{:S(2)}) async-start(bf16[8,128,1024]{2,1,0:T(8,128)(2,1)} %shard_map.102), calls=%async_computation | async-start | bytes 4194304 | tf_op jit(solution)/shard_map/all_to_all | solution.py:119
  13.1 19.3 %collective-permute-start.3 = (f32[32,256]{1,0:T(8,128)S(1)}, f32[32,256]{1,0:T(8,128)S(1)}, u32[]{:S(2)}, u32[]{:S(2)}) collective-permute-start(f32[32,256]{1,0:T(8,128)S(1)} %get-tuple-element.27), channel_id=1, source_target_pairs={{0,32},{32,0},{1,33},{33,1},{2,34},{34,2},{3,35},{35,3},{4,36},{36... | collective-permute-start | bytes 98312 | tf_op jit(solution)/shard_map/ppermute | solution.py:129
  17.4 32.8 %collective-permute-start = (bf16[256,512]{1,0:T(8,128)(2,1)S(1)}, bf16[256,512]{1,0:T(8,128)(2,1)S(1)}, u32[]{:S(2)}, u32[]{:S(2)}) collective-permute-start(bf16[256,512]{1,0:T(8,128)(2,1)S(1)} %bitcast_convert_fusion.refs_0_), channel_id=1, source_target_pairs={{0,1},{1,2},{2,3},{3,0},{4,5},{5,6},{6,7},{7,4},{8,9},{9,10},{10,1... | collective-permute-start | bytes 786440 | tf_op jit(solution)/shard_map/ppermute | solution.py:114
  21.9 38.7 %collective-permute-start.1 = (bf16[256,512]{1,0:T(8,128)(2,1)S(1)}, bf16[256,512]{1,0:T(8,128)(2,1)S(1)}, u32[]{:S(2)}, u32[]{:S(2)}) collective-permute-start(bf16[256,512]{1,0:T(8,128)(2,1)S(1)} %bitcast_convert_fusion.refs_0_), channel_id=1, source_target_pairs={{0,2},{1,3},{2,0},{3,1},{4,6},{5,7},{6,4},{7,5},{8,10},{9,11},{10,... | collective-permute-start | bytes 786440 | tf_op jit(solution)/shard_map/ppermute | solution.py:114
  28.8 31.8 %collective-permute-start.2 = (bf16[256,512]{1,0:T(8,128)(2,1)S(1)}, bf16[256,512]{1,0:T(8,128)(2,1)S(1)}, u32[]{:S(2)}, u32[]{:S(2)}) collective-permute-start(bf16[256,512]{1,0:T(8,128)(2,1)S(1)} %bitcast_convert_fusion.refs_0_), channel_id=1, source_target_pairs={{0,3},{1,0},{2,1},{3,2},{4,7},{5,4},{6,5},{7,6},{8,11},{9,8},{10,9... | collective-permute-start | bytes 786440 | tf_op jit(solution)/shard_map/ppermute | solution.py:114
  32.4 17.8 %collective-permute-start.4 = (f32[2,32,256]{2,1,0:T(8,128)S(1)}, f32[2,32,256]{2,1,0:T(8,128)S(1)}, u32[]{:S(2)}, u32[]{:S(2)}) collective-permute-start(f32[2,32,256]{2,1,0:T(8,128)S(1)} %bitcast_dynamic-update-slice_fusion.6), channel_id=1, source_target_pairs={{0,256},{256,0},{1,257},{257,1},{2,258},{258,2},{3,259},{259,3},{4... | collective-permute-start | bytes 196616 | tf_op jit(solution)/shard_map/ppermute | solution.py:129
  61.9 20.0 %copy-start.4 = (bf16[1,128,512]{2,1,0:T(8,128)(2,1)S(1)}, bf16[1,128,512]{2,1,0:T(8,128)(2,1)}, u32[]{:S(2)}) copy-start(bf16[1,128,512]{2,1,0:T(8,128)(2,1)} %param.8) | copy-start | bytes 393220
  62.0 20.0 %copy-start.5 = (f32[128]{0:T(128)S(1)}, f32[128]{0:T(128)}, u32[]{:S(2)}) copy-start(f32[128]{0:T(128)} %param.9) | copy-start | bytes 1540
  83.5 19.7 %all-to-all-start.2 = ((bf16[8,512,128]{2,1,0:T(8,128)(2,1)}), bf16[8,512,128]{2,1,0:T(8,128)(2,1)S(1)}, u32[]{:S(2)}, u32[]{:S(2)}) async-start(bf16[8,512,128]{2,1,0:T(8,128)(2,1)} %shard_map.104), calls=%async_computation.2 | async-start | bytes 2097152 | tf_op jit(solution)/shard_map/all_to_all | solution.py:119
  88.3 10.6 %collective-permute-start.5 = (f32[2,2,32,256]{3,2,1,0:T(8,128)S(1)}, f32[2,2,32,256]{3,2,1,0:T(8,128)S(1)}, u32[]{:S(2)}, u32[]{:S(2)}) collective-permute-start(f32[2,2,32,256]{3,2,1,0:T(8,128)S(1)} %bitcast_dynamic-update-slice_fusion.4), channel_id=1, source_target_pairs={{0,64},{64,128},{128,192},{192,0},{1,65},{65,129},{129,193},{193,1... | collective-permute-start | bytes 393224 | tf_op jit(solution)/shard_map/ppermute | solution.py:129
  91.5 7.6 %collective-permute-start.6 = (f32[2,2,32,256]{3,2,1,0:T(8,128)S(1)}, f32[2,2,32,256]{3,2,1,0:T(8,128)S(1)}, u32[]{:S(2)}, u32[]{:S(2)}) collective-permute-start(f32[2,2,32,256]{3,2,1,0:T(8,128)S(1)} %bitcast_dynamic-update-slice_fusion.4), channel_id=1, source_target_pairs={{0,128},{64,192},{128,0},{192,64},{1,129},{65,193},{129,1},{193,65... | collective-permute-start | bytes 393224 | tf_op jit(solution)/shard_map/ppermute | solution.py:129
  95.8 5.7 %collective-permute-start.7 = (f32[2,2,32,256]{3,2,1,0:T(8,128)S(1)}, f32[2,2,32,256]{3,2,1,0:T(8,128)S(1)}, u32[]{:S(2)}, u32[]{:S(2)}) collective-permute-start(f32[2,2,32,256]{3,2,1,0:T(8,128)S(1)} %bitcast_dynamic-update-slice_fusion.4), channel_id=1, source_target_pairs={{0,192},{64,0},{128,64},{192,128},{1,193},{65,1},{129,65},{193,129... | collective-permute-start | bytes 393224 | tf_op jit(solution)/shard_map/ppermute | solution.py:129
  101.6 0.8 copy-start
  104.9 47.9 %copy-start.3 = (f32[1,256,512]{2,1,0:T(8,128)S(1)}, f32[1,256,512]{2,1,0:T(8,128)}, u32[]{:S(2)}) copy-start(f32[1,256,512]{2,1,0:T(8,128)} %param.10) | copy-start | bytes 1572868
  135.9 31.5 %copy-start.1 = (f32[4,2,2,32,256]{4,3,2,1,0:T(8,128)S(1)}, f32[4,2,2,32,256]{4,3,2,1,0:T(8,128)}, u32[]{:S(2)}) copy-start(f32[4,2,2,32,256]{4,3,2,1,0:T(8,128)} %copy-done) | copy-start | bytes 1572868
  153.8 20.8 %all-to-all-start.5 = ((f16[16,32,256]{2,1,0:T(8,128)(2,1)}), f16[16,32,256]{2,1,0:T(8,128)(2,1)S(1)}, u32[]{:S(2)}, u32[]{:S(2)}) async-start(f16[16,32,256]{2,1,0:T(8,128)(2,1)} %bitcast.20), calls=%async_computation.5 | async-start | bytes 524288 | tf_op jit(solution)/shard_map/all_to_all | solution.py:299

commit v7 on v6

--- a/solution.py
+++ b/solution.py
@@ -65,28 +65,34 @@
 
 
 def split_kernel(core_ref, feats_ref, out_ref, held, sems, out_sems):
-    core = core_ref[0]
     width = feats_ref.shape[1] // (EIGHT * FOUR)
-    loads, stores = [], []
-    for p in range(EIGHT):
-        for q in range(FOUR):
-            block = jnp.where(core == 0, FOUR * p + q, EIGHT * q + p)
-            loads.append(
-                pltpu.make_async_copy(
-                    feats_ref.at[:, pl.ds(pl.multiple_of(block * width, width), width)],
-                    held.at[p, :, pl.ds(q * width, width)],
-                    sems.at[p, q],
-                )
-            )
-        stores.append(pltpu.make_async_copy(held.at[p], out_ref.at[p], out_sems.at[p]))
-    for load in loads:
-        load.start()
-    for p in range(EIGHT):
-        for load in loads[FOUR * p : FOUR * (p + 1)]:
-            load.wait()
-        stores[p].start()
-    for store in stores:
-        store.wait()
+
+    def load(first, size, p, q):
+        return pltpu.make_async_copy(
+            feats_ref.at[:, pl.ds(first * width, size * width)],
+            held.at[p, :, pl.ds(q * width, size * width)],
+            sems.at[p, q],
+        )
+
+    def move(loads):
+        stores = [pltpu.make_async_copy(held.at[p], out_ref.at[p], out_sems.at[p]) for p in range(EIGHT)]
+        for group in loads:
+            for copy in group:
+                copy.start()
+        for group, store in zip(loads, stores):
+            for copy in group:
+                copy.wait()
+            store.start()
+        for store in stores:
+            store.wait()
+
+    @pl.when(core_ref[0] == 0)
+    def _():
+        move([[load(FOUR * p, FOUR, p, 0)] for p in range(EIGHT)])
+
+    @pl.when(core_ref[0] != 0)
+    def _():
+        move([[load(EIGHT * q + p, 1, p, q) for q in range(FOUR)] for p in range(EIGHT)])
 
 
 def split_columns(core, feats):
@@ -238,12 +244,14 @@
 
 
 def blend_kernel(after_ref, new_ref, out_ref):
-    xs, y_los, cores, width, rows = new_ref.shape
+    cores, y_los, xs, width, _ = new_ref.shape
+    size = 2 * cores * width
     for y_lo in range(y_los):
-        for x in range(xs):
+        for x in range(0, xs, 2):
+            pieces = [new_ref[core, y_lo, x + i] for i in range(2) for core in range(cores)]
             first = (y_lo * xs + x) * cores * width
-            part = slice(first, first + cores * width)
-            new = new_ref[x, y_lo].reshape(cores * width, rows)
+            part = slice(first, first + size)
+            new = jnp.concatenate(pieces, axis=0)
             out_ref[:, part] = (blend_rate * new + (1.0 - blend_rate) * after_ref[part, :]).T
 
 
@@ -278,13 +286,13 @@
     global_t, momentum_t, late_t = global_weight.T, outer_momentum.T, late_delta.T
     next_momentum_t = keep_rate * momentum_t + late_t
     next_global_t = global_t - outer_rate * (late_t + keep_rate * next_momentum_t)
-    new_rows_t = gather_by_permutes(gather_by_permutes(next_global_t, "core"), "y_lo")
+    new_rows_t = gather_by_permutes(gather_by_permutes(next_global_t, "x"), "y_lo")
     owned, weight, new_rows_t = lax.optimization_barrier((owned, weight, new_rows_t))
     parts = project(q.reshape(1), owned, weight).reshape(EIGHT, tokens, columns)
     parts = exchange(parts, RINGS_OF_8)
     slopes = key_slopes(parts, key_cotangent[0], key_gain.reshape(1, HEAD), factor)
     slopes, new_rows_t = lax.optimization_barrier((slopes, new_rows_t))
-    new_rows_t = gather_by_permutes(new_rows_t, "x")
+    new_rows_t = gather_by_permutes(new_rows_t, "core")
     slopes = exchange(slopes, RINGS_OF_8)
     slopes, new_rows_t = lax.optimization_barrier((slopes, new_rows_t))
 

time: 176 us -> 175 us (level)
  starting transfers between devices: 61 us -> 68 us
  waiting for transfers between devices: 34.2 us -> 27.9 us
  blocking collectives: 67.3 us -> 65.1 us
    ppermute x5, waiting for transfers between devices: 17 us -> 9.06 us  [gather_by_permutes(): piece = lax.ppermute(x, axis, [(i, (i + step) % size) for i in range(size)])]
    ppermute x5, starting transfers between devices: 18 us -> 24.1 us  [gather_by_permutes(): piece = lax.ppermute(x, axis, [(i, (i + step) % size) for i in range(size)])]
    all_to_all x2, waiting for transfers between devices: 0.9 us -> 3.66 us  [exchange(): return lax.all_to_all(x, ALL, 0, 0, axis_index_groups=rings)]
    ppermute x3, starting transfers between devices: 15 us -> 17.1 us  [gather_rows(): out.append(lax.ppermute(x, ALL, pairs))]
  transfers between devices with their start and end apart: 11 -> 11, of which waited for: 5 -> 5; matrix products, arithmetic and copies ran while one was open for 0% -> 1% of each run, Pallas kernels for 1% -> 1%
where the time goes in v7:
time: 175 us
  starting transfers between devices  68 us (39%)
  blocking collectives  65.1 us (37%)
  waiting for transfers between devices  27.9 us (16%)
  Pallas kernels  8.39 us (5%)
  other arithmetic  2.14 us (1%)
  local copies, waits for them, and re-layouts  1.97 us (1%)
    all_to_all x2, blocking collectives, exchange(): return lax.all_to_all(x, ALL, 0, 0, axis_index_groups=rings)  48.9 us
    ppermute x5, starting transfers between devices, gather_by_permutes(): piece = lax.ppermute(x, axis, [(i, (i + step) % size) for i in range(size)])  24.1 us
    ppermute x3, starting transfers between devices, gather_rows(): out.append(lax.ppermute(x, ALL, pairs))  17.1 us
    all_to_all x1, blocking collectives, shards(): lax.all_to_all(squares_for_all(gradient_t, EIGHT * FOUR), FSDP, 0, 0)  16.2 us
    all_to_all x1, starting transfers between devices, shards(): lax.all_to_all(sent_rows.astype(jnp.float16), REPLICA, 0, 0)  13.6 us
    all_to_all x2, starting transfers between devices, exchange(): return lax.all_to_all(x, ALL, 0, 0, axis_index_groups=rings)  13.2 us
    ppermute x5, waiting for transfers between devices, gather_by_permutes(): piece = lax.ppermute(x, axis, [(i, (i + step) % size) for i in range(size)])  9.06 us
    ppermute x3, waiting for transfers between devices, gather_rows(): out.append(lax.ppermute(x, ALL, pairs))  9.03 us
  transfers between devices with their start and end apart: 11, of which 5 were waited for; matrix products, arithmetic and copies ran while one was open for 1% of the time, Pallas kernels for 1%

profile of v7, /device:TPU:1, one launch (start us, length us, event | category | flops | bytes accessed | tf_op | source)
XLA Modules:
  0.0 174.6 jit_solution(4654944760751961590)
XLA Ops:
  0.6 2.7 %shard_map.102 = bf16[8,128,1024]{2,1,0:T(8,128)(2,1)} custom-call(s32[1]{0:T(128)} %bitcast.core_ref, bf16[128,8192]{1,0:T(8,128)(2,1)} %bitcast.52), custom_call_target="tpu_custom_call" | custom-call | bytes 4194304 | tf_op jit(solution)/shard_map/pallas_call | solution.py:101
  3.4 9.6 %all-to-all-start = ((bf16[8,128,1024]{2,1,0:T(8,128)(2,1)}), bf16[8,128,1024]{2,1,0:T(8,128)(2,1)S(1)}, u32[]{:S(2)}, u32[]{:S(2)}) async-start(bf16[8,128,1024]{2,1,0:T(8,128)(2,1)} %shard_map.102), calls=%async_computation | async-start | bytes 4194304 | tf_op jit(solution)/shard_map/all_to_all | solution.py:125
  13.1 3.1 %collective-permute-start.3 = (f32[32,256]{1,0:T(8,128)S(1)}, f32[32,256]{1,0:T(8,128)S(1)}, u32[]{:S(2)}, u32[]{:S(2)}) collective-permute-start(f32[32,256]{1,0:T(8,128)S(1)} %get-tuple-element.27), channel_id=1, source_target_pairs={{0,64},{64,128},{128,192},{192,0},{1,65},{65,129},{129,193},{193,1... | collective-permute-start | bytes 98312 | tf_op jit(solution)/shard_map/ppermute | solution.py:135
  16.2 4.4 %collective-permute-start.4 = (f32[32,256]{1,0:T(8,128)S(1)}, f32[32,256]{1,0:T(8,128)S(1)}, u32[]{:S(2)}, u32[]{:S(2)}) collective-permute-start(f32[32,256]{1,0:T(8,128)S(1)} %get-tuple-element.27), channel_id=1, source_target_pairs={{0,128},{64,192},{128,0},{192,64},{1,129},{65,193},{129,1},{193,65... | collective-permute-start | bytes 98312 | tf_op jit(solution)/shard_map/ppermute | solution.py:135
  20.6 3.1 %collective-permute-start.5 = (f32[32,256]{1,0:T(8,128)S(1)}, f32[32,256]{1,0:T(8,128)S(1)}, u32[]{:S(2)}, u32[]{:S(2)}) collective-permute-start(f32[32,256]{1,0:T(8,128)S(1)} %get-tuple-element.27), channel_id=1, source_target_pairs={{0,192},{64,0},{128,64},{192,128},{1,193},{65,1},{129,65},{193,129... | collective-permute-start | bytes 98312 | tf_op jit(solution)/shard_map/ppermute | solution.py:135
  23.7 5.8 %collective-permute-start = (bf16[256,512]{1,0:T(8,128)(2,1)S(1)}, bf16[256,512]{1,0:T(8,128)(2,1)S(1)}, u32[]{:S(2)}, u32[]{:S(2)}) collective-permute-start(bf16[256,512]{1,0:T(8,128)(2,1)S(1)} %bitcast_convert_fusion.refs_0_), channel_id=1, source_target_pairs={{0,1},{1,2},{2,3},{3,0},{4,5},{5,6},{6,7},{7,4},{8,9},{9,10},{10,1... | collective-permute-start | bytes 786440 | tf_op jit(solution)/shard_map/ppermute | solution.py:120
  29.5 7.9 %collective-permute-start.1 = (bf16[256,512]{1,0:T(8,128)(2,1)S(1)}, bf16[256,512]{1,0:T(8,128)(2,1)S(1)}, u32[]{:S(2)}, u32[]{:S(2)}) collective-permute-start(bf16[256,512]{1,0:T(8,128)(2,1)S(1)} %bitcast_convert_fusion.refs_0_), channel_id=1, source_target_pairs={{0,2},{1,3},{2,0},{3,1},{4,6},{5,7},{6,4},{7,5},{8,10},{9,11},{10,... | collective-permute-start | bytes 786440 | tf_op jit(solution)/shard_map/ppermute | solution.py:120
  37.5 3.4 %collective-permute-start.2 = (bf16[256,512]{1,0:T(8,128)(2,1)S(1)}, bf16[256,512]{1,0:T(8,128)(2,1)S(1)}, u32[]{:S(2)}, u32[]{:S(2)}) collective-permute-start(bf16[256,512]{1,0:T(8,128)(2,1)S(1)} %bitcast_convert_fusion.refs_0_), channel_id=1, source_target_pairs={{0,3},{1,0},{2,1},{3,2},{4,7},{5,4},{6,5},{7,6},{8,11},{9,8},{10,9... | collective-permute-start | bytes 786440 | tf_op jit(solution)/shard_map/ppermute | solution.py:120
  41.0 2.3 %collective-permute-start.6 = (f32[4,32,256]{2,1,0:T(8,128)S(1)}, f32[4,32,256]{2,1,0:T(8,128)S(1)}, u32[]{:S(2)}, u32[]{:S(2)}) collective-permute-start(f32[4,32,256]{2,1,0:T(8,128)S(1)} %bitcast_dynamic-update-slice_fusion.4), channel_id=1, source_target_pairs={{0,256},{256,0},{1,257},{257,1},{2,258},{258,2},{3,259},{259,3},{4... | collective-permute-start | bytes 393224 | tf_op jit(solution)/shard_map/ppermute | solution.py:135
  43.4 7.9 %collective-permute-done.6 = f32[4,32,256]{2,1,0:T(8,128)S(1)} collective-permute-done((f32[4,32,256]{2,1,0:T(8,128)S(1)}, f32[4,32,256]{2,1,0:T(8,128)S(1)}, u32[]{:S(2)}, u32[]{:S(2)}) %collective-permute-start.6) | collective-permute-done | bytes 131104 | tf_op jit(solution)/shard_map/ppermute | solution.py:135
  51.3 9.0 %collective-permute-done.1.refs_2_ = bf16[256,512]{1,0:T(8,128)(2,1)S(1)} collective-permute-done((bf16[256,512]{1,0:T(8,128)(2,1)S(1)}, bf16[256,512]{1,0:T(8,128)(2,1)S(1)}, u32[]{:S(2)}, u32[]{:S(2)}) %collective-permute-start.1) | collective-permute-done | bytes 262176 | tf_op jit(solution)/shard_map/ppermute | solution.py:120
  60.3 1.3 shard_map.103
  61.7 23.3 %all_to_all.30.parts_ref = bf16[8,128,512]{2,1,0:T(8,128)(2,1)S(1)} all-to-all(bf16[8,128,512]{2,1,0:T(8,128)(2,1)S(1)} %bitcast.48), channel_id=1, replica_groups={{0,4,8,12,16,20,24,28},{1,5,9,13,17,21,25,29},{2,6,10,14,18,22,26,30},{..., dimensions={0} | all-to-all | bytes 2097152 | tf_op jit(solution)/shard_map/all_to_all | solution.py:125
  85.0 1.5 shard_map.104
  86.5 3.6 %all-to-all-start.2 = ((bf16[8,512,128]{2,1,0:T(8,128)(2,1)}), bf16[8,512,128]{2,1,0:T(8,128)(2,1)S(1)}, u32[]{:S(2)}, u32[]{:S(2)}) async-start(bf16[8,512,128]{2,1,0:T(8,128)(2,1)} %shard_map.104), calls=%async_computation.2 | async-start | bytes 2097152 | tf_op jit(solution)/shard_map/all_to_all | solution.py:125
  90.1 11.3 %collective-permute-start.7 = (f32[2,4,32,256]{3,2,1,0:T(8,128)S(1)}, f32[2,4,32,256]{3,2,1,0:T(8,128)}, u32[]{:S(2)}, u32[]{:S(2)}) collective-permute-start(f32[2,4,32,256]{3,2,1,0:T(8,128)S(1)} %bitcast_dynamic-update-slice_fusion.2), channel_id=1, source_target_pairs={{0,32},{32,0},{1,33},{33,1},{2,34},{34,2},{3,35},{35,3},{4,36},{36... | collective-permute-start | bytes 786440 | tf_op jit(solution)/shard_map/ppermute | solution.py:135
  101.5 1.2 collective-permute-done.7
  104.4 3.7 %all-to-all-done.2.slopes_ref = bf16[8,512,128]{2,1,0:T(8,128)(2,1)S(1)} async-done(((bf16[8,512,128]{2,1,0:T(8,128)(2,1)}), bf16[8,512,128]{2,1,0:T(8,128)(2,1)S(1)}, u32[]{:S(2)}, u32[]{:S(2)}) %all-to-all-start.2) | async-done | bytes 1048608 | tf_op jit(solution)/shard_map/all_to_all | solution.py:125
  108.1 1.4 shard_map.105
  109.7 25.6 %all_to_all.31 = f16[4,528,256]{2,1,0:T(8,128)(2,1)S(1)} all-to-all(f16[4,528,256]{2,1,0:T(8,128)(2,1)S(1)} %convert_element_type.23), channel_id=1, replica_groups={{0,1,2,3},{4,5,6,7},{8,9,10,11},{12,13,14,15},{16,17,18,19},{20,21,22,2..., dimensions={0} | all-to-all | bytes 2162688 | tf_op jit(solution)/shard_map/all_to_all | solution.py:125
  135.9 16.2 %all_to_all.32.shares_ref = f32[32,8,128]{2,1,0:T(8,128)S(1)} all-to-all(f32[32,8,128]{2,1,0:T(8,128)S(1)} %shard_map.106), channel_id=1, replica_groups=mesh['y_lo'=2,'x'=4,'core'=2,'z'=8,'y_hi'=4] {'z','y_hi'}, dimensions={0} | all-to-all | bytes 262144 | tf_op jit(solution)/shard_map/all_to_all | solution.py:303
  153.0 13.6 %all-to-all-start.5 = ((f16[16,32,256]{2,1,0:T(8,128)(2,1)}), f16[16,32,256]{2,1,0:T(8,128)(2,1)S(1)}, u32[]{:S(2)}, u32[]{:S(2)}) async-start(f16[16,32,256]{2,1,0:T(8,128)(2,1)} %bitcast.20), calls=%async_computation.5 | async-start | bytes 524288 | tf_op jit(solution)/shard_map/all_to_all | solution.py:307
  166.7 1.0 shard_map.108
  167.7 6.2 %all-to-all-done.5 = f16[16,32,256]{2,1,0:T(8,128)(2,1)S(1)} async-done(((f16[16,32,256]{2,1,0:T(8,128)(2,1)}), f16[16,32,256]{2,1,0:T(8,128)(2,1)S(1)}, u32[]{:S(2)}, u32[]{:S(2)}) %all-to-all-start.5) | async-done | bytes 262176 | tf_op jit(solution)/shard_map/all_to_all | solution.py:307
  (50 shorter events, 4.5 us)
Async XLA Ops:
  3.4 9.7 %copy-start.6 = (f32[256,32]{0,1:T(8,128)S(1)}, f32[256,32]{0,1:T(8,128)}, u32[]{:S(2)}) copy-start(f32[256,32]{0,1:T(8,128)} %param.12) | copy-start | bytes 98308
  3.4 9.7 %copy-start.8 = (f32[256,32]{0,1:T(8,128)S(1)}, f32[256,32]{0,1:T(8,128)}, u32[]{:S(2)}) copy-start(f32[256,32]{0,1:T(8,128)} %param.13) | copy-start | bytes 98308
  3.4 9.7 %copy-start.10 = (f32[256,32]{0,1:T(8,128)S(1)}, f32[256,32]{0,1:T(8,128)}, u32[]{:S(2)}) copy-start(f32[256,32]{0,1:T(8,128)} %param.11) | copy-start | bytes 98308
  3.4 20.2 %copy-start.2 = (f32[1,256,512]{2,1,0:T(8,128)S(1)}, f32[1,256,512]{2,1,0:T(8,128)}, u32[]{:S(2)}) copy-start(f32[1,256,512]{2,1,0:T(8,128)} %param.10) | copy-start | bytes 1572868
  3.4 56.9 %all-to-all-start = ((bf16[8,128,1024]{2,1,0:T(8,128)(2,1)}), bf16[8,128,1024]{2,1,0:T(8,128)(2,1)S(1)}, u32[]{:S(2)}, u32[]{:S(2)}) async-start(bf16[8,128,1024]{2,1,0:T(8,128)(2,1)} %shard_map.102), calls=%async_computation | async-start | bytes 4194304 | tf_op jit(solution)/shard_map/all_to_all | solution.py:125
  13.1 24.4 %collective-permute-start.3 = (f32[32,256]{1,0:T(8,128)S(1)}, f32[32,256]{1,0:T(8,128)S(1)}, u32[]{:S(2)}, u32[]{:S(2)}) collective-permute-start(f32[32,256]{1,0:T(8,128)S(1)} %get-tuple-element.27), channel_id=1, source_target_pairs={{0,64},{64,128},{128,192},{192,0},{1,65},{65,129},{129,193},{193,1... | collective-permute-start | bytes 98312 | tf_op jit(solution)/shard_map/ppermute | solution.py:135
  16.2 24.7 %collective-permute-start.4 = (f32[32,256]{1,0:T(8,128)S(1)}, f32[32,256]{1,0:T(8,128)S(1)}, u32[]{:S(2)}, u32[]{:S(2)}) collective-permute-start(f32[32,256]{1,0:T(8,128)S(1)} %get-tuple-element.27), channel_id=1, source_target_pairs={{0,128},{64,192},{128,0},{192,64},{1,129},{65,193},{129,1},{193,65... | collective-permute-start | bytes 98312 | tf_op jit(solution)/shard_map/ppermute | solution.py:135
  20.6 20.4 %collective-permute-start.5 = (f32[32,256]{1,0:T(8,128)S(1)}, f32[32,256]{1,0:T(8,128)S(1)}, u32[]{:S(2)}, u32[]{:S(2)}) collective-permute-start(f32[32,256]{1,0:T(8,128)S(1)} %get-tuple-element.27), channel_id=1, source_target_pairs={{0,192},{64,0},{128,64},{192,128},{1,193},{65,1},{129,65},{193,129... | collective-permute-start | bytes 98312 | tf_op jit(solution)/shard_map/ppermute | solution.py:135
  23.7 27.6 %collective-permute-start = (bf16[256,512]{1,0:T(8,128)(2,1)S(1)}, bf16[256,512]{1,0:T(8,128)(2,1)S(1)}, u32[]{:S(2)}, u32[]{:S(2)}) collective-permute-start(bf16[256,512]{1,0:T(8,128)(2,1)S(1)} %bitcast_convert_fusion.refs_0_), channel_id=1, source_target_pairs={{0,1},{1,2},{2,3},{3,0},{4,5},{5,6},{6,7},{7,4},{8,9},{9,10},{10,1... | collective-permute-start | bytes 786440 | tf_op jit(solution)/shard_map/ppermute | solution.py:120
  29.5 30.8 %collective-permute-start.1 = (bf16[256,512]{1,0:T(8,128)(2,1)S(1)}, bf16[256,512]{1,0:T(8,128)(2,1)S(1)}, u32[]{:S(2)}, u32[]{:S(2)}) collective-permute-start(bf16[256,512]{1,0:T(8,128)(2,1)S(1)} %bitcast_convert_fusion.refs_0_), channel_id=1, source_target_pairs={{0,2},{1,3},{2,0},{3,1},{4,6},{5,7},{6,4},{7,5},{8,10},{9,11},{10,... | collective-permute-start | bytes 786440 | tf_op jit(solution)/shard_map/ppermute | solution.py:120
  37.5 22.8 %collective-permute-start.2 = (bf16[256,512]{1,0:T(8,128)(2,1)S(1)}, bf16[256,512]{1,0:T(8,128)(2,1)S(1)}, u32[]{:S(2)}, u32[]{:S(2)}) collective-permute-start(bf16[256,512]{1,0:T(8,128)(2,1)S(1)} %bitcast_convert_fusion.refs_0_), channel_id=1, source_target_pairs={{0,3},{1,0},{2,1},{3,2},{4,7},{5,4},{6,5},{7,6},{8,11},{9,8},{10,9... | collective-permute-start | bytes 786440 | tf_op jit(solution)/shard_map/ppermute | solution.py:120
  41.0 10.2 %collective-permute-start.6 = (f32[4,32,256]{2,1,0:T(8,128)S(1)}, f32[4,32,256]{2,1,0:T(8,128)S(1)}, u32[]{:S(2)}, u32[]{:S(2)}) collective-permute-start(f32[4,32,256]{2,1,0:T(8,128)S(1)} %bitcast_dynamic-update-slice_fusion.4), channel_id=1, source_target_pairs={{0,256},{256,0},{1,257},{257,1},{2,258},{258,2},{3,259},{259,3},{4... | collective-permute-start | bytes 393224 | tf_op jit(solution)/shard_map/ppermute | solution.py:135
  61.6 23.3 %copy-start.4 = (bf16[1,128,512]{2,1,0:T(8,128)(2,1)S(1)}, bf16[1,128,512]{2,1,0:T(8,128)(2,1)}, u32[]{:S(2)}) copy-start(bf16[1,128,512]{2,1,0:T(8,128)(2,1)} %param.8) | copy-start | bytes 393220
  61.7 23.3 %copy-start.5 = (f32[128]{0:T(128)S(1)}, f32[128]{0:T(128)}, u32[]{:S(2)}) copy-start(f32[128]{0:T(128)} %param.9) | copy-start | bytes 1540
  86.5 21.5 %all-to-all-start.2 = ((bf16[8,512,128]{2,1,0:T(8,128)(2,1)}), bf16[8,512,128]{2,1,0:T(8,128)(2,1)S(1)}, u32[]{:S(2)}, u32[]{:S(2)}) async-start(bf16[8,512,128]{2,1,0:T(8,128)(2,1)} %shard_map.104), calls=%async_computation.2 | async-start | bytes 2097152 | tf_op jit(solution)/shard_map/all_to_all | solution.py:125
  90.1 12.5 %collective-permute-start.7 = (f32[2,4,32,256]{3,2,1,0:T(8,128)S(1)}, f32[2,4,32,256]{3,2,1,0:T(8,128)}, u32[]{:S(2)}, u32[]{:S(2)}) collective-permute-start(f32[2,4,32,256]{3,2,1,0:T(8,128)S(1)} %bitcast_dynamic-update-slice_fusion.2), channel_id=1, source_target_pairs={{0,32},{32,0},{1,33},{33,1},{2,34},{34,2},{3,35},{35,3},{4,36},{36... | collective-permute-start | bytes 786440 | tf_op jit(solution)/shard_map/ppermute | solution.py:135
  103.6 0.8 copy-start
  109.7 42.4 %copy-start.3 = (f32[1,256,512]{2,1,0:T(8,128)S(1)}, f32[1,256,512]{2,1,0:T(8,128)}, u32[]{:S(2)}) copy-start(f32[1,256,512]{2,1,0:T(8,128)} %param.10) | copy-start | bytes 1572868
  135.7 30.9 %copy-start.1 = (f32[2,2,4,32,256]{4,3,2,1,0:T(8,128)S(1)}, f32[2,2,4,32,256]{4,3,2,1,0:T(8,128)}, u32[]{:S(2)}) copy-start(f32[2,2,4,32,256]{4,3,2,1,0:T(8,128)} %copy-done) | copy-start | bytes 1572868
  152.1 21.8 %copy-start.7 = (f32[256,32]{0,1:T(8,128)S(1)}, f32[256,32]{0,1:T(8,128)}, u32[]{:S(2)}) copy-start(f32[256,32]{0,1:T(8,128)} %param.12) | copy-start | bytes 98308
  152.1 21.8 %copy-start.9 = (f32[256,32]{0,1:T(8,128)S(1)}, f32[256,32]{0,1:T(8,128)}, u32[]{:S(2)}) copy-start(f32[256,32]{0,1:T(8,128)} %param.13) | copy-start | bytes 98308
  152.1 21.8 %copy-start.11 = (f32[256,32]{0,1:T(8,128)S(1)}, f32[256,32]{0,1:T(8,128)}, u32[]{:S(2)}) copy-start(f32[256,32]{0,1:T(8,128)} %param.11) | copy-start | bytes 98308
  153.0 20.8 %all-to-all-start.5 = ((f16[16,32,256]{2,1,0:T(8,128)(2,1)}), f16[16,32,256]{2,1,0:T(8,128)(2,1)S(1)}, u32[]{:S(2)}, u32[]{:S(2)}) async-start(f16[16,32,256]{2,1,0:T(8,128)(2,1)} %bitcast.20), calls=%async_computation.5 | async-start | bytes 524288 | tf_op jit(solution)/shard_map/all_to_all | solution.py:307

commit v8 on v7

--- a/solution.py
+++ b/solution.py
@@ -286,7 +286,8 @@
     global_t, momentum_t, late_t = global_weight.T, outer_momentum.T, late_delta.T
     next_momentum_t = keep_rate * momentum_t + late_t
     next_global_t = global_t - outer_rate * (late_t + keep_rate * next_momentum_t)
-    new_rows_t = gather_by_permutes(gather_by_permutes(next_global_t, "x"), "y_lo")
+    new_rows_t = next_global_t.astype(jnp.float16)
+    new_rows_t = gather_by_permutes(gather_by_permutes(new_rows_t, "x"), "y_lo")
     owned, weight, new_rows_t = lax.optimization_barrier((owned, weight, new_rows_t))
     parts = project(q.reshape(1), owned, weight).reshape(EIGHT, tokens, columns)
     parts = exchange(parts, RINGS_OF_8)
@@ -306,7 +307,7 @@
     sent_rows = after_step_t.reshape(replicas, columns // replicas, rows)
     received = lax.all_to_all(sent_rows.astype(jnp.float16), REPLICA, 0, 0).astype(jnp.float32)
     outer_delta_t = global_t - jnp.sum(received, axis=0) / replicas
-    next_local = blend(after_step_t, new_rows_t)
+    next_local = blend(after_step_t, new_rows_t.astype(jnp.float32))
     return (next_local[None], next_global_t.T, next_momentum_t.T, outer_delta_t.T)
 
 

time: 175 us -> 175 us (level)
  waiting for transfers between devices: 27.9 us -> 29.8 us
  local copies, waits for them, and re-layouts: 1.97 us -> 0.22 us
    all_to_all x2, waiting for transfers between devices: 3.66 us -> 5.86 us  [exchange(): return lax.all_to_all(x, ALL, 0, 0, axis_index_groups=rings)]
    ppermute x5, waiting for transfers between devices: 9.06 us -> 7.19 us  [gather_by_permutes(): piece = lax.ppermute(x, axis, [(i, (i + step) % size) for i in range(size)])]
  transfers between devices with their start and end apart: 11 -> 11, of which waited for: 5 -> 6; matrix products, arithmetic and copies ran while one was open for 1% -> 0% of each run, Pallas kernels for 1% -> 1%
where the time goes in v8:
time: 175 us
  starting transfers between devices  68 us (39%)
  blocking collectives  64.9 us (37%)
  waiting for transfers between devices  29.8 us (17%)
  Pallas kernels  8.41 us (5%)
  other arithmetic  2.17 us (1%)
    all_to_all x2, blocking collectives, exchange(): return lax.all_to_all(x, ALL, 0, 0, axis_index_groups=rings)  48.6 us
    ppermute x5, starting transfers between devices, gather_by_permutes(): piece = lax.ppermute(x, axis, [(i, (i + step) % size) for i in range(size)])  24.1 us
    ppermute x3, starting transfers between devices, gather_rows(): out.append(lax.ppermute(x, ALL, pairs))  17.1 us
    all_to_all x1, blocking collectives, shards(): lax.all_to_all(squares_for_all(gradient_t, EIGHT * FOUR), FSDP, 0, 0)  16.3 us
    all_to_all x1, starting transfers between devices, shards(): lax.all_to_all(sent_rows.astype(jnp.float16), REPLICA, 0, 0)  13.7 us
    all_to_all x2, starting transfers between devices, exchange(): return lax.all_to_all(x, ALL, 0, 0, axis_index_groups=rings)  13.2 us
    ppermute x3, waiting for transfers between devices, gather_rows(): out.append(lax.ppermute(x, ALL, pairs))  10.6 us
    ppermute x5, waiting for transfers between devices, gather_by_permutes(): piece = lax.ppermute(x, axis, [(i, (i + step) % size) for i in range(size)])  7.19 us
  transfers between devices with their start and end apart: 11, of which 6 were waited for; matrix products, arithmetic and copies ran while one was open for 0% of the time, Pallas kernels for 1%

profile of v8, /device:TPU:1, one launch (start us, length us, event | category | flops | bytes accessed | tf_op | source)
XLA Modules:
  0.0 174.6 jit_solution(901109960351544340)
XLA Ops:
  0.6 2.7 %shard_map.102 = bf16[8,128,1024]{2,1,0:T(8,128)(2,1)} custom-call(s32[1]{0:T(128)} %bitcast.core_ref, bf16[128,8192]{1,0:T(8,128)(2,1)} %bitcast.54), custom_call_target="tpu_custom_call" | custom-call | bytes 4194304 | tf_op jit(solution)/shard_map/pallas_call | solution.py:101
  3.4 9.6 %all-to-all-start = ((bf16[8,128,1024]{2,1,0:T(8,128)(2,1)}), bf16[8,128,1024]{2,1,0:T(8,128)(2,1)S(1)}, u32[]{:S(2)}, u32[]{:S(2)}) async-start(bf16[8,128,1024]{2,1,0:T(8,128)(2,1)} %shard_map.102), calls=%async_computation | async-start | bytes 4194304 | tf_op jit(solution)/shard_map/all_to_all | solution.py:125
  13.1 3.1 %collective-permute-start.3 = (f16[32,256]{1,0:T(8,128)(2,1)S(1)}, f16[32,256]{1,0:T(8,128)(2,1)S(1)}, u32[]{:S(2)}, u32[]{:S(2)}) collective-permute-start(f16[32,256]{1,0:T(8,128)(2,1)S(1)} %get-tuple-element.27), channel_id=1, source_target_pairs={{0,64},{64,128},{128,192},{192,0},{1,65},{65,129},{129,193},{193,1... | collective-permute-start | bytes 49160 | tf_op jit(solution)/shard_map/ppermute | solution.py:135
  16.2 4.4 %collective-permute-start.4 = (f16[32,256]{1,0:T(8,128)(2,1)S(1)}, f16[32,256]{1,0:T(8,128)(2,1)S(1)}, u32[]{:S(2)}, u32[]{:S(2)}) collective-permute-start(f16[32,256]{1,0:T(8,128)(2,1)S(1)} %get-tuple-element.27), channel_id=1, source_target_pairs={{0,128},{64,192},{128,0},{192,64},{1,129},{65,193},{129,1},{193,65... | collective-permute-start | bytes 49160 | tf_op jit(solution)/shard_map/ppermute | solution.py:135
  20.6 3.1 %collective-permute-start.5 = (f16[32,256]{1,0:T(8,128)(2,1)S(1)}, f16[32,256]{1,0:T(8,128)(2,1)S(1)}, u32[]{:S(2)}, u32[]{:S(2)}) collective-permute-start(f16[32,256]{1,0:T(8,128)(2,1)S(1)} %get-tuple-element.27), channel_id=1, source_target_pairs={{0,192},{64,0},{128,64},{192,128},{1,193},{65,1},{129,65},{193,129... | collective-permute-start | bytes 49160 | tf_op jit(solution)/shard_map/ppermute | solution.py:135
  23.7 5.8 %collective-permute-start = (bf16[256,512]{1,0:T(8,128)(2,1)S(1)}, bf16[256,512]{1,0:T(8,128)(2,1)S(1)}, u32[]{:S(2)}, u32[]{:S(2)}) collective-permute-start(bf16[256,512]{1,0:T(8,128)(2,1)S(1)} %bitcast_convert_fusion.refs_0_), channel_id=1, source_target_pairs={{0,1},{1,2},{2,3},{3,0},{4,5},{5,6},{6,7},{7,4},{8,9},{9,10},{10,1... | collective-permute-start | bytes 786440 | tf_op jit(solution)/shard_map/ppermute | solution.py:120
  29.5 7.9 %collective-permute-start.1 = (bf16[256,512]{1,0:T(8,128)(2,1)S(1)}, bf16[256,512]{1,0:T(8,128)(2,1)S(1)}, u32[]{:S(2)}, u32[]{:S(2)}) collective-permute-start(bf16[256,512]{1,0:T(8,128)(2,1)S(1)} %bitcast_convert_fusion.refs_0_), channel_id=1, source_target_pairs={{0,2},{1,3},{2,0},{3,1},{4,6},{5,7},{6,4},{7,5},{8,10},{9,11},{10,... | collective-permute-start | bytes 786440 | tf_op jit(solution)/shard_map/ppermute | solution.py:120
  37.5 3.4 %collective-permute-start.2 = (bf16[256,512]{1,0:T(8,128)(2,1)S(1)}, bf16[256,512]{1,0:T(8,128)(2,1)S(1)}, u32[]{:S(2)}, u32[]{:S(2)}) collective-permute-start(bf16[256,512]{1,0:T(8,128)(2,1)S(1)} %bitcast_convert_fusion.refs_0_), channel_id=1, source_target_pairs={{0,3},{1,0},{2,1},{3,2},{4,7},{5,4},{6,5},{7,6},{8,11},{9,8},{10,9... | collective-permute-start | bytes 786440 | tf_op jit(solution)/shard_map/ppermute | solution.py:120
  41.0 2.3 %collective-permute-start.6 = (f16[4,32,256]{2,1,0:T(8,128)(2,1)S(1)}, f16[4,32,256]{2,1,0:T(8,128)(2,1)S(1)}, u32[]{:S(2)}, u32[]{:S(2)}) collective-permute-start(f16[4,32,256]{2,1,0:T(8,128)(2,1)S(1)} %bitcast_dynamic-update-slice_fusion.4), channel_id=1, source_target_pairs={{0,256},{256,0},{1,257},{257,1},{2,258},{258,2},{3,259},{259,3},{4... | collective-permute-start | bytes 196616 | tf_op jit(solution)/shard_map/ppermute | solution.py:135
  43.4 6.3 %collective-permute-done.6 = f16[4,32,256]{2,1,0:T(8,128)(2,1)S(1)} collective-permute-done((f16[4,32,256]{2,1,0:T(8,128)(2,1)S(1)}, f16[4,32,256]{2,1,0:T(8,128)(2,1)S(1)}, u32[]{:S(2)}, u32[]{:S(2)}) %collective-permute-start.6) | collective-permute-done | bytes 65568 | tf_op jit(solution)/shard_map/ppermute | solution.py:135
  50.0 10.3 %collective-permute-done.1.refs_2_ = bf16[256,512]{1,0:T(8,128)(2,1)S(1)} collective-permute-done((bf16[256,512]{1,0:T(8,128)(2,1)S(1)}, bf16[256,512]{1,0:T(8,128)(2,1)S(1)}, u32[]{:S(2)}, u32[]{:S(2)}) %collective-permute-start.1) | collective-permute-done | bytes 262176 | tf_op jit(solution)/shard_map/ppermute | solution.py:120
  60.3 1.3 shard_map.103
  61.7 23.4 %all_to_all.30.parts_ref = bf16[8,128,512]{2,1,0:T(8,128)(2,1)S(1)} all-to-all(bf16[8,128,512]{2,1,0:T(8,128)(2,1)S(1)} %bitcast.50), channel_id=1, replica_groups={{0,4,8,12,16,20,24,28},{1,5,9,13,17,21,25,29},{2,6,10,14,18,22,26,30},{..., dimensions={0} | all-to-all | bytes 2097152 | tf_op jit(solution)/shard_map/all_to_all | solution.py:125
  85.0 1.6 shard_map.104
  86.6 3.6 %all-to-all-start.2 = ((bf16[8,512,128]{2,1,0:T(8,128)(2,1)}), bf16[8,512,128]{2,1,0:T(8,128)(2,1)S(1)}, u32[]{:S(2)}, u32[]{:S(2)}) async-start(bf16[8,512,128]{2,1,0:T(8,128)(2,1)} %shard_map.104), calls=%async_computation.2 | async-start | bytes 2097152 | tf_op jit(solution)/shard_map/all_to_all | solution.py:125
  90.2 11.2 %collective-permute-start.7 = (f16[2,4,32,256]{3,2,1,0:T(8,128)(2,1)S(1)}, f16[2,4,32,256]{3,2,1,0:T(8,128)(2,1)S(1)}, u32[]{:S(2)}, u32[]{:S(2)}) collective-permute-start(f16[2,4,32,256]{3,2,1,0:T(8,128)(2,1)S(1)} %bitcast_dynamic-update-slice_fusion.2), channel_id=1, source_target_pairs={{0,32},{32,0},{1,33},{33,1},{2,34},{34,2},{3,35},{35,3},{4,36},{36... | collective-permute-start | bytes 393224 | tf_op jit(solution)/shard_map/ppermute | solution.py:135
  101.5 0.9 collective-permute-done.7
  102.4 5.9 %all-to-all-done.2.slopes_ref = bf16[8,512,128]{2,1,0:T(8,128)(2,1)S(1)} async-done(((bf16[8,512,128]{2,1,0:T(8,128)(2,1)}), bf16[8,512,128]{2,1,0:T(8,128)(2,1)S(1)}, u32[]{:S(2)}, u32[]{:S(2)}) %all-to-all-start.2) | async-done | bytes 1048608 | tf_op jit(solution)/shard_map/all_to_all | solution.py:125
  108.3 1.4 shard_map.105
  109.9 25.3 %all_to_all.31 = f16[4,528,256]{2,1,0:T(8,128)(2,1)S(1)} all-to-all(f16[4,528,256]{2,1,0:T(8,128)(2,1)S(1)} %convert_element_type.30), channel_id=1, replica_groups={{0,1,2,3},{4,5,6,7},{8,9,10,11},{12,13,14,15},{16,17,18,19},{20,21,22,2..., dimensions={0} | all-to-all | bytes 2162688 | tf_op jit(solution)/shard_map/all_to_all | solution.py:125
  135.8 16.3 %all_to_all.32.shares_ref = f32[32,8,128]{2,1,0:T(8,128)S(1)} all-to-all(f32[32,8,128]{2,1,0:T(8,128)S(1)} %shard_map.106), channel_id=1, replica_groups=mesh['y_lo'=2,'x'=4,'core'=2,'z'=8,'y_hi'=4] {'z','y_hi'}, dimensions={0} | all-to-all | bytes 262144 | tf_op jit(solution)/shard_map/all_to_all | solution.py:304
  153.0 13.7 %all-to-all-start.5 = ((f16[16,32,256]{2,1,0:T(8,128)(2,1)}), f16[16,32,256]{2,1,0:T(8,128)(2,1)S(1)}, u32[]{:S(2)}, u32[]{:S(2)}) async-start(f16[16,32,256]{2,1,0:T(8,128)(2,1)} %bitcast.20), calls=%async_computation.5 | async-start | bytes 524288 | tf_op jit(solution)/shard_map/all_to_all | solution.py:308
  166.7 1.0 shard_map.108
  167.7 6.1 %all-to-all-done.5 = f16[16,32,256]{2,1,0:T(8,128)(2,1)S(1)} async-done(((f16[16,32,256]{2,1,0:T(8,128)(2,1)}), f16[16,32,256]{2,1,0:T(8,128)(2,1)S(1)}, u32[]{:S(2)}, u32[]{:S(2)}) %all-to-all-start.5) | async-done | bytes 262176 | tf_op jit(solution)/shard_map/all_to_all | solution.py:308
  (47 shorter events, 3.1 us)
Async XLA Ops:
  3.4 9.7 %copy-start.4 = (f32[256,32]{0,1:T(8,128)S(1)}, f32[256,32]{0,1:T(8,128)}, u32[]{:S(2)}) copy-start(f32[256,32]{0,1:T(8,128)} %param.12) | copy-start | bytes 98308
  3.4 9.7 %copy-start.6 = (f32[256,32]{0,1:T(8,128)S(1)}, f32[256,32]{0,1:T(8,128)}, u32[]{:S(2)}) copy-start(f32[256,32]{0,1:T(8,128)} %param.13) | copy-start | bytes 98308
  3.4 9.7 %copy-start.8 = (f32[256,32]{0,1:T(8,128)S(1)}, f32[256,32]{0,1:T(8,128)}, u32[]{:S(2)}) copy-start(f32[256,32]{0,1:T(8,128)} %param.11) | copy-start | bytes 98308
  3.4 20.2 %copy-start = (f32[1,256,512]{2,1,0:T(8,128)S(1)}, f32[1,256,512]{2,1,0:T(8,128)}, u32[]{:S(2)}) copy-start(f32[1,256,512]{2,1,0:T(8,128)} %param.10) | copy-start | bytes 1572868
  3.4 56.9 %all-to-all-start = ((bf16[8,128,1024]{2,1,0:T(8,128)(2,1)}), bf16[8,128,1024]{2,1,0:T(8,128)(2,1)S(1)}, u32[]{:S(2)}, u32[]{:S(2)}) async-start(bf16[8,128,1024]{2,1,0:T(8,128)(2,1)} %shard_map.102), calls=%async_computation | async-start | bytes 4194304 | tf_op jit(solution)/shard_map/all_to_all | solution.py:125
  13.1 24.4 %collective-permute-start.3 = (f16[32,256]{1,0:T(8,128)(2,1)S(1)}, f16[32,256]{1,0:T(8,128)(2,1)S(1)}, u32[]{:S(2)}, u32[]{:S(2)}) collective-permute-start(f16[32,256]{1,0:T(8,128)(2,1)S(1)} %get-tuple-element.27), channel_id=1, source_target_pairs={{0,64},{64,128},{128,192},{192,0},{1,65},{65,129},{129,193},{193,1... | collective-permute-start | bytes 49160 | tf_op jit(solution)/shard_map/ppermute | solution.py:135
  16.2 24.7 %collective-permute-start.4 = (f16[32,256]{1,0:T(8,128)(2,1)S(1)}, f16[32,256]{1,0:T(8,128)(2,1)S(1)}, u32[]{:S(2)}, u32[]{:S(2)}) collective-permute-start(f16[32,256]{1,0:T(8,128)(2,1)S(1)} %get-tuple-element.27), channel_id=1, source_target_pairs={{0,128},{64,192},{128,0},{192,64},{1,129},{65,193},{129,1},{193,65... | collective-permute-start | bytes 49160 | tf_op jit(solution)/shard_map/ppermute | solution.py:135
  20.6 20.4 %collective-permute-start.5 = (f16[32,256]{1,0:T(8,128)(2,1)S(1)}, f16[32,256]{1,0:T(8,128)(2,1)S(1)}, u32[]{:S(2)}, u32[]{:S(2)}) collective-permute-start(f16[32,256]{1,0:T(8,128)(2,1)S(1)} %get-tuple-element.27), channel_id=1, source_target_pairs={{0,192},{64,0},{128,64},{192,128},{1,193},{65,1},{129,65},{193,129... | collective-permute-start | bytes 49160 | tf_op jit(solution)/shard_map/ppermute | solution.py:135
  23.7 26.3 %collective-permute-start = (bf16[256,512]{1,0:T(8,128)(2,1)S(1)}, bf16[256,512]{1,0:T(8,128)(2,1)S(1)}, u32[]{:S(2)}, u32[]{:S(2)}) collective-permute-start(bf16[256,512]{1,0:T(8,128)(2,1)S(1)} %bitcast_convert_fusion.refs_0_), channel_id=1, source_target_pairs={{0,1},{1,2},{2,3},{3,0},{4,5},{5,6},{6,7},{7,4},{8,9},{9,10},{10,1... | collective-permute-start | bytes 786440 | tf_op jit(solution)/shard_map/ppermute | solution.py:120
  29.5 30.7 %collective-permute-start.1 = (bf16[256,512]{1,0:T(8,128)(2,1)S(1)}, bf16[256,512]{1,0:T(8,128)(2,1)S(1)}, u32[]{:S(2)}, u32[]{:S(2)}) collective-permute-start(bf16[256,512]{1,0:T(8,128)(2,1)S(1)} %bitcast_convert_fusion.refs_0_), channel_id=1, source_target_pairs={{0,2},{1,3},{2,0},{3,1},{4,6},{5,7},{6,4},{7,5},{8,10},{9,11},{10,... | collective-permute-start | bytes 786440 | tf_op jit(solution)/shard_map/ppermute | solution.py:120
  37.5 22.7 %collective-permute-start.2 = (bf16[256,512]{1,0:T(8,128)(2,1)S(1)}, bf16[256,512]{1,0:T(8,128)(2,1)S(1)}, u32[]{:S(2)}, u32[]{:S(2)}) collective-permute-start(bf16[256,512]{1,0:T(8,128)(2,1)S(1)} %bitcast_convert_fusion.refs_0_), channel_id=1, source_target_pairs={{0,3},{1,0},{2,1},{3,2},{4,7},{5,4},{6,5},{7,6},{8,11},{9,8},{10,9... | collective-permute-start | bytes 786440 | tf_op jit(solution)/shard_map/ppermute | solution.py:120
  41.0 8.6 %collective-permute-start.6 = (f16[4,32,256]{2,1,0:T(8,128)(2,1)S(1)}, f16[4,32,256]{2,1,0:T(8,128)(2,1)S(1)}, u32[]{:S(2)}, u32[]{:S(2)}) collective-permute-start(f16[4,32,256]{2,1,0:T(8,128)(2,1)S(1)} %bitcast_dynamic-update-slice_fusion.4), channel_id=1, source_target_pairs={{0,256},{256,0},{1,257},{257,1},{2,258},{258,2},{3,259},{259,3},{4... | collective-permute-start | bytes 196616 | tf_op jit(solution)/shard_map/ppermute | solution.py:135
  61.6 23.4 %copy-start.2 = (bf16[1,128,512]{2,1,0:T(8,128)(2,1)S(1)}, bf16[1,128,512]{2,1,0:T(8,128)(2,1)}, u32[]{:S(2)}) copy-start(bf16[1,128,512]{2,1,0:T(8,128)(2,1)} %param.8) | copy-start | bytes 393220
  61.6 23.4 %copy-start.3 = (f32[128]{0:T(128)S(1)}, f32[128]{0:T(128)}, u32[]{:S(2)}) copy-start(f32[128]{0:T(128)} %param.9) | copy-start | bytes 1540
  86.6 21.7 %all-to-all-start.2 = ((bf16[8,512,128]{2,1,0:T(8,128)(2,1)}), bf16[8,512,128]{2,1,0:T(8,128)(2,1)S(1)}, u32[]{:S(2)}, u32[]{:S(2)}) async-start(bf16[8,512,128]{2,1,0:T(8,128)(2,1)} %shard_map.104), calls=%async_computation.2 | async-start | bytes 2097152 | tf_op jit(solution)/shard_map/all_to_all | solution.py:125
  90.2 12.2 %collective-permute-start.7 = (f16[2,4,32,256]{3,2,1,0:T(8,128)(2,1)S(1)}, f16[2,4,32,256]{3,2,1,0:T(8,128)(2,1)S(1)}, u32[]{:S(2)}, u32[]{:S(2)}) collective-permute-start(f16[2,4,32,256]{3,2,1,0:T(8,128)(2,1)S(1)} %bitcast_dynamic-update-slice_fusion.2), channel_id=1, source_target_pairs={{0,32},{32,0},{1,33},{33,1},{2,34},{34,2},{3,35},{35,3},{4,36},{36... | collective-permute-start | bytes 393224 | tf_op jit(solution)/shard_map/ppermute | solution.py:135
  109.9 42.2 %copy-start.1 = (f32[1,256,512]{2,1,0:T(8,128)S(1)}, f32[1,256,512]{2,1,0:T(8,128)}, u32[]{:S(2)}) copy-start(f32[1,256,512]{2,1,0:T(8,128)} %param.10) | copy-start | bytes 1572868
  152.3 21.6 %copy-start.5 = (f32[256,32]{0,1:T(8,128)S(1)}, f32[256,32]{0,1:T(8,128)}, u32[]{:S(2)}) copy-start(f32[256,32]{0,1:T(8,128)} %param.12) | copy-start | bytes 98308
  152.3 21.6 %copy-start.7 = (f32[256,32]{0,1:T(8,128)S(1)}, f32[256,32]{0,1:T(8,128)}, u32[]{:S(2)}) copy-start(f32[256,32]{0,1:T(8,128)} %param.13) | copy-start | bytes 98308
  152.3 21.6 %copy-start.9 = (f32[256,32]{0,1:T(8,128)S(1)}, f32[256,32]{0,1:T(8,128)}, u32[]{:S(2)}) copy-start(f32[256,32]{0,1:T(8,128)} %param.11) | copy-start | bytes 98308
  153.0 20.8 %all-to-all-start.5 = ((f16[16,32,256]{2,1,0:T(8,128)(2,1)}), f16[16,32,256]{2,1,0:T(8,128)(2,1)S(1)}, u32[]{:S(2)}, u32[]{:S(2)}) async-start(f16[16,32,256]{2,1,0:T(8,128)(2,1)} %bitcast.20), calls=%async_computation.5 | async-start | bytes 524288 | tf_op jit(solution)/shard_map/all_to_all | solution.py:308
